TPU v7x, 256 devices: a whole 4x4x8 slice. The times are simulated.
256 devices in a mesh: row: 16 (over x, y), col: 16 (over z, core).
Axes of the slice: x: 4, y: 4, z: 8, core: 2. Of those that a mesh axis runs over, the one named last changes fastest.
Arguments:
- basis: bfloat16 [64, 524288], P(None, ('col', 'row'))
- values: bfloat16 [2048, 2048, 128], P('row', 'col')
- block_row: int32 [16, 2048], P('row', 'col'), may hold values from 0 to 255
- block_col: int32 [16, 2048], P('row', 'col'), may hold values from 0 to 255
- block_count: int32 [16, 16], P('row', 'col'), may hold values from 1 to 128, as said below
Outputs:
- embedding: float32 [64, 524288], P(None, ('row', 'col'))
- factor: float32 [64, 64], replicated
Inputs may be any that keep to these rules, and one draw needn't show every extreme that they name: `block_count`: every group stores at least one block, and at least one group fills all 128 slots.
All inputs are finite; a program needn't handle non-finite values.
Results may differ from a plain program's by a relative error of at most 0.0003.
Values may be sent and summed in bfloat16 or wider, within the bound.
No kernel may reach another device: no remote copies, remote signals or barrier semaphores. Data moves between devices by JAX's collectives and lax.ppermute only.
A program may use at most 64 MiB of HBM per device.

v0:
```python
import math

import jax
import jax.numpy as jnp
from jax import lax
from jax.sharding import PartitionSpec as P


def upper_factor(gram):
    order = gram.shape[0]
    index = jnp.arange(order, dtype=jnp.int32)

    def upper_step(column, lower):
        row_here = lax.dynamic_index_in_dim(lower, column, 0, keepdims=False)
        source = lax.dynamic_index_in_dim(gram, column, 1, keepdims=False)
        remain = source - jnp.dot(lower, row_here, precision=lax.Precision.HIGHEST)
        pivot = lax.dynamic_index_in_dim(remain, column, 0, keepdims=False)
        filled = jnp.where(index >= column, remain / jnp.sqrt(pivot), 0.0)
        return lower + filled[:, None] * (index[None, :] == column).astype(jnp.float32)

    lower = lax.fori_loop(0, order, upper_step, jnp.zeros_like(gram))
    return lower.T


def invert_upper(upper):
    order = upper.shape[0]
    index = jnp.arange(order, dtype=jnp.int32)

    def invert_step(count, inverse):
        which = order - 1 - count
        row_here = lax.dynamic_index_in_dim(upper, which, 0, keepdims=False)
        target = (index == which).astype(jnp.float32)
        rhs = target - jnp.dot(row_here, inverse, precision=lax.Precision.HIGHEST)
        pivot = lax.dynamic_index_in_dim(row_here, which, 0, keepdims=False)
        return inverse + target[:, None] * (rhs / pivot)[None, :]

    return lax.fori_loop(0, order, invert_step, jnp.zeros_like(upper))


def body(basis, values, block_row, block_col, block_count):
    highest = lax.Precision.HIGHEST
    width_k, width = basis.shape
    slots, _, size = values.shape
    blocks_here = width // size
    row_blocks = blocks_here * lax.axis_size("col")
    total_rows = width * lax.axis_size("row") * lax.axis_size("col")
    slab = lax.all_gather(basis, "row", axis=1, tiled=True)
    col_blocks = slab.shape[1] // size
    select = (block_col[0][:, None] == jnp.arange(col_blocks, dtype=jnp.int32)[None, :]).astype(
        jnp.bfloat16
    )
    picked = jnp.einsum(
        "sc,kcj->ksj",
        select,
        slab.reshape(width_k, col_blocks, size),
        preferred_element_type=jnp.float32,
    ).astype(jnp.bfloat16)
    prods = jnp.einsum("ksj,sij->ski", picked, values, preferred_element_type=jnp.float32)
    live = jnp.arange(slots, dtype=jnp.int32) < block_count[0, 0]
    targets = jnp.arange(row_blocks, dtype=jnp.int32)
    onehot = ((block_row[0][None, :] == targets[:, None]) & live[None, :]).astype(jnp.float32)
    mine = lax.psum_scatter(
        jnp.einsum("rs,ski->rki", onehot, prods, precision=highest),
        "col",
        scatter_dimension=0,
        tiled=True,
    )
    product = mine.transpose(1, 0, 2).reshape(width_k, width)
    gram = lax.psum(jnp.dot(product, product.T, precision=highest), ("row", "col"))
    upper = upper_factor(gram)
    inverse = invert_upper(upper)
    final = jnp.dot(inverse.T, product, precision=highest)
    scale = math.sqrt(total_rows)
    return (final * scale, upper / scale)


def solution(mesh):
    in_specs = (
        P(None, ("col", "row")),
        P("row", "col", None),
        P("row", "col"),
        P("row", "col"),
        P("row", "col"),
    )
    out_specs = (P(None, ("row", "col")), P())
    return jax.shard_map(body, mesh=mesh, in_specs=in_specs, out_specs=out_specs, check_vma=False)
```

profile of v0, /device:TPU:8, one launch (start us, length us, event | category | flops | bytes accessed | tf_op | source)
XLA Modules:
  0.0 427.9 jit_solution(626451947979621340)
XLA Ops:
  8.6 61.4 %all-gather.2.cloned.1.call-done = bf16[64,32768]{1,0:T(8,128)(2,1)} async-done(((bf16[64,2048]{1,0:T(8,128)(2,1)}), bf16[64,32768]{1,0:T(8,128)(2,1)}) %all-gather.2.cloned.1.call-update) | async-done | bytes 4194320 | tf_op jit(solution)/shard_map/all_gather | solution.py:47
  70.0 3.4 copy.13
  73.3 0.8 fusion.29
  74.1 1.4 copy-done
  75.5 3.0 fusion.20
  78.5 9.3 %fusion.17 = f32[256,64,128]{2,0,1:T(8,128)} fusion(f32[128,64,128]{2,1,0:T(8,128)S(1)} %fusion.20, s32[128]{0:T(128)S(1)} %bitcast.72, pred[128]{0:T(512)(128)(4,1)S(1)} %iota_compare_fusion.2), kind=kOutput, calls=%fused_computation.23 | convolution fusion | flops 3221291008 | bytes 12583552 | tf_op jit(solution)/shard_map/rs,ski->rki/dot_general | solution.py:63
  87.8 70.5 %reduce-scatter.2.cloned.1.call-done = f32[16,64,128]{2,0,1:T(8,128)} async-done(((f32[256,64,128]{2,0,1:T(8,128)}), f32[16,64,128]{2,0,1:T(8,128)}) %reduce-scatter.2.cloned.1.call-update) | async-done | bytes 524304 | tf_op jit(solution)/shard_map/reduce_scatter | solution.py:62
  158.3 2.0 convolution_bitcast_fusion.2
  160.3 75.3 %psum.7 = f32[64,64]{1,0:T(8,128)S(1)} all-reduce(f32[64,64]{1,0:T(8,128)S(1)} %convolution_bitcast_fusion.2), channel_id=1, replica_groups=mesh['row'=16,'col'=16] {'row','col'}, use_global_device_ids=true, to_apply=%region_1.0 | all-reduce | flops 4096 | bytes 32768 | tf_op jit(solution)/shard_map/psum | solution.py:69
  235.6 94.5 %while.33 = (s32[]{:T(128)}, f32[64,64]{1,0:T(8,128)S(1)}, f32[64,64]{0,1:T(8,128)S(1)}, s32[]{:T(128)}, s32[]{:T(128)}) while((s32[]{:T(128)}, f32[64,64]{1,0:T(8,128)S(1)}, f32[64,64]{0,1:T(8,128)S(1)}, s32[]{:T(128)}, s32[]{:T(128)}) %tuple.78), condition=%wide.region_3.4_spmd.clone.clone, body=%wide.region_2.3_spmd.clone.clone.sunk | while | flops 65923 | bytes 101992 | solution.py:21
  330.8 87.7 %while.32 = (s32[]{:T(128)}, f32[64,64]{1,0:T(8,128)S(1)}, f32[64,64]{1,0:T(8,128)S(1)}, s32[]{:T(128)}, s32[]{:T(128)}, /*index=5*/s32[]{:T(128)}, s32[]{:T(128)}) while((s32[]{:T(128)}, f32[64,64]{1,0:T(8,128)S(1)}, f32[64,64]{1,0:T(8,128)S(1)}, s32[]{:T(128)}, s32[]{:T(128)}, /*index=5*/s32[]{:T(128)}, s32[]{:T(128)}) %tuple.88), condition=%wide.region_5.6_spmd.clone, body=%wide.region_4.5_spmd.clone.sunk | while | flops 65928 | bytes 67250 | solution.py:37
  331.4 0.7 fusion.46
  332.7 0.7 fusion.46
  334.1 0.7 fusion.46
  335.5 0.7 fusion.46
  336.8 0.7 fusion.46
  338.2 0.7 fusion.46
  339.6 0.7 fusion.46
  341.0 0.7 fusion.46
  342.3 0.7 fusion.46
  343.7 0.7 fusion.46
  345.1 0.7 fusion.46
  346.4 0.7 fusion.46
  347.8 0.7 fusion.46
  349.2 0.7 fusion.46
  350.5 0.7 fusion.46
  351.9 0.7 fusion.46
  353.3 0.7 fusion.46
  354.7 0.7 fusion.46
  356.0 0.7 fusion.46
  357.4 0.7 fusion.46
  418.5 2.6 convolution_multiply_fusion
  (635 shorter events, 129.6 us)
Async XLA Ops:
  7.2 62.8 %all-gather.2.cloned.1.call-start = ((), (), s32[]{:S(2)}) async-start(), calls=%async_computation.1 | async-start | bytes 4456448 | tf_op jit(solution)/shard_map/all_gather | solution.py:47
  7.9 150.4 %reduce-scatter.2.cloned.1.call-start = ((), (), s32[]{:S(2)}) async-start(), calls=%async_computation.2 | async-start | bytes 8912896 | tf_op jit(solution)/shard_map/reduce_scatter | solution.py:62
  70.0 3.4 copy-start.1
  73.3 2.2 copy-start
  75.5 3.0 copy-start.2
Sparse Core Ops, SparseCore 0:
  10.5 59.4 all-gather.1
  87.9 70.3 reduce-scatter.1
where the time goes:
time: 432 us; the launch traced here: 428 us
  waiting for transfers between devices  133 us (31%)
  local copies, waits for them, and re-layouts  81.7 us (19%)
  blocking collectives  75.3 us (17%)
  matrix products  71.3 us (17%)
  loops' own time  40.2 us (9%)
  between operations  14.7 us (3%)
  other arithmetic  12.1 us (3%)
    psum x1, blocking collectives, body(): lax.psum(jnp.dot(product, product.T, precision=highest), ('row', 'col'))  75.3 us
    reduce_scatter x1, waiting for transfers between devices, body(): lax.psum_scatter(jnp.einsum('rs,ski->rki', onehot, prods, precision=highe...  70.5 us
    all_gather x1, waiting for transfers between devices, body(): slab = lax.all_gather(basis, 'row', axis=1, tiled=True)  61.4 us
    dot_general x64, matrix products, invert_step(): rhs = target - jnp.dot(row_here, inverse, precision=lax.Precision.HIGHEST)  44.6 us
    another operation x1, loops' own time, upper_factor(): lower = lax.fori_loop(0, order, upper_step, jnp.zeros_like(gram))  40 us
    dynamic_slice x64, local copies, waits for them, and re-layouts, upper_step(): pivot = lax.dynamic_index_in_dim(remain, column, 0, keepdims=False)  39.2 us
    dynamic_slice x64, local copies, waits for them, and re-layouts, invert_step(): pivot = lax.dynamic_index_in_dim(row_here, which, 0, keepdims=False)  37.6 us
    dot_general x1, matrix products, body(): jnp.einsum('rs,ski->rki', onehot, prods, precision=highest)  9.27 us
  transfers between devices with their start and end apart: 2, of which 2 were waited for; matrix products, arithmetic and copies ran while one was open for 0% of the time, Pallas kernels for 0%

commit v1 on v0

v1 whole, which is shorter than its diff:
```python
import functools
import math

import jax
import jax.numpy as jnp
from jax import lax
from jax.experimental import pallas as pl
from jax.experimental.pallas import tpu as pltpu
from jax.sharding import PartitionSpec as P

GROUP = 8
HIGHEST = lax.Precision.HIGHEST


def product_kernel(rows, cols, count, slab, values, out):
    size = values.shape[1]
    per_part = slab.shape[2] // size
    out[...] = jnp.zeros_like(out)

    def block(slot):
        column = cols[0, slot]
        part = lax.div(column, per_part)
        offset = pl.multiple_of(lax.rem(column, per_part) * size, size)
        return lax.dot_general(
            slab[part, :, pl.ds(offset, size)],
            values[slot],
            (((1,), (1,)), ((), ())),
            preferred_element_type=jnp.float32,
        )

    def group(step, carry):
        first = step * GROUP
        made = [block(first + i) for i in range(GROUP)]
        for i in range(GROUP):
            row = rows[0, first + i]
            out[row] = out[row] + made[i]
        return carry

    def single(slot, carry):
        row = rows[0, slot]
        out[row] = out[row] + block(slot)
        return carry

    live = jnp.minimum(count[0, 0], values.shape[0])
    whole = lax.div(live, GROUP)
    lax.fori_loop(0, whole, group, 0)
    lax.fori_loop(whole * GROUP, live, single, 0)


def block_product(rows, cols, count, slab, values, row_blocks):
    slots, size, _ = values.shape
    width_k = slab.shape[1]
    smem = pl.BlockSpec(memory_space=pltpu.SMEM)
    vmem = pl.BlockSpec(memory_space=pltpu.VMEM)
    return pl.pallas_call(
        product_kernel,
        out_shape=jax.ShapeDtypeStruct((row_blocks, width_k, size), jnp.float32),
        in_specs=[smem, smem, smem, vmem, vmem],
        out_specs=vmem,
        compiler_params=pltpu.CompilerParams(vmem_limit_bytes=40 * 2**20),
        cost_estimate=pl.CostEstimate(
            flops=2 * slots * size * size * width_k,
            bytes_accessed=slab.size * 2 + values.size * 2 + row_blocks * width_k * size * 4,
            transcendentals=0,
        ),
    )(rows, cols, count, slab, values)


def gram_kernel(mine, out):
    total = jnp.zeros(out.shape, jnp.float32)
    for b in range(mine.shape[0]):
        total += lax.dot_general(
            mine[b], mine[b], (((1,), (1,)), ((), ())),
            precision=HIGHEST, preferred_element_type=jnp.float32,
        )
    out[...] = total


def local_gram(mine):
    width_k = mine.shape[1]
    return pl.pallas_call(
        gram_kernel,
        out_shape=jax.ShapeDtypeStruct((width_k, width_k), jnp.float32),
    )(mine)


def finish_kernel(scale, gram, mine, embedding, factor, work):
    order = gram.shape[0]
    tile = 8
    tiles = order // tile
    lane = lax.broadcasted_iota(jnp.int32, (tile, 2 * order), 1)
    sub = lax.broadcasted_iota(jnp.int32, (tile, 2 * order), 0)
    work[:, :order] = gram[...]
    work[:, order:] = jnp.zeros((order, order), jnp.float32)
    rest = []
    for t in range(tiles):
        here = work[t * tile : (t + 1) * tile, :]
        rest.append(jnp.where(lane == sub + (order + t * tile), 1.0, here))
    for j in range(order):
        t, s = divmod(j, tile)
        row = rest[t][s : s + 1, :]
        pivot = rest[t][s : s + 1, j : j + 1]
        root = lax.rsqrt(pivot)
        root = root * (1.5 - 0.5 * (pivot * root) * root)
        unit = row * root
        work[j : j + 1, :] = unit
        for u in range(t, tiles):
            rest[u] = rest[u] - (rest[u][:, j : j + 1] * root) * unit
    done = work[...]
    row_id = lax.broadcasted_iota(jnp.int32, (order, 2 * order), 0)
    lane_id = lax.broadcasted_iota(jnp.int32, (order, 2 * order), 1)
    upper = jnp.where(lane_id >= row_id, done, 0.0)[:, :order]
    lower = jnp.where(lane_id <= row_id + order, done, 0.0)[:, order:]
    factor[...] = upper * (1.0 / scale)
    lower = lower * scale
    size = mine.shape[2]
    for b in range(mine.shape[0]):
        embedding[:, b * size : (b + 1) * size] = lax.dot_general(
            lower, mine[b], (((1,), (0,)), ((), ())),
            precision=HIGHEST, preferred_element_type=jnp.float32,
        )


def finish(gram, mine, scale):
    blocks, width_k, size = mine.shape
    return pl.pallas_call(
        functools.partial(finish_kernel, scale),
        out_shape=(
            jax.ShapeDtypeStruct((width_k, blocks * size), jnp.float32),
            jax.ShapeDtypeStruct((width_k, width_k), jnp.float32),
        ),
        scratch_shapes=[pltpu.VMEM((width_k, 2 * width_k), jnp.float32)],
    )(gram, mine)


def add_over(value, axis):
    count = lax.axis_size(axis)
    step = 1
    while step < count:
        value = value + lax.ppermute(value, axis, [(i, i ^ step) for i in range(count)])
        step *= 2
    return value


def body(basis, values, block_row, block_col, block_count):
    width_k, width = basis.shape
    size = values.shape[2]
    row_blocks = width // size * lax.axis_size("col")
    total_rows = width * lax.axis_size("row") * lax.axis_size("col")
    slab = lax.all_gather(basis, "row")
    share = block_product(block_row, block_col, block_count, slab, values, row_blocks)
    mine = lax.psum_scatter(share, "col", scatter_dimension=0, tiled=True)
    gram = add_over(add_over(local_gram(mine), "col"), "row")
    return finish(gram, mine, math.sqrt(total_rows))


def solution(mesh):
    in_specs = (
        P(None, ("col", "row")),
        P("row", "col", None),
        P("row", "col"),
        P("row", "col"),
        P("row", "col"),
    )
    out_specs = (P(None, ("row", "col")), P())
    return jax.shard_map(body, mesh=mesh, in_specs=in_specs, out_specs=out_specs, check_vma=False)
```

time: 432 us -> 212 us (0.49)
  local copies, waits for them, and re-layouts: 81.7 us -> 5.68 us
  blocking collectives: 75.3 us -> 0 us
  matrix products: 71.3 us -> 0 us
  loops' own time: 40.2 us -> 0 us
  waiting for transfers between devices: 133 us -> 160 us
  Pallas kernels: 0 us -> 19.1 us
  starting transfers between devices: 0.08 us -> 11 us
  other arithmetic: 12.1 us -> 1.4 us
    dynamic_slice x128 -> x0, local copies, waits for them, and re-layouts: 76.8 us -> none  [the longest x64 39.2 us: upper_step(): pivot = lax.dynamic_index_in_dim(remain, column, 0, keepdims=False)]
    psum x1 -> x0, blocking collectives: 75.3 us -> none  [body(): lax.psum(jnp.dot(product, product.T, precision=highest), ('row', 'col'))]
    dot_general x133 -> x0, matrix products: 71.3 us -> none  [the longest x64 44.6 us: invert_step(): rhs = target - jnp.dot(row_here, inverse, precision=lax.Precision.HIGHEST)]
    another operation x2 -> x0, loops' own time: 40.2 us -> none  [the longest x1 40 us: upper_factor(): lower = lax.fori_loop(0, order, upper_step, jnp.zeros_like(gram))]
    ppermute x0 -> x8, waiting for transfers between devices: none -> 26.3 us  [add_over(): lax.ppermute(value, axis, [(i, i ^ step) for i in range(count)])]
    pallas_call x0 -> x3, Pallas kernels: none -> 19.1 us  [the longest x1 8.29 us: finish(): pl.pallas_call(functools.partial(finish_kernel, scale), out_shape=(jax.Sh...]
    ppermute x0 -> x8, starting transfers between devices: none -> 10.9 us  [add_over(): lax.ppermute(value, axis, [(i, i ^ step) for i in range(count)])]
    add x128 -> x8, other arithmetic: 10.1 us -> 1.4 us  [add_over(): value + lax.ppermute(value, axis, [(i, i ^ step) for i in range(count)])]
  transfers between devices with their start and end apart: 2 -> 10, of which waited for: 2 -> 10; matrix products, arithmetic and copies ran while one was open for 0% -> 0% of each run, Pallas kernels for 0% -> 0%
where the time goes in v1:
time: 212 us
  waiting for transfers between devices  160 us (75%)
  Pallas kernels  19.1 us (9%)
  between operations  14.7 us (7%)
  starting transfers between devices  11 us (5%)
  local copies, waits for them, and re-layouts  5.68 us (3%)
    reduce_scatter x1, waiting for transfers between devices, body(): mine = lax.psum_scatter(share, 'col', scatter_dimension=0, tiled=True)  71.6 us
    all_gather x1, waiting for transfers between devices, body(): slab = lax.all_gather(basis, 'row')  61.2 us
    ppermute x8, waiting for transfers between devices, add_over(): lax.ppermute(value, axis, [(i, i ^ step) for i in range(count)])  26.3 us
    ppermute x8, starting transfers between devices, add_over(): lax.ppermute(value, axis, [(i, i ^ step) for i in range(count)])  10.9 us
    pallas_call x1, Pallas kernels, finish(): pl.pallas_call(functools.partial(finish_kernel, scale), out_shape=(jax.Sh...  8.29 us
    pallas_call x1, Pallas kernels, block_product(): pl.pallas_call(product_kernel, out_shape=jax.ShapeDtypeStruct((row_blocks...  8.2 us
    unnamed x8, local copies, waits for them, and re-layouts  5.68 us
  transfers between devices with their start and end apart: 10, of which 10 were waited for; matrix products, arithmetic and copies ran while one was open for 0% of the time, Pallas kernels for 0%

profile of v1, /device:TPU:8, one launch (start us, length us, event | category | flops | bytes accessed | tf_op | source)
XLA Modules:
  0.0 211.7 jit_solution(10255211412188219889)
XLA Ops:
  7.2 0.0 all-gather.3.cloned.1.call-start
  7.2 0.7 all-gather.3.cloned.1.call-update
  7.9 0.0 reduce-scatter.2.cloned.1.call-start
  8.6 61.2 %all-gather.3.cloned.1.call-done = bf16[1024,2048]{1,0:T(8,128)(2,1)} async-done(((bf16[64,2048]{1,0:T(8,128)(2,1)}), bf16[1024,2048]{1,0:T(8,128)(2,1)}) %all-gather.3.cloned.1.call-update) | async-done | bytes 4194320 | tf_op jit(solution)/shard_map/all_gather | solution.py:150
  69.8 0.0 copy-start
  69.8 2.2 %copy-done = bf16[128,128,128]{2,1,0:T(8,128)(2,1)S(1)} copy-done((bf16[128,128,128]{2,1,0:T(8,128)(2,1)S(1)}, bf16[128,128,128]{2,1,0:T(8,128)(2,1)}, u32[]{:S(2)}) %copy-start) | copy-done | bytes 4194328
  72.0 2.2 %copy-done.1 = bf16[1024,2048]{1,0:T(8,128)(2,1)S(1)} copy-done((bf16[1024,2048]{1,0:T(8,128)(2,1)S(1)}, bf16[1024,2048]{1,0:T(8,128)(2,1)}, u32[]{:S(2)}) %copy-start.1) | copy-done | bytes 4194328
  74.2 0.7 copy-done.2
  74.9 0.7 copy-done.3
  75.5 8.2 %shard_map.68 = f32[256,64,128]{2,1,0:T(8,128)} custom-call(s32[1,128]{1,0:T(1,128)S(1)} %copy-done.2, s32[1,128]{1,0:T(1,128)S(1)} %copy-done.3, s32[1,1]{1,0:T(1,128)S(6)} %copy.7.count, bf16[16,64,2048]{2,1,0:T(8,128)(2,1)S(1)} %bitcast.1, bf16[128,128,128]{2,1,0:T(8,128)(2,1)S(1)} %copy-done), custom_call_target="tpu_custom_call" | custom-call | flops 268435456 | bytes 16777216 | tf_op jit(solution)/shard_map/pallas_call | solution.py:55
  83.7 0.0 reduce-scatter.2.cloned.1.call-update
  83.8 71.6 %reduce-scatter.2.cloned.1.call-done.mine = f32[16,64,128]{2,1,0:T(8,128)} async-done(((f32[256,64,128]{2,1,0:T(8,128)}), f32[16,64,128]{2,1,0:T(8,128)}) %reduce-scatter.2.cloned.1.call-update) | async-done | bytes 524304 | tf_op jit(solution)/shard_map/reduce_scatter | solution.py:152
  155.3 2.6 %shard_map.69 = f32[64,64]{1,0:T(8,128)} custom-call(f32[16,64,128]{2,1,0:T(8,128)} %reduce-scatter.2.cloned.1.call-done.mine), custom_call_target="tpu_custom_call" | custom-call | tf_op jit(solution)/shard_map/pallas_call | solution.py:81
  157.9 0.0 collective-permute-start
  157.9 1.4 collective-permute-done
  159.3 0.8 add.26
  160.1 0.0 collective-permute-start.1
  160.1 3.9 %collective-permute-done.1 = f32[64,64]{1,0:T(8,128)S(1)} collective-permute-done((f32[64,64]{1,0:T(8,128)S(1)}, f32[64,64]{1,0:T(8,128)S(1)}, u32[]{:S(2)}, u32[]{:S(2)}) %collective-permute-start.1) | collective-permute-done | bytes 16416 | tf_op jit(solution)/shard_map/ppermute | solution.py:140
  164.0 1.3 collective-permute-start.2
  165.4 3.7 %collective-permute-done.2 = f32[64,64]{1,0:T(8,128)S(1)} collective-permute-done((f32[64,64]{1,0:T(8,128)S(1)}, f32[64,64]{1,0:T(8,128)S(1)}, u32[]{:S(2)}, u32[]{:S(2)}) %collective-permute-start.2) | collective-permute-done | bytes 16416 | tf_op jit(solution)/shard_map/ppermute | solution.py:140
  169.1 2.8 %collective-permute-start.3 = (f32[64,64]{1,0:T(8,128)S(1)}, f32[64,64]{1,0:T(8,128)S(1)}, u32[]{:S(2)}, u32[]{:S(2)}) collective-permute-start(f32[64,64]{1,0:T(8,128)S(1)} %add.28), channel_id=1, source_target_pairs={{0,8},{1,9},{2,10},{3,11},{4,12},{5,13},{6,14},{7,15},{8,0},{9,1},... | collective-permute-start | bytes 49160 | tf_op jit(solution)/shard_map/ppermute | solution.py:140
  171.9 5.3 %collective-permute-done.3 = f32[64,64]{1,0:T(8,128)S(1)} collective-permute-done((f32[64,64]{1,0:T(8,128)S(1)}, f32[64,64]{1,0:T(8,128)S(1)}, u32[]{:S(2)}, u32[]{:S(2)}) %collective-permute-start.3) | collective-permute-done | bytes 16416 | tf_op jit(solution)/shard_map/ppermute | solution.py:140
  177.2 0.5 collective-permute-start.4
  177.7 3.5 %collective-permute-done.4 = f32[64,64]{1,0:T(8,128)S(1)} collective-permute-done((f32[64,64]{1,0:T(8,128)S(1)}, f32[64,64]{1,0:T(8,128)S(1)}, u32[]{:S(2)}, u32[]{:S(2)}) %collective-permute-start.4) | collective-permute-done | bytes 16416 | tf_op jit(solution)/shard_map/ppermute | solution.py:140
  181.2 2.0 collective-permute-start.5
  183.2 3.5 %collective-permute-done.5 = f32[64,64]{1,0:T(8,128)S(1)} collective-permute-done((f32[64,64]{1,0:T(8,128)S(1)}, f32[64,64]{1,0:T(8,128)S(1)}, u32[]{:S(2)}, u32[]{:S(2)}) %collective-permute-start.5) | collective-permute-done | bytes 16416 | tf_op jit(solution)/shard_map/ppermute | solution.py:140
  186.7 1.3 collective-permute-start.6
  188.0 2.6 %collective-permute-done.6 = f32[64,64]{1,0:T(8,128)S(1)} collective-permute-done((f32[64,64]{1,0:T(8,128)S(1)}, f32[64,64]{1,0:T(8,128)S(1)}, u32[]{:S(2)}, u32[]{:S(2)}) %collective-permute-start.6) | collective-permute-done | bytes 16416 | tf_op jit(solution)/shard_map/ppermute | solution.py:140
  190.6 3.0 %collective-permute-start.7 = (f32[64,64]{1,0:T(8,128)S(1)}, f32[64,64]{1,0:T(8,128)S(1)}, u32[]{:S(2)}, u32[]{:S(2)}) collective-permute-start(f32[64,64]{1,0:T(8,128)S(1)} %add.32), channel_id=1, source_target_pairs={{0,128},{16,144},{32,160},{48,176},{64,192},{80,208},{96,224},{112... | collective-permute-start | bytes 49160 | tf_op jit(solution)/shard_map/ppermute | solution.py:140
  193.6 2.4 %collective-permute-done.7 = f32[64,64]{1,0:T(8,128)S(1)} collective-permute-done((f32[64,64]{1,0:T(8,128)S(1)}, f32[64,64]{1,0:T(8,128)S(1)}, u32[]{:S(2)}, u32[]{:S(2)}) %collective-permute-start.7) | collective-permute-done | bytes 16416 | tf_op jit(solution)/shard_map/ppermute | solution.py:140
  196.0 0.6 add.33.gram
  196.6 8.3 %shard_map.70 = (f32[64,2048]{1,0:T(8,128)}, f32[64,64]{1,0:T(8,128)}) custom-call(f32[64,64]{1,0:T(8,128)} %add.33.gram, f32[16,64,128]{2,1,0:T(8,128)} %reduce-scatter.2.cloned.1.call-done.mine), custom_call_target="tpu_custom_call" | custom-call | tf_op jit(solution)/shard_map/pallas_call | solution.py:126
  (9 shorter events, 0.0 us)
Async XLA Ops:
  7.2 62.7 %all-gather.3.cloned.1.call-start = ((), (), s32[]{:S(2)}) async-start(), calls=%async_computation.2 | async-start | bytes 4456448 | tf_op jit(solution)/shard_map/all_gather | solution.py:150
  7.9 147.4 %reduce-scatter.2.cloned.1.call-start = ((), (), s32[]{:S(2)}) async-start(), calls=%async_computation.1 | async-start | bytes 8912896 | tf_op jit(solution)/shard_map/reduce_scatter | solution.py:152
  69.8 2.2 %copy-start = (bf16[128,128,128]{2,1,0:T(8,128)(2,1)S(1)}, bf16[128,128,128]{2,1,0:T(8,128)(2,1)}, u32[]{:S(2)}) copy-start(bf16[128,128,128]{2,1,0:T(8,128)(2,1)} %values.1) | copy-start | bytes 12582916
  72.0 2.2 %copy-start.1 = (bf16[1024,2048]{1,0:T(8,128)(2,1)S(1)}, bf16[1024,2048]{1,0:T(8,128)(2,1)}, u32[]{:S(2)}) copy-start(bf16[1024,2048]{1,0:T(8,128)(2,1)} %all-gather.3.cloned.1.call-done) | copy-start | bytes 12582916
  74.2 0.7 copy-start.2
  74.9 0.7 copy-start.3
  157.9 1.4 collective-permute-start
  160.1 3.9 %collective-permute-start.1 = (f32[64,64]{1,0:T(8,128)S(1)}, f32[64,64]{1,0:T(8,128)S(1)}, u32[]{:S(2)}, u32[]{:S(2)}) collective-permute-start(f32[64,64]{1,0:T(8,128)S(1)} %add.26), channel_id=1, source_target_pairs={{0,2},{1,3},{2,0},{3,1},{4,6},{5,7},{6,4},{7,5},{8,10},{9,11},{10,... | collective-permute-start | bytes 49160 | tf_op jit(solution)/shard_map/ppermute | solution.py:140
  164.0 5.0 %collective-permute-start.2 = (f32[64,64]{1,0:T(8,128)S(1)}, f32[64,64]{1,0:T(8,128)S(1)}, u32[]{:S(2)}, u32[]{:S(2)}) collective-permute-start(f32[64,64]{1,0:T(8,128)S(1)} %add.27), channel_id=1, source_target_pairs={{0,4},{1,5},{2,6},{3,7},{4,0},{5,1},{6,2},{7,3},{8,12},{9,13},{10,... | collective-permute-start | bytes 49160 | tf_op jit(solution)/shard_map/ppermute | solution.py:140
  169.1 8.2 %collective-permute-start.3 = (f32[64,64]{1,0:T(8,128)S(1)}, f32[64,64]{1,0:T(8,128)S(1)}, u32[]{:S(2)}, u32[]{:S(2)}) collective-permute-start(f32[64,64]{1,0:T(8,128)S(1)} %add.28), channel_id=1, source_target_pairs={{0,8},{1,9},{2,10},{3,11},{4,12},{5,13},{6,14},{7,15},{8,0},{9,1},... | collective-permute-start | bytes 49160 | tf_op jit(solution)/shard_map/ppermute | solution.py:140
  177.2 4.0 %collective-permute-start.4 = (f32[64,64]{1,0:T(8,128)S(1)}, f32[64,64]{1,0:T(8,128)S(1)}, u32[]{:S(2)}, u32[]{:S(2)}) collective-permute-start(f32[64,64]{1,0:T(8,128)S(1)} %add.29), channel_id=1, source_target_pairs={{0,16},{16,0},{32,48},{48,32},{64,80},{80,64},{96,112},{112,96},{1... | collective-permute-start | bytes 49160 | tf_op jit(solution)/shard_map/ppermute | solution.py:140
  181.2 5.4 %collective-permute-start.5 = (f32[64,64]{1,0:T(8,128)S(1)}, f32[64,64]{1,0:T(8,128)S(1)}, u32[]{:S(2)}, u32[]{:S(2)}) collective-permute-start(f32[64,64]{1,0:T(8,128)S(1)} %add.30), channel_id=1, source_target_pairs={{0,32},{16,48},{32,0},{48,16},{64,96},{80,112},{96,64},{112,80},{1... | collective-permute-start | bytes 49160 | tf_op jit(solution)/shard_map/ppermute | solution.py:140
  186.7 3.9 %collective-permute-start.6 = (f32[64,64]{1,0:T(8,128)S(1)}, f32[64,64]{1,0:T(8,128)S(1)}, u32[]{:S(2)}, u32[]{:S(2)}) collective-permute-start(f32[64,64]{1,0:T(8,128)S(1)} %add.31), channel_id=1, source_target_pairs={{0,64},{16,80},{32,96},{48,112},{64,0},{80,16},{96,32},{112,48},{1... | collective-permute-start | bytes 49160 | tf_op jit(solution)/shard_map/ppermute | solution.py:140
  190.6 5.4 %collective-permute-start.7 = (f32[64,64]{1,0:T(8,128)S(1)}, f32[64,64]{1,0:T(8,128)S(1)}, u32[]{:S(2)}, u32[]{:S(2)}) collective-permute-start(f32[64,64]{1,0:T(8,128)S(1)} %add.32), channel_id=1, source_target_pairs={{0,128},{16,144},{32,160},{48,176},{64,192},{80,208},{96,224},{112... | collective-permute-start | bytes 49160 | tf_op jit(solution)/shard_map/ppermute | solution.py:140
Sparse Core Ops, SparseCore 0:
  10.4 59.3 all-gather.2
  83.9 71.4 reduce-scatter.1

commit v2 on v1

v2 whole, which is shorter than its diff:
```python
import functools
import math

import jax
import jax.numpy as jnp
from jax import lax
from jax.experimental import pallas as pl
from jax.experimental.pallas import tpu as pltpu
from jax.sharding import PartitionSpec as P

GROUP = 8
FINE = 16.0
PANEL = 4
HIGHEST = lax.Precision.HIGHEST


def listed(packed, side, want, entries, filler):
    slots = packed.shape[1]

    def place(step, filled):
        for i in range(GROUP):
            entry = packed[side, step * GROUP + i]
            entries[side, filled] = entry
            filled = filled + jnp.where((entry & 3) == want, 1, 0)
        return filled

    filled = lax.fori_loop(0, slots // GROUP, place, 0)
    for i in range(GROUP):
        entries[side, filled + i] = filler
    return filled


def add_products(entries, side, count, block, out):
    def make(step):
        return [block(step * GROUP + i) for i in range(GROUP)]

    def flush(step, made):
        for i in range(GROUP):
            row = (entries[side, step * GROUP + i] >> 10) & 511
            out[row] = out[row] + made[i]

    def loop(step, made):
        later = make(step)
        flush(step - 1, made)
        return later

    steps = jnp.maximum(lax.div(count + (GROUP - 1), GROUP), 1)
    flush(steps - 1, lax.fori_loop(1, steps, loop, make(0)))


def product(slab, side, entry, part_index, value):
    size = value.shape[0]
    part = part_index((entry >> 6) & 15)
    offset = pl.multiple_of(((entry >> 2) & 15) * size, size)
    return lax.dot_general(
        slab[part, side, :, pl.ds(offset, size)], value, (((1,), (1,)), ((), ())), preferred_element_type=jnp.float32
    )


def early_kernel(filler, packed, a0, b0, a1, b1, a3, b3, own_values, other_values, out, slab, blocks, entries, sems):
    copies = [
        pltpu.make_async_copy(values, blocks.at[n, pl.ds(0, values.shape[0])], sems.at[6 + n])
        for n, values in enumerate((own_values, other_values))
    ] + [
        pltpu.make_async_copy(piece, slab.at[pl.ds(2 * n, 2)], sems.at[n])
        for n, piece in enumerate((a0, b0, a1, b1, a3, b3))
    ]
    for copy in copies:
        copy.start()
    out[...] = jnp.zeros_like(out)
    counts = [listed(packed, side, 0, entries, filler) for side in range(2)]
    for copy in copies:
        copy.wait()
    for side in range(2):

        def block(n, side=side):
            entry = entries[side, n]
            return product(
                slab, side, entry, lambda part: jnp.where(part >= 12, part - 4, part), blocks[side, entry >> 19]
            )

        add_products(entries, side, counts[side], block, out)


def late_kernel(filler, packed, a2, b2, own_values, other_values, share, out, slab, blocks, entries, sems):
    copies = [
        pltpu.make_async_copy(piece, slab.at[pl.ds(2 * n, 2)], sems.at[n]) for n, piece in enumerate((a2, b2))
    ]
    for copy in copies:
        copy.start()
    counts = [listed(packed, side, 1, entries, filler | (2 << 8)) for side in range(2)]

    def fetch(side, n):
        source = (own_values, other_values)[side]
        return pltpu.make_async_copy(source.at[entries[side, n] >> 19], blocks.at[side, n], sems.at[2 + side])

    for side in range(2):
        lax.fori_loop(0, counts[side], lambda n, c, side=side: (fetch(side, n).start(), c)[1], 0)
    out[...] = share[...]
    for copy in copies:
        copy.wait()
    for side in range(2):
        lax.fori_loop(0, counts[side], lambda n, c, side=side: (fetch(side, n).wait(), c)[1], 0)
    for side in range(2):

        def block(n, side=side):
            return product(slab, side, entries[side, n], lambda part: part - 8, blocks[side, n])

        add_products(entries, side, counts[side], block, out)


def add_blocks(kernel, packed, pieces, own_values, other_values, before, row_blocks):
    slots, size, _ = own_values.shape
    half = pieces[0].shape[2]
    hbm = pl.BlockSpec(memory_space=pltpu.HBM)
    vmem = pl.BlockSpec(memory_space=pltpu.VMEM)
    return pl.pallas_call(
        functools.partial(kernel, row_blocks << 10),
        out_shape=jax.ShapeDtypeStruct((row_blocks + 1, half, size), jnp.float32),
        in_specs=[pl.BlockSpec(memory_space=pltpu.SMEM)]
        + [pl.BlockSpec(memory_space=pl.ANY)] * len(pieces)
        + [hbm] * 2
        + [vmem] * len(before),
        out_specs=vmem,
        scratch_shapes=[
            pltpu.VMEM((2 * len(pieces),) + pieces[0].shape[1:], jnp.bfloat16),
            pltpu.VMEM((2, slots + GROUP, size, size), jnp.bfloat16),
            pltpu.SMEM((2, slots + GROUP), jnp.int32),
            pltpu.SemaphoreType.DMA((len(pieces) + 2,)),
        ],
        compiler_params=pltpu.CompilerParams(vmem_limit_bytes=26 * 2**20),
        cost_estimate=pl.CostEstimate(
            flops=4 * slots * size * size * half, bytes_accessed=16 * 2**20, transcendentals=0
        ),
    )(packed, *pieces, own_values, other_values, *before)


def code_into(total, out):
    count = total.shape[0]
    top = jnp.abs(total[0])
    for b in range(1, count):
        top = jnp.maximum(top, jnp.abs(total[b]))
    top = jnp.maximum(top, 1e-30)
    power = jnp.ceil(FINE * (jnp.log2(top) - math.log2(32000.0)))
    out[count] = power.astype(jnp.int32).astype(jnp.int16)
    step = jnp.exp2(power * (-1.0 / FINE))
    for b in range(count):
        out[b] = jnp.round(total[b] * step).astype(jnp.int32).astype(jnp.int16)


def decoded(coded, b, step):
    return coded[b].astype(jnp.int32).astype(jnp.float32) * step


def step_of(coded):
    last = coded.shape[0] - 1
    return jnp.exp2(coded[last].astype(jnp.int32).astype(jnp.float32) * (1.0 / FINE))


def first_kernel(place, index, share, out_right, out_left):
    half = out_right.shape[0] - 1
    here = index[place]
    code_into(share.at[pl.ds(here, half)], out_right)
    code_into(share.at[pl.ds(here + half, half)], out_left)


def pass_kernel(place, begin, index, share, coded, out, total):
    count = coded.shape[0] - 1
    here = index[place]
    step = step_of(coded)
    for b in range(total.shape[0]):
        if begin <= b < begin + count:
            total[b] = share[here + b] + decoded(coded, b - begin, step)
        else:
            total[b] = share[here + b]
    code_into(total, out)


def last_kernel(place, index, share, right, left, out):
    here = index[place]
    step_right, step_left = step_of(right), step_of(left)
    for b in range(out.shape[0]):
        out[b] = share[here + b] + decoded(right, b, step_right) + decoded(left, b, step_left)


def on_chunk(kernel, index, share, coded, out_shape, scratch=()):
    vmem = pl.BlockSpec(memory_space=pltpu.VMEM)
    return pl.pallas_call(
        kernel,
        out_shape=out_shape,
        in_specs=[pl.BlockSpec(memory_space=pltpu.SMEM)] + [vmem] * (1 + len(coded)),
        out_specs=[vmem] * len(out_shape),
        scratch_shapes=list(scratch),
        compiler_params=pltpu.CompilerParams(vmem_limit_bytes=8 * 2**20),
        cost_estimate=pl.CostEstimate(flops=2**20, bytes_accessed=2**20, transcendentals=0),
    )(index, share, *coded)


def gram_kernel(core, ours, theirs, mine, out):
    count, half, _ = ours.shape
    first = core[0] == 0
    blocks = []
    for b in range(count):
        low = jnp.where(first, ours[b], theirs[b])
        high = jnp.where(first, theirs[b], ours[b])
        blocks.append(jnp.concatenate([low, high], axis=0))
    for b in range(count // 2):
        mine[b] = jnp.where(first, blocks[b], blocks[b + count // 2])
    wide = jnp.concatenate(blocks, axis=1)
    gram = lax.dot_general(
        wide, wide, (((1,), (1,)), ((), ())), precision=HIGHEST, preferred_element_type=jnp.float32
    )
    out[:, : 2 * half] = gram[:half]
    out[:, 2 * half :] = gram[half:]


def local_gram(core, ours, theirs):
    count, half, size = ours.shape
    vmem = pl.BlockSpec(memory_space=pltpu.VMEM)
    return pl.pallas_call(
        gram_kernel,
        out_shape=(
            jax.ShapeDtypeStruct((count // 2, 2 * half, size), jnp.float32),
            jax.ShapeDtypeStruct((half, 4 * half), jnp.float32),
        ),
        in_specs=[pl.BlockSpec(memory_space=pltpu.SMEM), vmem, vmem],
        out_specs=(vmem, vmem),
        compiler_params=pltpu.CompilerParams(vmem_limit_bytes=8 * 2**20),
    )(core, ours, theirs)


def finish_kernel(scale, grams, mine, embedding, factor, work):
    order = factor.shape[0]
    tile = 8
    tiles = order // tile
    total = grams[0]
    for n in range(1, grams.shape[0]):
        total = total + grams[n]
    work[: order // 2, :order] = total[:, :order]
    work[order // 2 :, :order] = total[:, order:]
    work[:, order:] = jnp.zeros((order, order), jnp.float32)
    lane = lax.broadcasted_iota(jnp.int32, (tile, 2 * order), 1)
    sub = lax.broadcasted_iota(jnp.int32, (tile, 2 * order), 0)
    rest = []
    for t in range(tiles):
        here = work[t * tile : (t + 1) * tile, :]
        rest.append(jnp.where(lane == sub + (order + t * tile), 1.0, here))
    shape = (tile, 2 * order)
    for j in range(0, order, PANEL):
        t, s = divmod(j, tile)
        rows = [rest[t][s + p : s + p + 1, :] for p in range(PANEL)]
        columns = [
            {u: jnp.broadcast_to(rest[u][:, j + p : j + p + 1], shape) for u in range(t, tiles)} for p in range(PANEL)
        ]
        for p in range(PANEL):
            pivot = columns[p][t][s + p : s + p + 1, :]
            root = lax.rsqrt(pivot)
            root = root * (1.5 - 0.5 * (pivot * root) * root)
            rows[p] = rows[p] * root
            work[j + p : j + p + 1, :] = rows[p]
            scaled = {u: columns[p][u] * root for u in range(t, tiles)}
            for q in range(p + 1, PANEL):
                across = scaled[t][s + q : s + q + 1, :]
                rows[q] = rows[q] - across * rows[p]
                for u in range(t, tiles):
                    columns[q][u] = columns[q][u] - scaled[u] * across
            for u in range(t, tiles):
                rest[u] = rest[u] - scaled[u] * rows[p]
    done = work[...]
    row_id = lax.broadcasted_iota(jnp.int32, (order, 2 * order), 0)
    lane_id = lax.broadcasted_iota(jnp.int32, (order, 2 * order), 1)
    upper = jnp.where(lane_id >= row_id, done, 0.0)[:, :order]
    lower = jnp.where(lane_id <= row_id + order, done, 0.0)[:, order:]
    factor[...] = upper * (1.0 / scale)
    wide = jnp.concatenate([mine[b] for b in range(mine.shape[0])], axis=1)
    embedding[...] = lax.dot_general(
        lower * scale, wide, (((1,), (0,)), ((), ())), precision=HIGHEST, preferred_element_type=jnp.float32
    )


def finish(grams, mine, scale):
    blocks, width_k, size = mine.shape
    vmem = pl.BlockSpec(memory_space=pltpu.VMEM)
    return pl.pallas_call(
        functools.partial(finish_kernel, scale),
        out_shape=(
            jax.ShapeDtypeStruct((width_k, blocks * size), jnp.float32),
            jax.ShapeDtypeStruct((width_k, width_k), jnp.float32),
        ),
        in_specs=[vmem, vmem],
        out_specs=(vmem, vmem),
        scratch_shapes=[pltpu.VMEM((width_k, 2 * width_k), jnp.float32)],
        compiler_params=pltpu.CompilerParams(vmem_limit_bytes=8 * 2**20),
    )(grams, mine)


SIDE = 4
BOTH = ("row", "col")


def permutes(rows, cols):
    depth = cols // 2

    def pairs(move):
        made = []
        for x in range(SIDE):
            for y in range(rows // SIDE):
                for z in range(depth):
                    for core in range(2):
                        a, b, c, d = move(x, y, z, core)
                        to = (a % SIDE) * (rows // SIDE) + b % (rows // SIDE)
                        made.append(
                            ((x * (rows // SIDE) + y) * cols + 2 * z + core, to * cols + 2 * (c % depth) + d)
                        )
        return made

    def along(first):
        def send(d):
            return pairs(lambda x, y, z, core: (x + d, y, z, core) if (core == 0) == first else (x, y + d, z, core))
        return send

    return (
        pairs(lambda x, y, z, core: (x, y, z, 1 - core)),
        along(True),
        along(False),
        lambda d: pairs(lambda x, y, z, core: (x, y, z + d, core)),
    )


def body(basis, values, block_row, block_col, block_count):
    width_k, width = basis.shape
    slots, size, _ = values.shape
    rows, cols = lax.axis_size("row"), lax.axis_size("col")
    half = width_k // 2
    per_device = width // size
    row_blocks = per_device * cols
    total_rows = width * rows * cols
    swap, first, second, deep = permutes(rows, cols)

    def move(array, pairs):
        return lax.ppermute(array, BOTH, pairs)

    row, col = lax.axis_index("row"), lax.axis_index("col")
    x, y = lax.div(row, SIDE), lax.rem(row, SIDE)
    z, core = lax.div(col, 2), lax.rem(col, 2)

    other_basis = move(basis, swap)
    values, other_basis = lax.optimization_barrier((values, other_basis))
    other_values = move(values, swap)

    def packed_for(which):
        slot = lax.broadcasted_iota(jnp.int32, block_row.shape, 1)
        source, offset = block_col >> 4, block_col & 15
        dx, dy = ((source >> 2) - x) & 3, (source - y) & 3
        near, far = jnp.where(which == 0, dx, dy), jnp.where(which == 0, dy, dx)
        key = jnp.where(slot < block_count, jnp.where(far == 2, 1, 0), 2)
        return key | (offset << 2) | (near << 6) | (far << 8) | (block_row << 10) | (slot << 19)

    packed = jnp.concatenate([packed_for(core), move(packed_for(1 - core), swap)])

    chunk = lax.dynamic_slice_in_dim(jnp.stack([basis, other_basis]), core * half, half, 1)
    from_low, from_high = move(chunk, first(1)), move(chunk, first(-1))
    a0 = jnp.stack([chunk, from_high])
    across = jnp.stack([move(from_low[0], first(1)), move(from_high[1], first(-1))])
    a3, a1 = move(a0, second(1)), move(a0, second(-1))
    b0 = jnp.stack([across, from_low])
    b1, b3 = move(b0, second(-1)), move(b0, second(1))
    a2, b2 = move(a3, second(1)), move(b1, second(-1))

    share = add_blocks(early_kernel, packed, (a0, b0, a1, b1, a3, b3), values, other_values, (), row_blocks)
    share = add_blocks(late_kernel, packed, (a2, b2), values, other_values, (share,), row_blocks)

    depth = cols // 2
    coded = jax.ShapeDtypeStruct((2 * per_device + 1, half, size), jnp.int16)
    part = jax.ShapeDtypeStruct((per_device + 1, half, size), jnp.int16)
    scratch = [pltpu.VMEM((2 * per_device, half, size), jnp.float32)]
    index = ((z + jnp.arange(depth, dtype=jnp.int32)) & (depth - 1)) * (2 * per_device)

    def run(kernel, d, arrays, shapes, scratch=()):
        return on_chunk(functools.partial(kernel, d % depth), index, share, arrays, shapes, scratch)

    right, left = run(first_kernel, depth // 2, [], [part, part])
    for d in range(depth // 2 - 1, 0, -1):
        right, left = move(right, deep(1)), move(left, deep(-1))
        begin = per_device if d == depth // 2 - 1 else 0
        (right,) = run(lambda place, *refs: pass_kernel(place, 0, *refs), d, [right], [coded], scratch)
        (left,) = run(lambda place, *refs, begin=begin: pass_kernel(place, begin, *refs), -d, [left], [coded], scratch)
    right, left = move(right, deep(1)), move(left, deep(-1))
    whole = jax.ShapeDtypeStruct((2 * per_device, half, size), jnp.float32)
    (ours,) = run(last_kernel, 0, [right, left], [whole])
    mine, gram = local_gram(core[None].astype(jnp.int32), ours, move(ours, swap))

    def spread(array, axis, groups):
        count = len(groups[0])
        copies = jnp.broadcast_to(array[None], (count,) + array.shape)
        return lax.all_to_all(copies, axis, 0, 0, axis_index_groups=groups)

    gram = spread(gram, "col", [list(range(c, cols, 2)) for c in range(2)]).sum(0)
    grams = spread(gram, "row", [list(range(rows))])
    return finish(grams, mine, math.sqrt(total_rows))


def solution(mesh):
    in_specs = (
        P(None, ("col", "row")),
        P("row", "col", None),
        P("row", "col"),
        P("row", "col"),
        P("row", "col"),
    )
    out_specs = (P(None, ("row", "col")), P())
    return jax.shard_map(body, mesh=mesh, in_specs=in_specs, out_specs=out_specs, check_vma=False)
```

time: 212 us -> 131 us (0.62)
  waiting for transfers between devices: 160 us -> 40.2 us
  blocking collectives: 0 us -> 26.6 us
  starting transfers between devices: 11 us -> 33.1 us
  between operations: 14.7 us -> 1.53 us
  Pallas kernels: 19.1 us -> 25 us
  local copies, waits for them, and re-layouts: 5.68 us -> 2.25 us
    reduce_scatter x1 -> x0, waiting for transfers between devices: 71.6 us -> none  [body(): mine = lax.psum_scatter(share, 'col', scatter_dimension=0, tiled=True)]
    all_gather x1 -> x0, waiting for transfers between devices: 61.2 us -> none  [body(): slab = lax.all_gather(basis, 'row')]
    all_to_all x0 -> x2, blocking collectives: none -> 26.6 us  [spread(): return lax.all_to_all(copies, axis, 0, 0, axis_index_groups=groups)]
    ppermute x8 -> x22, starting transfers between devices: 10.9 us -> 33.1 us  [move(): return lax.ppermute(array, BOTH, pairs)]
    ppermute x8 -> x22, waiting for transfers between devices: 26.3 us -> 40.2 us  [move(): return lax.ppermute(array, BOTH, pairs)]
    pallas_call x2 -> x11, Pallas kernels: 10.8 us -> 21 us  [the longest x2 14.5 us: add_blocks(): pl.pallas_call(functools.partial(kernel, row_blocks << 10), out_shape=jax...]
    pallas_call x1, Pallas kernels: 8.29 us -> 3.98 us  [finish(): pl.pallas_call(functools.partial(finish_kernel, scale), out_shape=(jax.Sh...]
    unnamed x8, local copies, waits for them, and re-layouts: 5.68 us -> 2.2 us
  transfers between devices with their start and end apart: 10 -> 22, of which waited for: 10 -> 12; matrix products, arithmetic and copies ran while one was open for 0% -> 2% of each run, Pallas kernels for 0% -> 10%
where the time goes in v2:
time: 131 us
  waiting for transfers between devices  40.2 us (31%)
  starting transfers between devices  33.1 us (25%)
  blocking collectives  26.6 us (20%)
  Pallas kernels  25 us (19%)
  local copies, waits for them, and re-layouts  2.25 us (2%)
  other arithmetic  2.01 us (2%)
  between operations  1.53 us (1%)
    ppermute x22, waiting for transfers between devices, move(): return lax.ppermute(array, BOTH, pairs)  40.2 us
    ppermute x22, starting transfers between devices, move(): return lax.ppermute(array, BOTH, pairs)  33.1 us
    all_to_all x2, blocking collectives, spread(): return lax.all_to_all(copies, axis, 0, 0, axis_index_groups=groups)  26.6 us
    pallas_call x2, Pallas kernels, add_blocks(): pl.pallas_call(functools.partial(kernel, row_blocks << 10), out_shape=jax...  14.5 us
    pallas_call x8, Pallas kernels, on_chunk(): pl.pallas_call(kernel, out_shape=out_shape, in_specs=[pl.BlockSpec(memory...  5.39 us
    pallas_call x1, Pallas kernels, finish(): pl.pallas_call(functools.partial(finish_kernel, scale), out_shape=(jax.Sh...  3.98 us
  transfers between devices with their start and end apart: 22, of which 12 were waited for; matrix products, arithmetic and copies ran while one was open for 2% of the time, Pallas kernels for 10%

profile of v2, /device:TPU:8, one launch (start us, length us, event | category | flops | bytes accessed | tf_op | source)
XLA Modules:
  0.0 130.7 jit_solution(13375690292817259485)
XLA Ops:
  0.8 1.7 %collective-permute-done.1 = bf16[64,2048]{1,0:T(8,128)(2,1)S(1)} collective-permute-done((bf16[64,2048]{1,0:T(8,128)(2,1)}, bf16[64,2048]{1,0:T(8,128)(2,1)S(1)}, u32[]{:S(2)}, u32[]{:S(2)}) %collective-permute-start.1) | collective-permute-done | bytes 262176 | tf_op jit(solution)/shard_map/ppermute | solution.py:341
  2.6 0.9 fusion
  3.5 2.8 %collective-permute-start.2 = (bf16[2,32,2048]{2,1,0:T(8,128)(2,1)S(1)}, bf16[2,32,2048]{2,1,0:T(8,128)(2,1)S(1)}, u32[]{:S(2)}, u32[]{:S(2)}) collective-permute-start(bf16[2,32,2048]{2,1,0:T(8,128)(2,1)S(1)} %fusion), channel_id=1, source_target_pairs={{0,192},{1,49},{2,194},{3,51},{4,196},{5,53},{6,198},{7,55},{8,200... | collective-permute-start | bytes 786440 | tf_op jit(solution)/shard_map/ppermute | solution.py:341
  6.4 0.9 fusion.10
  7.3 3.0 %collective-permute-done.2 = bf16[2,32,2048]{2,1,0:T(8,128)(2,1)S(1)} collective-permute-done((bf16[2,32,2048]{2,1,0:T(8,128)(2,1)S(1)}, bf16[2,32,2048]{2,1,0:T(8,128)(2,1)S(1)}, u32[]{:S(2)}, u32[]{:S(2)}) %collective-permute-start.2) | collective-permute-done | bytes 262176 | tf_op jit(solution)/shard_map/ppermute | solution.py:341
  10.3 3.8 %collective-permute-start.7 = (bf16[32,2048]{1,0:T(8,128)(2,1)S(1)}, bf16[32,2048]{1,0:T(8,128)(2,1)S(1)}, u32[]{:S(2)}, u32[]{:S(2)}) collective-permute-start(bf16[32,2048]{1,0:T(8,128)(2,1)S(1)} %slice_bitcast_fusion), channel_id=1, source_target_pairs={{0,192},{1,49},{2,194},{3,51},{4,196},{5,53},{6,198},{7,55},{8,200... | collective-permute-start | bytes 393224 | tf_op jit(solution)/shard_map/ppermute | solution.py:341
  14.2 1.7 %collective-permute-start.3 = (bf16[2,2,32,2048]{3,2,1,0:T(8,128)(2,1)S(1)}, bf16[2,2,32,2048]{3,2,1,0:T(8,128)(2,1)S(1)}, u32[]{:S(2)}, u32[]{:S(2)}) collective-permute-start(bf16[2,2,32,2048]{3,2,1,0:T(8,128)(2,1)S(1)} %pad_maximum_fusion.a0), channel_id=1, source_target_pairs={{0,16},{1,65},{2,18},{3,67},{4,20},{5,69},{6,22},{7,71},{8,24},{9,... | collective-permute-start | bytes 1572872 | tf_op jit(solution)/shard_map/ppermute | solution.py:341
  15.9 0.7 collective-permute-done.7
  16.6 5.2 %collective-permute-done.6 = bf16[32,2048]{1,0:T(8,128)(2,1)S(1)} collective-permute-done((bf16[32,2048]{1,0:T(8,128)(2,1)S(1)}, bf16[32,2048]{1,0:T(8,128)(2,1)S(1)}, u32[]{:S(2)}, u32[]{:S(2)}) %collective-permute-start.6) | collective-permute-done | bytes 131104 | tf_op jit(solution)/shard_map/ppermute | solution.py:341
  23.2 3.1 %collective-permute-start.11 = (bf16[2,2,32,2048]{3,2,1,0:T(8,128)(2,1)S(1)}, bf16[2,2,32,2048]{3,2,1,0:T(8,128)(2,1)S(1)}, u32[]{:S(2)}, u32[]{:S(2)}) collective-permute-start(bf16[2,2,32,2048]{3,2,1,0:T(8,128)(2,1)S(1)} %pad_maximum_fusion.a0), channel_id=1, source_target_pairs={{0,48},{1,193},{2,50},{3,195},{4,52},{5,197},{6,54},{7,199},{8,56}... | collective-permute-start | bytes 1572872 | tf_op jit(solution)/shard_map/ppermute | solution.py:341
  26.3 1.2 collective-permute-start.4
  27.5 3.7 %collective-permute-done.8.b1 = bf16[2,2,32,2048]{3,2,1,0:T(8,128)(2,1)S(1)} collective-permute-done((bf16[2,2,32,2048]{3,2,1,0:T(8,128)(2,1)S(1)}, bf16[2,2,32,2048]{3,2,1,0:T(8,128)(2,1)S(1)}, u32[]{:S(2)}, u32[]{:S(2)}) %collective-permute-start.8) | collective-permute-done | bytes 524320 | tf_op jit(solution)/shard_map/ppermute | solution.py:341
  31.1 1.0 collective-permute-start.9
  32.1 4.6 %collective-permute-done.11.a1 = bf16[2,2,32,2048]{3,2,1,0:T(8,128)(2,1)S(1)} collective-permute-done((bf16[2,2,32,2048]{3,2,1,0:T(8,128)(2,1)S(1)}, bf16[2,2,32,2048]{3,2,1,0:T(8,128)(2,1)S(1)}, u32[]{:S(2)}, u32[]{:S(2)}) %collective-permute-start.11) | collective-permute-done | bytes 524320 | tf_op jit(solution)/shard_map/ppermute | solution.py:341
  36.8 2.2 %copy-done = bf16[128,128,128]{2,1,0:T(8,128)(2,1)S(1)} copy-done((bf16[128,128,128]{2,1,0:T(8,128)(2,1)S(1)}, bf16[128,128,128]{2,1,0:T(8,128)(2,1)}, u32[]{:S(2)}) %copy-start) | copy-done | bytes 4194328
  39.0 8.6 %shard_map.68.share = f32[257,32,128]{2,1,0:T(8,128)S(1)} custom-call(s32[2,128]{1,0:T(2,128)S(1)} %pad_add_fusion.packed, bf16[2,2,32,2048]{3,2,1,0:T(8,128)(2,1)S(1)} %pad_maximum_fusion.a0, bf16[2,2,32,2048]{3,2,1,0:T(8,128)(2,1)S(1)} %pad_maximum_fusion.1.b0, bf16[2,2,32,2048]{3,2,1,0:T(8,128)(2,1)S(1)} %collective-permute-done.11.a1, ...), custom_call_target="tpu_custom_call" | custom-call | flops 268435456 | bytes 16777216 | tf_op jit(solution)/shard_map/pallas_call | solution.py:117
  47.5 6.0 %shard_map.69.share.refs_1_ = f32[257,32,128]{2,1,0:T(8,128)S(1)} custom-call(s32[2,128]{1,0:T(2,128)S(1)} %pad_add_fusion.packed, bf16[2,2,32,2048]{3,2,1,0:T(8,128)(2,1)S(1)} %collective-permute-done.4.a2, bf16[2,2,32,2048]{3,2,1,0:T(8,128)(2,1)} %collective-permute-done.9.b2, bf16[128,128,128]{2,1,0:T(8,128)(2,1)S(1)} %copy-done.1, ...), custom_call_target="tpu_custom_call" | custom-call | flops 268435456 | bytes 16777216 | tf_op jit(solution)/shard_map/pallas_call | solution.py:117
  54.2 6.4 %collective-permute-start.17 = (s16[17,32,128]{2,1,0:T(8,128)(2,1)S(1)}, s16[17,32,128]{2,1,0:T(8,128)(2,1)S(1)}, u32[]{:S(2)}, u32[]{:S(2)}) collective-permute-start(s16[17,32,128]{2,1,0:T(8,128)(2,1)S(1)} %get-tuple-element.11), channel_id=1, source_target_pairs={{0,14},{1,15},{2,0},{3,1},{4,2},{5,3},{6,4},{7,5},{8,6},{9,7},{10,... | collective-permute-start | bytes 417800 | tf_op jit(solution)/shard_map/ppermute | solution.py:341
  60.6 2.6 %collective-permute-done.17.refs_2_ = s16[17,32,128]{2,1,0:T(8,128)(2,1)S(1)} collective-permute-done((s16[17,32,128]{2,1,0:T(8,128)(2,1)S(1)}, s16[17,32,128]{2,1,0:T(8,128)(2,1)S(1)}, u32[]{:S(2)}, u32[]{:S(2)}) %collective-permute-start.17) | collective-permute-done | bytes 139296 | tf_op jit(solution)/shard_map/ppermute | solution.py:341
  63.9 4.1 %collective-permute-start.18 = (s16[33,32,128]{2,1,0:T(8,128)(2,1)S(1)}, s16[33,32,128]{2,1,0:T(8,128)(2,1)S(1)}, u32[]{:S(2)}, u32[]{:S(2)}) collective-permute-start(s16[33,32,128]{2,1,0:T(8,128)(2,1)S(1)} %shard_map.74), channel_id=1, source_target_pairs={{0,14},{1,15},{2,0},{3,1},{4,2},{5,3},{6,4},{7,5},{8,6},{9,7},{10,... | collective-permute-start | bytes 811016 | tf_op jit(solution)/shard_map/ppermute | solution.py:341
  68.8 3.8 %collective-permute-done.18.refs_2_ = s16[33,32,128]{2,1,0:T(8,128)(2,1)S(1)} collective-permute-done((s16[33,32,128]{2,1,0:T(8,128)(2,1)S(1)}, s16[33,32,128]{2,1,0:T(8,128)(2,1)S(1)}, u32[]{:S(2)}, u32[]{:S(2)}) %collective-permute-start.18) | collective-permute-done | bytes 270368 | tf_op jit(solution)/shard_map/ppermute | solution.py:341
  73.3 4.0 %collective-permute-start.19 = (s16[33,32,128]{2,1,0:T(8,128)(2,1)S(1)}, s16[33,32,128]{2,1,0:T(8,128)(2,1)S(1)}, u32[]{:S(2)}, u32[]{:S(2)}) collective-permute-start(s16[33,32,128]{2,1,0:T(8,128)(2,1)S(1)} %shard_map.75), channel_id=1, source_target_pairs={{0,14},{1,15},{2,0},{3,1},{4,2},{5,3},{6,4},{7,5},{8,6},{9,7},{10,... | collective-permute-start | bytes 811016 | tf_op jit(solution)/shard_map/ppermute | solution.py:341
  78.1 5.2 %collective-permute-done.19.refs_2_ = s16[33,32,128]{2,1,0:T(8,128)(2,1)S(1)} collective-permute-done((s16[33,32,128]{2,1,0:T(8,128)(2,1)S(1)}, s16[33,32,128]{2,1,0:T(8,128)(2,1)S(1)}, u32[]{:S(2)}, u32[]{:S(2)}) %collective-permute-start.19) | collective-permute-done | bytes 270368 | tf_op jit(solution)/shard_map/ppermute | solution.py:341
  84.0 3.8 %collective-permute-start.20 = (s16[33,32,128]{2,1,0:T(8,128)(2,1)S(1)}, s16[33,32,128]{2,1,0:T(8,128)(2,1)S(1)}, u32[]{:S(2)}, u32[]{:S(2)}) collective-permute-start(s16[33,32,128]{2,1,0:T(8,128)(2,1)S(1)} %shard_map.76), channel_id=1, source_target_pairs={{0,14},{1,15},{2,0},{3,1},{4,2},{5,3},{6,4},{7,5},{8,6},{9,7},{10,... | collective-permute-start | bytes 811016 | tf_op jit(solution)/shard_map/ppermute | solution.py:341
  88.6 3.2 %collective-permute-done.20.left = s16[33,32,128]{2,1,0:T(8,128)(2,1)S(1)} collective-permute-done((s16[33,32,128]{2,1,0:T(8,128)(2,1)S(1)}, s16[33,32,128]{2,1,0:T(8,128)(2,1)S(1)}, u32[]{:S(2)}, u32[]{:S(2)}) %collective-permute-start.20) | collective-permute-done | bytes 270368 | tf_op jit(solution)/shard_map/ppermute | solution.py:341
  91.8 4.5 %collective-permute-done.16.right = s16[33,32,128]{2,1,0:T(8,128)(2,1)S(1)} collective-permute-done((s16[33,32,128]{2,1,0:T(8,128)(2,1)S(1)}, s16[33,32,128]{2,1,0:T(8,128)(2,1)S(1)}, u32[]{:S(2)}, u32[]{:S(2)}) %collective-permute-start.16) | collective-permute-done | bytes 270368 | tf_op jit(solution)/shard_map/ppermute | solution.py:341
  96.3 0.7 shard_map.77.ours
  97.1 1.9 %collective-permute-done.21.theirs = f32[32,32,128]{2,1,0:T(8,128)S(1)} collective-permute-done((f32[32,32,128]{2,1,0:T(8,128)S(1)}, f32[32,32,128]{2,1,0:T(8,128)S(1)}, u32[]{:S(2)}, u32[]{:S(2)}) %collective-permute-start.21) | collective-permute-done | bytes 524320 | tf_op jit(solution)/shard_map/ppermute | solution.py:341
  99.0 1.1 shard_map.78
  100.0 12.0 %all_to_all.10 = f32[8,32,128]{2,1,0:T(8,128)S(1)} all-to-all(f32[8,32,128]{2,1,0:T(8,128)S(1)} %broadcast_in_dim.31), channel_id=1, replica_groups={{0,2,4,6,8,10,12,14},{1,3,5,7,9,11,13,15},{16,18,20,22,24,26,28,30},{17..., dimensions={0} | all-to-all | bytes 262144 | tf_op jit(solution)/shard_map/all_to_all | solution.py:396
  112.1 14.6 %all_to_all.11.grams = f32[16,32,128]{2,1,0:T(8,128)S(1)} all-to-all(f32[16,32,128]{2,1,0:T(8,128)S(1)} %broadcast_in_dim.32), channel_id=1, replica_groups={{0,16,32,48,64,80,96,112,128,144,160,176,192,208,224,240},{1,17,33,49,6..., dimensions={0} | all-to-all | bytes 524288 | tf_op jit(solution)/shard_map/all_to_all | solution.py:396
  126.7 4.0 %shard_map.79 = (f32[64,2048]{1,0:T(8,128)}, f32[64,64]{1,0:T(8,128)}) custom-call(f32[16,32,128]{2,1,0:T(8,128)S(1)} %all_to_all.11.grams, f32[16,64,128]{2,1,0:T(8,128)S(1)} %get-tuple-element.13.mine), custom_call_target="tpu_custom_call" | custom-call | tf_op jit(solution)/shard_map/pallas_call | solution.py:284
  (47 shorter events, 6.3 us)
Async XLA Ops:
  0.6 22.4 %copy-start.3 = (s32[1,128]{1,0:T(1,128)S(1)}, s32[1,128]{1,0:T(1,128)}, u32[]{:S(2)}) copy-start(s32[1,128]{1,0:T(1,128)} %param.8) | copy-start | bytes 1540
  0.6 22.4 %copy-start.2 = (s32[1,128]{1,0:T(1,128)S(1)}, s32[1,128]{1,0:T(1,128)}, u32[]{:S(2)}) copy-start(s32[1,128]{1,0:T(1,128)} %param.7) | copy-start | bytes 1540
  0.6 1.8 %collective-permute-start.1 = (bf16[64,2048]{1,0:T(8,128)(2,1)}, bf16[64,2048]{1,0:T(8,128)(2,1)S(1)}, u32[]{:S(2)}, u32[]{:S(2)}) collective-permute-start(bf16[64,2048]{1,0:T(8,128)(2,1)} %param.5), channel_id=1, source_target_pairs={{0,1},{1,0},{2,3},{3,2},{4,5},{5,4},{6,7},{7,6},{8,9},{9,8},{10,11... | collective-permute-start | bytes 786440 | tf_op jit(solution)/shard_map/ppermute | solution.py:341
  2.5 34.3 %collective-permute-start.10 = (bf16[128,128,128]{2,1,0:T(8,128)(2,1)}, bf16[128,128,128]{2,1,0:T(8,128)(2,1)}, u32[]{:S(2)}, u32[]{:S(2)}) collective-permute-start(bf16[128,128,128]{2,1,0:T(8,128)(2,1)} %own_values.1), channel_id=1, source_target_pairs={{0,1},{1,0},{2,3},{3,2},{4,5},{5,4},{6,7},{7,6},{8,9},{9,8},{10,11... | collective-permute-start | bytes 12582920 | tf_op jit(solution)/shard_map/ppermute | solution.py:341
  3.5 6.7 %collective-permute-start.2 = (bf16[2,32,2048]{2,1,0:T(8,128)(2,1)S(1)}, bf16[2,32,2048]{2,1,0:T(8,128)(2,1)S(1)}, u32[]{:S(2)}, u32[]{:S(2)}) collective-permute-start(bf16[2,32,2048]{2,1,0:T(8,128)(2,1)S(1)} %fusion), channel_id=1, source_target_pairs={{0,192},{1,49},{2,194},{3,51},{4,196},{5,53},{6,198},{7,55},{8,200... | collective-permute-start | bytes 786440 | tf_op jit(solution)/shard_map/ppermute | solution.py:341
  6.4 7.7 %collective-permute-start.5 = (bf16[2,32,2048]{2,1,0:T(8,128)(2,1)S(1)}, bf16[2,32,2048]{2,1,0:T(8,128)(2,1)S(1)}, u32[]{:S(2)}, u32[]{:S(2)}) collective-permute-start(bf16[2,32,2048]{2,1,0:T(8,128)(2,1)S(1)} %fusion), channel_id=1, source_target_pairs={{0,64},{1,17},{2,66},{3,19},{4,68},{5,21},{6,70},{7,23},{8,72},{9,... | collective-permute-start | bytes 786440 | tf_op jit(solution)/shard_map/ppermute | solution.py:341
  10.3 6.3 %collective-permute-start.7 = (bf16[32,2048]{1,0:T(8,128)(2,1)S(1)}, bf16[32,2048]{1,0:T(8,128)(2,1)S(1)}, u32[]{:S(2)}, u32[]{:S(2)}) collective-permute-start(bf16[32,2048]{1,0:T(8,128)(2,1)S(1)} %slice_bitcast_fusion), channel_id=1, source_target_pairs={{0,192},{1,49},{2,194},{3,51},{4,196},{5,53},{6,198},{7,55},{8,200... | collective-permute-start | bytes 393224 | tf_op jit(solution)/shard_map/ppermute | solution.py:341
  14.1 7.7 %collective-permute-start.6 = (bf16[32,2048]{1,0:T(8,128)(2,1)S(1)}, bf16[32,2048]{1,0:T(8,128)(2,1)S(1)}, u32[]{:S(2)}, u32[]{:S(2)}) collective-permute-start(bf16[32,2048]{1,0:T(8,128)(2,1)S(1)} %slice_bitcast_fusion.1), channel_id=1, source_target_pairs={{0,64},{1,17},{2,66},{3,19},{4,68},{5,21},{6,70},{7,23},{8,72},{9,... | collective-permute-start | bytes 393224 | tf_op jit(solution)/shard_map/ppermute | solution.py:341
  14.2 12.1 %collective-permute-start.3 = (bf16[2,2,32,2048]{3,2,1,0:T(8,128)(2,1)S(1)}, bf16[2,2,32,2048]{3,2,1,0:T(8,128)(2,1)S(1)}, u32[]{:S(2)}, u32[]{:S(2)}) collective-permute-start(bf16[2,2,32,2048]{3,2,1,0:T(8,128)(2,1)S(1)} %pad_maximum_fusion.a0), channel_id=1, source_target_pairs={{0,16},{1,65},{2,18},{3,67},{4,20},{5,69},{6,22},{7,71},{8,24},{9,... | collective-permute-start | bytes 1572872 | tf_op jit(solution)/shard_map/ppermute | solution.py:341
  21.9 9.3 %collective-permute-start.8 = (bf16[2,2,32,2048]{3,2,1,0:T(8,128)(2,1)S(1)}, bf16[2,2,32,2048]{3,2,1,0:T(8,128)(2,1)S(1)}, u32[]{:S(2)}, u32[]{:S(2)}) collective-permute-start(bf16[2,2,32,2048]{3,2,1,0:T(8,128)(2,1)S(1)} %pad_maximum_fusion.1.b0), channel_id=1, source_target_pairs={{0,48},{1,193},{2,50},{3,195},{4,52},{5,197},{6,54},{7,199},{8,56}... | collective-permute-start | bytes 1572872 | tf_op jit(solution)/shard_map/ppermute | solution.py:341
  23.1 3.2 %collective-permute-start = (s32[1,128]{1,0:T(1,128)S(1)}, s32[1,128]{1,0:T(1,128)S(1)}, u32[]{:S(2)}, u32[]{:S(2)}) collective-permute-start(s32[1,128]{1,0:T(1,128)S(1)} %get-tuple-element.15), channel_id=1, source_target_pairs={{0,1},{1,0},{2,3},{3,2},{4,5},{5,4},{6,7},{7,6},{8,9},{9,8},{10,11... | collective-permute-start | bytes 1544 | tf_op jit(solution)/shard_map/ppermute | solution.py:341
  23.2 13.6 %collective-permute-start.11 = (bf16[2,2,32,2048]{3,2,1,0:T(8,128)(2,1)S(1)}, bf16[2,2,32,2048]{3,2,1,0:T(8,128)(2,1)S(1)}, u32[]{:S(2)}, u32[]{:S(2)}) collective-permute-start(bf16[2,2,32,2048]{3,2,1,0:T(8,128)(2,1)S(1)} %pad_maximum_fusion.a0), channel_id=1, source_target_pairs={{0,48},{1,193},{2,50},{3,195},{4,52},{5,197},{6,54},{7,199},{8,56}... | collective-permute-start | bytes 1572872 | tf_op jit(solution)/shard_map/ppermute | solution.py:341
  26.3 10.5 %collective-permute-start.12 = (bf16[2,2,32,2048]{3,2,1,0:T(8,128)(2,1)S(1)}, bf16[2,2,32,2048]{3,2,1,0:T(8,128)(2,1)}, u32[]{:S(2)}, u32[]{:S(2)}) collective-permute-start(bf16[2,2,32,2048]{3,2,1,0:T(8,128)(2,1)S(1)} %pad_maximum_fusion.1.b0), channel_id=1, source_target_pairs={{0,16},{1,65},{2,18},{3,67},{4,20},{5,69},{6,22},{7,71},{8,24},{9,... | collective-permute-start | bytes 1572872 | tf_op jit(solution)/shard_map/ppermute | solution.py:341
  26.3 21.2 %collective-permute-start.4 = (bf16[2,2,32,2048]{3,2,1,0:T(8,128)(2,1)S(1)}, bf16[2,2,32,2048]{3,2,1,0:T(8,128)(2,1)S(1)}, u32[]{:S(2)}, u32[]{:S(2)}) collective-permute-start(bf16[2,2,32,2048]{3,2,1,0:T(8,128)(2,1)S(1)} %collective-permute-done.3.a3), channel_id=1, source_target_pairs={{0,16},{1,65},{2,18},{3,67},{4,20},{5,69},{6,22},{7,71},{8,24},{9,... | collective-permute-start | bytes 1572872 | tf_op jit(solution)/shard_map/ppermute | solution.py:341
  31.1 16.4 %collective-permute-start.9 = (bf16[2,2,32,2048]{3,2,1,0:T(8,128)(2,1)S(1)}, bf16[2,2,32,2048]{3,2,1,0:T(8,128)(2,1)}, u32[]{:S(2)}, u32[]{:S(2)}) collective-permute-start(bf16[2,2,32,2048]{3,2,1,0:T(8,128)(2,1)S(1)} %collective-permute-done.8.b1), channel_id=1, source_target_pairs={{0,48},{1,193},{2,50},{3,195},{4,52},{5,197},{6,54},{7,199},{8,56}... | collective-permute-start | bytes 1572872 | tf_op jit(solution)/shard_map/ppermute | solution.py:341
  36.8 2.2 %copy-start = (bf16[128,128,128]{2,1,0:T(8,128)(2,1)S(1)}, bf16[128,128,128]{2,1,0:T(8,128)(2,1)}, u32[]{:S(2)}) copy-start(bf16[128,128,128]{2,1,0:T(8,128)(2,1)} %own_values.1) | copy-start | bytes 12582916
  39.0 8.6 %copy-start.1 = (bf16[128,128,128]{2,1,0:T(8,128)(2,1)S(1)}, bf16[128,128,128]{2,1,0:T(8,128)(2,1)}, u32[]{:S(2)}) copy-start(bf16[128,128,128]{2,1,0:T(8,128)(2,1)} %own_values.1) | copy-start | bytes 12582916
  54.2 9.0 %collective-permute-start.17 = (s16[17,32,128]{2,1,0:T(8,128)(2,1)S(1)}, s16[17,32,128]{2,1,0:T(8,128)(2,1)S(1)}, u32[]{:S(2)}, u32[]{:S(2)}) collective-permute-start(s16[17,32,128]{2,1,0:T(8,128)(2,1)S(1)} %get-tuple-element.11), channel_id=1, source_target_pairs={{0,14},{1,15},{2,0},{3,1},{4,2},{5,3},{6,4},{7,5},{8,6},{9,7},{10,... | collective-permute-start | bytes 417800 | tf_op jit(solution)/shard_map/ppermute | solution.py:341
  60.6 7.4 %collective-permute-start.13 = (s16[17,32,128]{2,1,0:T(8,128)(2,1)S(1)}, s16[17,32,128]{2,1,0:T(8,128)(2,1)S(1)}, u32[]{:S(2)}, u32[]{:S(2)}) collective-permute-start(s16[17,32,128]{2,1,0:T(8,128)(2,1)S(1)} %get-tuple-element.10), channel_id=1, source_target_pairs={{0,2},{1,3},{2,4},{3,5},{4,6},{5,7},{6,8},{7,9},{8,10},{9,11},{10,... | collective-permute-start | bytes 417800 | tf_op jit(solution)/shard_map/ppermute | solution.py:341
  63.9 8.7 %collective-permute-start.18 = (s16[33,32,128]{2,1,0:T(8,128)(2,1)S(1)}, s16[33,32,128]{2,1,0:T(8,128)(2,1)S(1)}, u32[]{:S(2)}, u32[]{:S(2)}) collective-permute-start(s16[33,32,128]{2,1,0:T(8,128)(2,1)S(1)} %shard_map.74), channel_id=1, source_target_pairs={{0,14},{1,15},{2,0},{3,1},{4,2},{5,3},{6,4},{7,5},{8,6},{9,7},{10,... | collective-permute-start | bytes 811016 | tf_op jit(solution)/shard_map/ppermute | solution.py:341
  68.7 8.6 %collective-permute-start.14 = (s16[33,32,128]{2,1,0:T(8,128)(2,1)S(1)}, s16[33,32,128]{2,1,0:T(8,128)(2,1)S(1)}, u32[]{:S(2)}, u32[]{:S(2)}) collective-permute-start(s16[33,32,128]{2,1,0:T(8,128)(2,1)S(1)} %shard_map.71), channel_id=1, source_target_pairs={{0,2},{1,3},{2,4},{3,5},{4,6},{5,7},{6,8},{7,9},{8,10},{9,11},{10,... | collective-permute-start | bytes 811016 | tf_op jit(solution)/shard_map/ppermute | solution.py:341
  73.3 10.0 %collective-permute-start.19 = (s16[33,32,128]{2,1,0:T(8,128)(2,1)S(1)}, s16[33,32,128]{2,1,0:T(8,128)(2,1)S(1)}, u32[]{:S(2)}, u32[]{:S(2)}) collective-permute-start(s16[33,32,128]{2,1,0:T(8,128)(2,1)S(1)} %shard_map.75), channel_id=1, source_target_pairs={{0,14},{1,15},{2,0},{3,1},{4,2},{5,3},{6,4},{7,5},{8,6},{9,7},{10,... | collective-permute-start | bytes 811016 | tf_op jit(solution)/shard_map/ppermute | solution.py:341
  78.0 9.8 %collective-permute-start.15 = (s16[33,32,128]{2,1,0:T(8,128)(2,1)S(1)}, s16[33,32,128]{2,1,0:T(8,128)(2,1)S(1)}, u32[]{:S(2)}, u32[]{:S(2)}) collective-permute-start(s16[33,32,128]{2,1,0:T(8,128)(2,1)S(1)} %shard_map.72), channel_id=1, source_target_pairs={{0,2},{1,3},{2,4},{3,5},{4,6},{5,7},{6,8},{7,9},{8,10},{9,11},{10,... | collective-permute-start | bytes 811016 | tf_op jit(solution)/shard_map/ppermute | solution.py:341
  84.0 7.7 %collective-permute-start.20 = (s16[33,32,128]{2,1,0:T(8,128)(2,1)S(1)}, s16[33,32,128]{2,1,0:T(8,128)(2,1)S(1)}, u32[]{:S(2)}, u32[]{:S(2)}) collective-permute-start(s16[33,32,128]{2,1,0:T(8,128)(2,1)S(1)} %shard_map.76), channel_id=1, source_target_pairs={{0,14},{1,15},{2,0},{3,1},{4,2},{5,3},{6,4},{7,5},{8,6},{9,7},{10,... | collective-permute-start | bytes 811016 | tf_op jit(solution)/shard_map/ppermute | solution.py:341
  88.5 7.7 %collective-permute-start.16 = (s16[33,32,128]{2,1,0:T(8,128)(2,1)S(1)}, s16[33,32,128]{2,1,0:T(8,128)(2,1)S(1)}, u32[]{:S(2)}, u32[]{:S(2)}) collective-permute-start(s16[33,32,128]{2,1,0:T(8,128)(2,1)S(1)} %shard_map.73), channel_id=1, source_target_pairs={{0,2},{1,3},{2,4},{3,5},{4,6},{5,7},{6,8},{7,9},{8,10},{9,11},{10,... | collective-permute-start | bytes 811016 | tf_op jit(solution)/shard_map/ppermute | solution.py:341
  97.0 2.0 %collective-permute-start.21 = (f32[32,32,128]{2,1,0:T(8,128)S(1)}, f32[32,32,128]{2,1,0:T(8,128)S(1)}, u32[]{:S(2)}, u32[]{:S(2)}) collective-permute-start(f32[32,32,128]{2,1,0:T(8,128)S(1)} %shard_map.77.ours), channel_id=1, source_target_pairs={{0,1},{1,0},{2,3},{3,2},{4,5},{5,4},{6,7},{7,6},{8,9},{9,8},{10,11... | collective-permute-start | bytes 1572872 | tf_op jit(solution)/shard_map/ppermute | solution.py:341

commit v3 on v2

--- a/solution.py
+++ b/solution.py
@@ -8,35 +8,25 @@
 from jax.experimental.pallas import tpu as pltpu
 from jax.sharding import PartitionSpec as P
 
-GROUP = 8
 FINE = 16.0
 PANEL = 4
+VMEM_ASK = 20 * 2**20
 HIGHEST = lax.Precision.HIGHEST
 
 
-def listed(packed, side, want, entries, filler):
-    slots = packed.shape[1]
-
-    def place(step, filled):
-        for i in range(GROUP):
-            entry = packed[side, step * GROUP + i]
-            entries[side, filled] = entry
-            filled = filled + jnp.where((entry & 3) == want, 1, 0)
-        return filled
-
-    filled = lax.fori_loop(0, slots // GROUP, place, 0)
-    for i in range(GROUP):
-        entries[side, filled + i] = filler
-    return filled
-
-
-def add_products(entries, side, count, block, out):
+def add_products(group, lists, side, begin, count, filler, block, out):
+    def entry(n):
+        return jnp.where(n < count, lists[side, begin + n], filler)
+
     def make(step):
-        return [block(step * GROUP + i) for i in range(GROUP)]
+        made = []
+        for i in range(0, group, 2):
+            made += block(entry(step * group + i), entry(step * group + i + 1))
+        return made
 
     def flush(step, made):
-        for i in range(GROUP):
-            row = (entries[side, step * GROUP + i] >> 10) & 511
+        for i in range(group):
+            row = (entry(step * group + i) >> 10) & 511
             out[row] = out[row] + made[i]
 
     def loop(step, made):
@@ -44,95 +34,99 @@
         flush(step - 1, made)
         return later
 
-    steps = jnp.maximum(lax.div(count + (GROUP - 1), GROUP), 1)
+    steps = jnp.maximum(lax.div(count + (group - 1), group), 1)
     flush(steps - 1, lax.fori_loop(1, steps, loop, make(0)))
 
 
-def product(slab, side, entry, part_index, value):
-    size = value.shape[0]
-    part = part_index((entry >> 6) & 15)
-    offset = pl.multiple_of(((entry >> 2) & 15) * size, size)
-    return lax.dot_general(
-        slab[part, side, :, pl.ds(offset, size)], value, (((1,), (1,)), ((), ())), preferred_element_type=jnp.float32
-    )
-
-
-def early_kernel(filler, packed, a0, b0, a1, b1, a3, b3, own_values, other_values, out, slab, blocks, entries, sems):
+def products(slab, side, entries, values):
+    size = values[0].shape[0]
+    left = []
+    for entry in entries:
+        offset = pl.multiple_of(((entry >> 2) & 15) * size, size)
+        left.append(slab[(entry >> 6) & 15, side, :, pl.ds(offset, size)])
+    both = lax.dot_general(
+        jnp.concatenate(left, axis=0),
+        jnp.concatenate(values, axis=0),
+        (((1,), (1,)), ((), ())),
+        preferred_element_type=jnp.float32,
+    )
+    half = left[0].shape[0]
+    return [both[:half, :size], both[half:, size:]]
+
+
+def load(pieces, slab, sems):
+    copies, at = [], 0
+    for n, piece in enumerate(pieces):
+        copies.append(pltpu.make_async_copy(piece, slab.at[pl.ds(at, piece.shape[0])], sems.at[n]))
+        at += piece.shape[0]
+    for copy in copies:
+        copy.start()
+    return copies
+
+
+def add_stage(stage, group, filler, lists, slab, blocks, out):
+    slots = blocks.shape[1]
+    for side in range(2):
+
+        def block(*entries, side=side):
+            return products(slab, side, entries, [blocks[side, entry >> 19] for entry in entries])
+
+        begin, count = lists[side, slots + stage], lists[side, slots + 4 + stage]
+        add_products(group, lists, side, begin, count, filler, block, out)
+
+
+def early_kernel(filler, lists, a0, b0, b1, a3, own_values, other_values, out, blocks, slab, sems):
     copies = [
-        pltpu.make_async_copy(values, blocks.at[n, pl.ds(0, values.shape[0])], sems.at[6 + n])
-        for n, values in enumerate((own_values, other_values))
-    ] + [
-        pltpu.make_async_copy(piece, slab.at[pl.ds(2 * n, 2)], sems.at[n])
-        for n, piece in enumerate((a0, b0, a1, b1, a3, b3))
+        pltpu.make_async_copy(values, blocks.at[n], sems.at[4 + n]) for n, values in enumerate((own_values, other_values))
     ]
     for copy in copies:
         copy.start()
+    copies += load((a0, b0, b1, a3), slab, sems)
     out[...] = jnp.zeros_like(out)
-    counts = [listed(packed, side, 0, entries, filler) for side in range(2)]
     for copy in copies:
         copy.wait()
-    for side in range(2):
-
-        def block(n, side=side):
-            entry = entries[side, n]
-            return product(
-                slab, side, entry, lambda part: jnp.where(part >= 12, part - 4, part), blocks[side, entry >> 19]
-            )
-
-        add_products(entries, side, counts[side], block, out)
-
-
-def late_kernel(filler, packed, a2, b2, own_values, other_values, share, out, slab, blocks, entries, sems):
-    copies = [
-        pltpu.make_async_copy(piece, slab.at[pl.ds(2 * n, 2)], sems.at[n]) for n, piece in enumerate((a2, b2))
-    ]
-    for copy in copies:
-        copy.start()
-    counts = [listed(packed, side, 1, entries, filler | (2 << 8)) for side in range(2)]
-
-    def fetch(side, n):
-        source = (own_values, other_values)[side]
-        return pltpu.make_async_copy(source.at[entries[side, n] >> 19], blocks.at[side, n], sems.at[2 + side])
-
-    for side in range(2):
-        lax.fori_loop(0, counts[side], lambda n, c, side=side: (fetch(side, n).start(), c)[1], 0)
+    add_stage(0, 32, filler, lists, slab, blocks, out)
+
+
+def middle_kernel(filler, lists, a1, b3, blocks, share, out, slab, sems):
+    copies = load((a1, b3), slab, sems)
     out[...] = share[...]
     for copy in copies:
         copy.wait()
-    for side in range(2):
-        lax.fori_loop(0, counts[side], lambda n, c, side=side: (fetch(side, n).wait(), c)[1], 0)
-    for side in range(2):
-
-        def block(n, side=side):
-            return product(slab, side, entries[side, n], lambda part: part - 8, blocks[side, n])
-
-        add_products(entries, side, counts[side], block, out)
-
-
-def add_blocks(kernel, packed, pieces, own_values, other_values, before, row_blocks):
-    slots, size, _ = own_values.shape
-    half = pieces[0].shape[2]
-    hbm = pl.BlockSpec(memory_space=pltpu.HBM)
+    add_stage(1, 16, filler, lists, slab, blocks, out)
+
+
+def late_kernel(filler, lists, a2, b2, index, blocks, share, out, out_right, out_left, slab, sems):
+    copies = load((a2, b2), slab, sems)
+    out[...] = share[...]
+    for copy in copies:
+        copy.wait()
+    add_stage(2, 16, filler, lists, slab, blocks, out)
+    half = out_right.shape[0] - 1
+    far = index[4]
+    code_into(out.at[pl.ds(far, half)], out_right)
+    code_into(out.at[pl.ds(far + half, half)], out_left)
+
+
+def add_blocks(kernel, flops, lists, pieces, values, whole, out_shape, row_blocks):
+    smem = pl.BlockSpec(memory_space=pltpu.SMEM)
     vmem = pl.BlockSpec(memory_space=pltpu.VMEM)
+    there = sum(piece.shape[0] for piece in pieces)
+    pieces = tuple(pieces) + tuple(values)
     return pl.pallas_call(
         functools.partial(kernel, row_blocks << 10),
-        out_shape=jax.ShapeDtypeStruct((row_blocks + 1, half, size), jnp.float32),
-        in_specs=[pl.BlockSpec(memory_space=pltpu.SMEM)]
+        out_shape=out_shape,
+        in_specs=[smem]
         + [pl.BlockSpec(memory_space=pl.ANY)] * len(pieces)
-        + [hbm] * 2
-        + [vmem] * len(before),
-        out_specs=vmem,
+        + [smem if array.ndim == 1 else vmem for array in whole],
+        out_specs=[vmem] * len(out_shape),
         scratch_shapes=[
-            pltpu.VMEM((2 * len(pieces),) + pieces[0].shape[1:], jnp.bfloat16),
-            pltpu.VMEM((2, slots + GROUP, size, size), jnp.bfloat16),
-            pltpu.SMEM((2, slots + GROUP), jnp.int32),
-            pltpu.SemaphoreType.DMA((len(pieces) + 2,)),
+            pltpu.VMEM((there,) + pieces[0].shape[1:], jnp.bfloat16),
+            pltpu.SemaphoreType.DMA((len(pieces),)),
         ],
-        compiler_params=pltpu.CompilerParams(vmem_limit_bytes=26 * 2**20),
-        cost_estimate=pl.CostEstimate(
-            flops=4 * slots * size * size * half, bytes_accessed=16 * 2**20, transcendentals=0
-        ),
-    )(packed, *pieces, own_values, other_values, *before)
+        compiler_params=pltpu.CompilerParams(vmem_limit_bytes=VMEM_ASK),
+        cost_estimate=pl.CostEstimate(flops=flops, bytes_accessed=12 * 2**20, transcendentals=0),
+    )(lists, *pieces, *whole)
 
 
 def code_into(total, out):
@@ -155,13 +149,6 @@
 def step_of(coded):
     last = coded.shape[0] - 1
     return jnp.exp2(coded[last].astype(jnp.int32).astype(jnp.float32) * (1.0 / FINE))
-
-
-def first_kernel(place, index, share, out_right, out_left):
-    half = out_right.shape[0] - 1
-    here = index[place]
-    code_into(share.at[pl.ds(here, half)], out_right)
-    code_into(share.at[pl.ds(here + half, half)], out_left)
 
 
 def pass_kernel(place, begin, index, share, coded, out, total):
@@ -348,18 +335,40 @@
     values, other_basis = lax.optimization_barrier((values, other_basis))
     other_values = move(values, swap)
 
+    low, high = slice(0, half), slice(half, None)
+    chunk = jnp.stack([jnp.where(core == 0, array[low], array[high]) for array in (basis, other_basis)])
+    chunk, block_row, block_col, block_count = lax.optimization_barrier((chunk, block_row, block_col, block_count))
+
     def packed_for(which):
         slot = lax.broadcasted_iota(jnp.int32, block_row.shape, 1)
         source, offset = block_col >> 4, block_col & 15
         dx, dy = ((source >> 2) - x) & 3, (source - y) & 3
         near, far = jnp.where(which == 0, dx, dy), jnp.where(which == 0, dy, dx)
-        key = jnp.where(slot < block_count, jnp.where(far == 2, 1, 0), 2)
-        return key | (offset << 2) | (near << 6) | (far << 8) | (block_row << 10) | (slot << 19)
-
-    packed = jnp.concatenate([packed_for(core), move(packed_for(1 - core), swap)])
-
-    chunk = lax.dynamic_slice_in_dim(jnp.stack([basis, other_basis]), core * half, half, 1)
+        middle = ((far == 1) & (near < 2)) | ((far == 3) & (near >= 2))
+        stage = jnp.where(far == 2, 2, jnp.where(middle, 1, 0))
+        place = near + jnp.where(stage > 0, 0, jnp.where(far == 0, 0, jnp.where(far == 1, 2, 6)))
+        stage = jnp.where(slot < block_count, stage, 3)
+        return stage | (offset << 2) | (place << 6) | (block_row << 10) | (slot << 19)
+
+    def listed(packed):
+        key = packed[0] & 3
+        place = jnp.arange(slots, dtype=jnp.int32)
+        order = key * slots + place
+        rank = jnp.sum((order[:, None] < order[None, :]).astype(jnp.int32), axis=0)
+        entries = jnp.sum(jnp.where(rank[None, :] == place[:, None], packed, 0), axis=1)
+        begins = jnp.sum((key[None, :] < place[:4, None]).astype(jnp.int32), axis=1)
+        counts = jnp.sum((key[None, :] == place[: slots - 4, None]).astype(jnp.int32), axis=1)
+        return jnp.concatenate([entries, begins, counts])[None]
+
+    other_lists = move(listed(packed_for(1 - core)), swap)
     from_low, from_high = move(chunk, first(1)), move(chunk, first(-1))
+    depth = cols // 2
+    index = ((z + jnp.arange(depth, dtype=jnp.int32)) & (depth - 1)) * (2 * per_device)
+    which = core[None].astype(jnp.int32)
+    from_low, from_high, other_lists, index, which = lax.optimization_barrier(
+        (from_low, from_high, other_lists, index, which)
+    )
+    lists = jnp.concatenate([listed(packed_for(core)), other_lists])
     a0 = jnp.stack([chunk, from_high])
     across = jnp.stack([move(from_low[0], first(1)), move(from_high[1], first(-1))])
     a3, a1 = move(a0, second(1)), move(a0, second(-1))
@@ -367,19 +376,24 @@
     b1, b3 = move(b0, second(-1)), move(b0, second(1))
     a2, b2 = move(a3, second(1)), move(b1, second(-1))
 
-    share = add_blocks(early_kernel, packed, (a0, b0, a1, b1, a3, b3), values, other_values, (), row_blocks)
-    share = add_blocks(late_kernel, packed, (a2, b2), values, other_values, (share,), row_blocks)
-
-    depth = cols // 2
     coded = jax.ShapeDtypeStruct((2 * per_device + 1, half, size), jnp.int16)
     part = jax.ShapeDtypeStruct((per_device + 1, half, size), jnp.int16)
     scratch = [pltpu.VMEM((2 * per_device, half, size), jnp.float32)]
-    index = ((z + jnp.arange(depth, dtype=jnp.int32)) & (depth - 1)) * (2 * per_device)
+
+    total = jax.ShapeDtypeStruct((row_blocks + 1, half, size), jnp.float32)
+    blocks = jax.ShapeDtypeStruct((2,) + values.shape, jnp.bfloat16)
+    work = 4 * slots * size * size * half
+    share, blocks = add_blocks(
+        early_kernel, work // 2, lists, (a0, b0, b1, a3), (values, other_values), (), (total, blocks), row_blocks
+    )
+    (share,) = add_blocks(middle_kernel, work // 4, lists, (a1, b3), (), (blocks, share), (total,), row_blocks)
+    share, right, left = add_blocks(
+        late_kernel, work // 4, lists, (a2, b2), (), (index, blocks, share), (total, part, part), row_blocks
+    )
 
     def run(kernel, d, arrays, shapes, scratch=()):
         return on_chunk(functools.partial(kernel, d % depth), index, share, arrays, shapes, scratch)
 
-    right, left = run(first_kernel, depth // 2, [], [part, part])
     for d in range(depth // 2 - 1, 0, -1):
         right, left = move(right, deep(1)), move(left, deep(-1))
         begin = per_device if d == depth // 2 - 1 else 0
@@ -388,7 +402,7 @@
     right, left = move(right, deep(1)), move(left, deep(-1))
     whole = jax.ShapeDtypeStruct((2 * per_device, half, size), jnp.float32)
     (ours,) = run(last_kernel, 0, [right, left], [whole])
-    mine, gram = local_gram(core[None].astype(jnp.int32), ours, move(ours, swap))
+    mine, gram = local_gram(which, ours, move(ours, swap))
 
     def spread(array, axis, groups):
         count = len(groups[0])

time: 131 us -> 121 us (0.924)
  Pallas kernels: 25 us -> 19.7 us
  waiting for transfers between devices: 40.2 us -> 35.7 us
  local copies, waits for them, and re-layouts: 2.25 us -> 0.06 us
  blocking collectives: 26.6 us -> 28.6 us
    pallas_call x2 -> x3, Pallas kernels: 14.5 us -> 9.91 us  [add_blocks(): pl.pallas_call(functools.partial(kernel, row_blocks << 10), out_shape=out...]
    ppermute x22, waiting for transfers between devices: 40.2 us -> 35.7 us  [move(): return lax.ppermute(array, BOTH, pairs)]
    unnamed x8 -> x2, local copies, waits for them, and re-layouts: 2.2 us -> 0.01 us
    all_to_all x2, blocking collectives: 26.6 us -> 28.6 us  [spread(): return lax.all_to_all(copies, axis, 0, 0, axis_index_groups=groups)]
    pallas_call x8 -> x7, Pallas kernels: 5.39 us -> 4.75 us  [on_chunk(): pl.pallas_call(kernel, out_shape=out_shape, in_specs=[pl.BlockSpec(memory...]
  transfers between devices with their start and end apart: 22 -> 22, of which waited for: 12 -> 16; matrix products, arithmetic and copies ran while one was open for 2% -> 2% of each run, Pallas kernels for 10% -> 9%
where the time goes in v3:
time: 121 us; the launch traced here: 120 us
  waiting for transfers between devices  35.7 us (30%)
  starting transfers between devices  32 us (26%)
  blocking collectives  28.6 us (24%)
  Pallas kernels  19.7 us (16%)
  other arithmetic  2.89 us (2%)
  between operations  1.55 us (1%)
    ppermute x22, waiting for transfers between devices, move(): return lax.ppermute(array, BOTH, pairs)  35.7 us
    ppermute x22, starting transfers between devices, move(): return lax.ppermute(array, BOTH, pairs)  32 us
    all_to_all x2, blocking collectives, spread(): return lax.all_to_all(copies, axis, 0, 0, axis_index_groups=groups)  28.6 us
    pallas_call x3, Pallas kernels, add_blocks(): pl.pallas_call(functools.partial(kernel, row_blocks << 10), out_shape=out...  9.91 us
    pallas_call x7, Pallas kernels, on_chunk(): pl.pallas_call(kernel, out_shape=out_shape, in_specs=[pl.BlockSpec(memory...  4.75 us
    pallas_call x1, Pallas kernels, finish(): pl.pallas_call(functools.partial(finish_kernel, scale), out_shape=(jax.Sh...  3.97 us
  transfers between devices with their start and end apart: 22, of which 16 were waited for; matrix products, arithmetic and copies ran while one was open for 2% of the time, Pallas kernels for 9%

profile of v3, /device:TPU:8, one launch (start us, length us, event | category | flops | bytes accessed | tf_op | source)
XLA Modules:
  0.0 120.5 jit_solution(11823592091186441817)
XLA Ops:
  1.4 1.1 select_bitcast_fusion.1
  3.2 1.6 %collective-permute-start.1 = (bf16[2,32,2048]{2,1,0:T(8,128)(2,1)S(1)}, bf16[2,32,2048]{2,1,0:T(8,128)(2,1)S(1)}, u32[]{:S(2)}, u32[]{:S(2)}) collective-permute-start(bf16[2,32,2048]{2,1,0:T(8,128)(2,1)S(1)} %pad_maximum_fusion.2), channel_id=1, source_target_pairs={{0,64},{1,17},{2,66},{3,19},{4,68},{5,21},{6,70},{7,23},{8,72},{9,... | collective-permute-start | bytes 786440 | tf_op jit(solution)/shard_map/ppermute | solution.py:328
  4.7 1.7 %collective-permute-start.2 = (bf16[2,32,2048]{2,1,0:T(8,128)(2,1)S(1)}, bf16[2,32,2048]{2,1,0:T(8,128)(2,1)S(1)}, u32[]{:S(2)}, u32[]{:S(2)}) collective-permute-start(bf16[2,32,2048]{2,1,0:T(8,128)(2,1)S(1)} %pad_maximum_fusion.2), channel_id=1, source_target_pairs={{0,192},{1,49},{2,194},{3,51},{4,196},{5,53},{6,198},{7,55},{8,200... | collective-permute-start | bytes 786440 | tf_op jit(solution)/shard_map/ppermute | solution.py:328
  8.0 2.0 %collective-permute-done.3 = s32[1,256]{1,0:T(1,128)S(1)} collective-permute-done((s32[1,256]{1,0:T(1,128)S(1)}, s32[1,256]{1,0:T(1,128)S(1)}, u32[]{:S(2)}, u32[]{:S(2)}) %collective-permute-start.3) | collective-permute-done | bytes 1056 | tf_op jit(solution)/shard_map/ppermute | solution.py:328
  9.9 0.9 collective-permute-done.1
  11.1 1.6 %collective-permute-start.6 = (bf16[32,2048]{1,0:T(8,128)(2,1)S(1)}, bf16[32,2048]{1,0:T(8,128)(2,1)S(1)}, u32[]{:S(2)}, u32[]{:S(2)}) collective-permute-start(bf16[32,2048]{1,0:T(8,128)(2,1)S(1)} %slice_bitcast_fusion.1), channel_id=1, source_target_pairs={{0,64},{1,17},{2,66},{3,19},{4,68},{5,21},{6,70},{7,23},{8,72},{9,... | collective-permute-start | bytes 393224 | tf_op jit(solution)/shard_map/ppermute | solution.py:328
  12.7 1.8 %collective-permute-start.7 = (bf16[32,2048]{1,0:T(8,128)(2,1)S(1)}, bf16[32,2048]{1,0:T(8,128)(2,1)S(1)}, u32[]{:S(2)}, u32[]{:S(2)}) collective-permute-start(bf16[32,2048]{1,0:T(8,128)(2,1)S(1)} %slice_bitcast_fusion), channel_id=1, source_target_pairs={{0,192},{1,49},{2,194},{3,51},{4,196},{5,53},{6,198},{7,55},{8,200... | collective-permute-start | bytes 393224 | tf_op jit(solution)/shard_map/ppermute | solution.py:328
  14.6 1.7 %collective-permute-start.4 = (bf16[2,2,32,2048]{3,2,1,0:T(8,128)(2,1)S(1)}, bf16[2,2,32,2048]{3,2,1,0:T(8,128)(2,1)S(1)}, u32[]{:S(2)}, u32[]{:S(2)}) collective-permute-start(bf16[2,2,32,2048]{3,2,1,0:T(8,128)(2,1)S(1)} %pad_maximum_fusion.a0), channel_id=1, source_target_pairs={{0,16},{1,65},{2,18},{3,67},{4,20},{5,69},{6,22},{7,71},{8,24},{9,... | collective-permute-start | bytes 1572872 | tf_op jit(solution)/shard_map/ppermute | solution.py:328
  16.2 2.3 %collective-permute-done.6 = bf16[32,2048]{1,0:T(8,128)(2,1)S(1)} collective-permute-done((bf16[32,2048]{1,0:T(8,128)(2,1)S(1)}, bf16[32,2048]{1,0:T(8,128)(2,1)S(1)}, u32[]{:S(2)}, u32[]{:S(2)}) %collective-permute-start.6) | collective-permute-done | bytes 131104 | tf_op jit(solution)/shard_map/ppermute | solution.py:328
  18.6 0.8 collective-permute-start.8
  19.5 2.0 %collective-permute-start.11 = (bf16[2,2,32,2048]{3,2,1,0:T(8,128)(2,1)S(1)}, bf16[2,2,32,2048]{3,2,1,0:T(8,128)(2,1)S(1)}, u32[]{:S(2)}, u32[]{:S(2)}) collective-permute-start(bf16[2,2,32,2048]{3,2,1,0:T(8,128)(2,1)S(1)} %pad_maximum_fusion.a0), channel_id=1, source_target_pairs={{0,48},{1,193},{2,50},{3,195},{4,52},{5,197},{6,54},{7,199},{8,56}... | collective-permute-start | bytes 1572872 | tf_op jit(solution)/shard_map/ppermute | solution.py:328
  21.5 2.4 %collective-permute-done.4.a3 = bf16[2,2,32,2048]{3,2,1,0:T(8,128)(2,1)S(1)} collective-permute-done((bf16[2,2,32,2048]{3,2,1,0:T(8,128)(2,1)S(1)}, bf16[2,2,32,2048]{3,2,1,0:T(8,128)(2,1)S(1)}, u32[]{:S(2)}, u32[]{:S(2)}) %collective-permute-start.4) | collective-permute-done | bytes 524320 | tf_op jit(solution)/shard_map/ppermute | solution.py:328
  23.9 1.6 %collective-permute-start.5 = (bf16[2,2,32,2048]{3,2,1,0:T(8,128)(2,1)S(1)}, bf16[2,2,32,2048]{3,2,1,0:T(8,128)(2,1)S(1)}, u32[]{:S(2)}, u32[]{:S(2)}) collective-permute-start(bf16[2,2,32,2048]{3,2,1,0:T(8,128)(2,1)S(1)} %collective-permute-done.4.a3), channel_id=1, source_target_pairs={{0,16},{1,65},{2,18},{3,67},{4,20},{5,69},{6,22},{7,71},{8,24},{9,... | collective-permute-start | bytes 1572872 | tf_op jit(solution)/shard_map/ppermute | solution.py:328
  25.4 2.5 %collective-permute-done.8.b1 = bf16[2,2,32,2048]{3,2,1,0:T(8,128)(2,1)S(1)} collective-permute-done((bf16[2,2,32,2048]{3,2,1,0:T(8,128)(2,1)S(1)}, bf16[2,2,32,2048]{3,2,1,0:T(8,128)(2,1)S(1)}, u32[]{:S(2)}, u32[]{:S(2)}) %collective-permute-start.8) | collective-permute-done | bytes 524320 | tf_op jit(solution)/shard_map/ppermute | solution.py:328
  28.9 4.4 %shard_map.68 = (f32[257,32,128]{2,1,0:T(8,128)S(1)}, bf16[2,128,128,128]{3,2,1,0:T(8,128)(2,1)S(1)}) custom-call(s32[2,256]{1,0:T(2,128)S(1)} %pad_add_fusion.lists, bf16[2,2,32,2048]{3,2,1,0:T(8,128)(2,1)S(1)} %pad_maximum_fusion.a0, bf16[2,2,32,2048]{3,2,1,0:T(8,128)(2,1)S(1)} %pad_maximum_fusion.1.b0, ...), custom_call_target="tpu_custom_call" | custom-call | flops 134217728 | bytes 12582912 | tf_op jit(solution)/shard_map/pallas_call | solution.py:116
  33.5 2.9 %shard_map.69.share = f32[257,32,128]{2,1,0:T(8,128)S(1)} custom-call(s32[2,256]{1,0:T(2,128)S(1)} %pad_add_fusion.lists, bf16[2,2,32,2048]{3,2,1,0:T(8,128)(2,1)S(1)} %collective-permute-done.11.a1, bf16[2,2,32,2048]{3,2,1,0:T(8,128)(2,1)S(1)} %collective-permute-done.12.b3, bf16[2,128,128,128]{3,2,1,0:T(8,128)(2,1)S(1)} %get-tuple-element.31.blocks, ...), custom_call_target="tpu_custom_call" | custom-call | flops 67108864 | bytes 12582912 | tf_op jit(solution)/shard_map/pallas_call | solution.py:116
  36.4 2.7 %collective-permute-done.9.b2 = bf16[2,2,32,2048]{3,2,1,0:T(8,128)(2,1)S(1)} collective-permute-done((bf16[2,2,32,2048]{3,2,1,0:T(8,128)(2,1)S(1)}, bf16[2,2,32,2048]{3,2,1,0:T(8,128)(2,1)S(1)}, u32[]{:S(2)}, u32[]{:S(2)}) %collective-permute-start.9) | collective-permute-done | bytes 524320 | tf_op jit(solution)/shard_map/ppermute | solution.py:328
  39.1 2.6 %shard_map.70 = (f32[257,32,128]{2,1,0:T(8,128)S(1)}, s16[17,32,128]{2,1,0:T(8,128)(2,1)S(1)}, s16[17,32,128]{2,1,0:T(8,128)(2,1)S(1)}) custom-call(s32[2,256]{1,0:T(2,128)S(1)} %pad_add_fusion.lists, bf16[2,2,32,2048]{3,2,1,0:T(8,128)(2,1)S(1)} %collective-permute-done.5.a2, bf16[2,2,32,2048]{3,2,1,0:T(8,128)(2,1)S(1)} %collective-permute-done.9.b2, ...), custom_call_target="tpu_custom_call" | custom-call | flops 67108864 | bytes 12582912 | tf_op jit(solution)/shard_map/pallas_call | solution.py:116
  41.7 5.8 %collective-permute-start.17 = (s16[17,32,128]{2,1,0:T(8,128)(2,1)S(1)}, s16[17,32,128]{2,1,0:T(8,128)(2,1)S(1)}, u32[]{:S(2)}, u32[]{:S(2)}) collective-permute-start(s16[17,32,128]{2,1,0:T(8,128)(2,1)S(1)} %get-tuple-element.35), channel_id=1, source_target_pairs={{0,14},{1,15},{2,0},{3,1},{4,2},{5,3},{6,4},{7,5},{8,6},{9,7},{10,... | collective-permute-start | bytes 417800 | tf_op jit(solution)/shard_map/ppermute | solution.py:328
  47.5 2.6 %collective-permute-done.17.refs_2_ = s16[17,32,128]{2,1,0:T(8,128)(2,1)S(1)} collective-permute-done((s16[17,32,128]{2,1,0:T(8,128)(2,1)S(1)}, s16[17,32,128]{2,1,0:T(8,128)(2,1)S(1)}, u32[]{:S(2)}, u32[]{:S(2)}) %collective-permute-start.17) | collective-permute-done | bytes 139296 | tf_op jit(solution)/shard_map/ppermute | solution.py:328
  50.8 3.8 %collective-permute-start.18 = (s16[33,32,128]{2,1,0:T(8,128)(2,1)S(1)}, s16[33,32,128]{2,1,0:T(8,128)(2,1)S(1)}, u32[]{:S(2)}, u32[]{:S(2)}) collective-permute-start(s16[33,32,128]{2,1,0:T(8,128)(2,1)S(1)} %shard_map.74), channel_id=1, source_target_pairs={{0,14},{1,15},{2,0},{3,1},{4,2},{5,3},{6,4},{7,5},{8,6},{9,7},{10,... | collective-permute-start | bytes 811016 | tf_op jit(solution)/shard_map/ppermute | solution.py:328
  55.4 4.3 %collective-permute-done.18.refs_2_ = s16[33,32,128]{2,1,0:T(8,128)(2,1)S(1)} collective-permute-done((s16[33,32,128]{2,1,0:T(8,128)(2,1)S(1)}, s16[33,32,128]{2,1,0:T(8,128)(2,1)S(1)}, u32[]{:S(2)}, u32[]{:S(2)}) %collective-permute-start.18) | collective-permute-done | bytes 270368 | tf_op jit(solution)/shard_map/ppermute | solution.py:328
  60.4 3.8 %collective-permute-start.19 = (s16[33,32,128]{2,1,0:T(8,128)(2,1)S(1)}, s16[33,32,128]{2,1,0:T(8,128)(2,1)S(1)}, u32[]{:S(2)}, u32[]{:S(2)}) collective-permute-start(s16[33,32,128]{2,1,0:T(8,128)(2,1)S(1)} %shard_map.75), channel_id=1, source_target_pairs={{0,14},{1,15},{2,0},{3,1},{4,2},{5,3},{6,4},{7,5},{8,6},{9,7},{10,... | collective-permute-start | bytes 811016 | tf_op jit(solution)/shard_map/ppermute | solution.py:328
  65.2 5.3 %collective-permute-done.19.refs_2_ = s16[33,32,128]{2,1,0:T(8,128)(2,1)S(1)} collective-permute-done((s16[33,32,128]{2,1,0:T(8,128)(2,1)S(1)}, s16[33,32,128]{2,1,0:T(8,128)(2,1)S(1)}, u32[]{:S(2)}, u32[]{:S(2)}) %collective-permute-start.19) | collective-permute-done | bytes 270368 | tf_op jit(solution)/shard_map/ppermute | solution.py:328
  71.1 3.8 %collective-permute-start.20 = (s16[33,32,128]{2,1,0:T(8,128)(2,1)S(1)}, s16[33,32,128]{2,1,0:T(8,128)(2,1)S(1)}, u32[]{:S(2)}, u32[]{:S(2)}) collective-permute-start(s16[33,32,128]{2,1,0:T(8,128)(2,1)S(1)} %shard_map.76), channel_id=1, source_target_pairs={{0,14},{1,15},{2,0},{3,1},{4,2},{5,3},{6,4},{7,5},{8,6},{9,7},{10,... | collective-permute-start | bytes 811016 | tf_op jit(solution)/shard_map/ppermute | solution.py:328
  76.2 2.7 %collective-permute-done.20.left = s16[33,32,128]{2,1,0:T(8,128)(2,1)S(1)} collective-permute-done((s16[33,32,128]{2,1,0:T(8,128)(2,1)S(1)}, s16[33,32,128]{2,1,0:T(8,128)(2,1)S(1)}, u32[]{:S(2)}, u32[]{:S(2)}) %collective-permute-start.20) | collective-permute-done | bytes 270368 | tf_op jit(solution)/shard_map/ppermute | solution.py:328
  78.9 5.0 %collective-permute-done.16.right = s16[33,32,128]{2,1,0:T(8,128)(2,1)S(1)} collective-permute-done((s16[33,32,128]{2,1,0:T(8,128)(2,1)S(1)}, s16[33,32,128]{2,1,0:T(8,128)(2,1)S(1)}, u32[]{:S(2)}, u32[]{:S(2)}) %collective-permute-start.16) | collective-permute-done | bytes 270368 | tf_op jit(solution)/shard_map/ppermute | solution.py:328
  84.8 1.9 %collective-permute-done.21.theirs = f32[32,32,128]{2,1,0:T(8,128)S(1)} collective-permute-done((f32[32,32,128]{2,1,0:T(8,128)S(1)}, f32[32,32,128]{2,1,0:T(8,128)S(1)}, u32[]{:S(2)}, u32[]{:S(2)}) %collective-permute-start.21) | collective-permute-done | bytes 524320 | tf_op jit(solution)/shard_map/ppermute | solution.py:328
  86.7 1.1 shard_map.78
  87.8 12.1 %all_to_all.10 = f32[8,32,128]{2,1,0:T(8,128)S(1)} all-to-all(f32[8,32,128]{2,1,0:T(8,128)S(1)} %broadcast_in_dim.88), channel_id=1, replica_groups={{0,2,4,6,8,10,12,14},{1,3,5,7,9,11,13,15},{16,18,20,22,24,26,28,30},{17..., dimensions={0} | all-to-all | bytes 262144 | tf_op jit(solution)/shard_map/all_to_all | solution.py:410
  100.0 16.5 %all_to_all.11.grams = f32[16,32,128]{2,1,0:T(8,128)S(1)} all-to-all(f32[16,32,128]{2,1,0:T(8,128)S(1)} %broadcast_in_dim.89), channel_id=1, replica_groups={{0,16,32,48,64,80,96,112,128,144,160,176,192,208,224,240},{1,17,33,49,6..., dimensions={0} | all-to-all | bytes 524288 | tf_op jit(solution)/shard_map/all_to_all | solution.py:410
  116.5 4.0 %shard_map.79 = (f32[64,2048]{1,0:T(8,128)}, f32[64,64]{1,0:T(8,128)}) custom-call(f32[16,32,128]{2,1,0:T(8,128)S(1)} %all_to_all.11.grams, f32[16,64,128]{2,1,0:T(8,128)S(1)} %get-tuple-element.37.mine), custom_call_target="tpu_custom_call" | custom-call | tf_op jit(solution)/shard_map/pallas_call | solution.py:271
  (53 shorter events, 9.9 us)
Async XLA Ops:
  0.6 1.9 %collective-permute-start = (bf16[64,2048]{1,0:T(8,128)(2,1)}, bf16[64,2048]{1,0:T(8,128)(2,1)S(1)}, u32[]{:S(2)}, u32[]{:S(2)}) collective-permute-start(bf16[64,2048]{1,0:T(8,128)(2,1)} %param.5), channel_id=1, source_target_pairs={{0,1},{1,0},{2,3},{3,2},{4,5},{5,4},{6,7},{7,6},{8,9},{9,8},{10,11... | collective-permute-start | bytes 786440 | tf_op jit(solution)/shard_map/ppermute | solution.py:328
  1.4 27.5 %copy-start = (bf16[128,128,128]{2,1,0:T(8,128)(2,1)S(1)}, bf16[128,128,128]{2,1,0:T(8,128)(2,1)}, u32[]{:S(2)}) copy-start(bf16[128,128,128]{2,1,0:T(8,128)(2,1)} %own_values) | copy-start | bytes 12582916
  2.6 26.3 %collective-permute-start.10 = (bf16[128,128,128]{2,1,0:T(8,128)(2,1)}, bf16[128,128,128]{2,1,0:T(8,128)(2,1)S(1)}, u32[]{:S(2)}, u32[]{:S(2)}) collective-permute-start(bf16[128,128,128]{2,1,0:T(8,128)(2,1)} %own_values), channel_id=1, source_target_pairs={{0,1},{1,0},{2,3},{3,2},{4,5},{5,4},{6,7},{7,6},{8,9},{9,8},{10,11... | collective-permute-start | bytes 12582920 | tf_op jit(solution)/shard_map/ppermute | solution.py:328
  3.2 7.7 %collective-permute-start.1 = (bf16[2,32,2048]{2,1,0:T(8,128)(2,1)S(1)}, bf16[2,32,2048]{2,1,0:T(8,128)(2,1)S(1)}, u32[]{:S(2)}, u32[]{:S(2)}) collective-permute-start(bf16[2,32,2048]{2,1,0:T(8,128)(2,1)S(1)} %pad_maximum_fusion.2), channel_id=1, source_target_pairs={{0,64},{1,17},{2,66},{3,19},{4,68},{5,21},{6,70},{7,23},{8,72},{9,... | collective-permute-start | bytes 786440 | tf_op jit(solution)/shard_map/ppermute | solution.py:328
  4.7 6.4 %collective-permute-start.2 = (bf16[2,32,2048]{2,1,0:T(8,128)(2,1)S(1)}, bf16[2,32,2048]{2,1,0:T(8,128)(2,1)S(1)}, u32[]{:S(2)}, u32[]{:S(2)}) collective-permute-start(bf16[2,32,2048]{2,1,0:T(8,128)(2,1)S(1)} %pad_maximum_fusion.2), channel_id=1, source_target_pairs={{0,192},{1,49},{2,194},{3,51},{4,196},{5,53},{6,198},{7,55},{8,200... | collective-permute-start | bytes 786440 | tf_op jit(solution)/shard_map/ppermute | solution.py:328
  7.9 2.0 %collective-permute-start.3 = (s32[1,256]{1,0:T(1,128)S(1)}, s32[1,256]{1,0:T(1,128)S(1)}, u32[]{:S(2)}, u32[]{:S(2)}) collective-permute-start(s32[1,256]{1,0:T(1,128)S(1)} %bitcast.40), channel_id=1, source_target_pairs={{0,1},{1,0},{2,3},{3,2},{4,5},{5,4},{6,7},{7,6},{8,9},{9,8},{10,11... | collective-permute-start | bytes 3080 | tf_op jit(solution)/shard_map/ppermute | solution.py:328
  11.1 7.4 %collective-permute-start.6 = (bf16[32,2048]{1,0:T(8,128)(2,1)S(1)}, bf16[32,2048]{1,0:T(8,128)(2,1)S(1)}, u32[]{:S(2)}, u32[]{:S(2)}) collective-permute-start(bf16[32,2048]{1,0:T(8,128)(2,1)S(1)} %slice_bitcast_fusion.1), channel_id=1, source_target_pairs={{0,64},{1,17},{2,66},{3,19},{4,68},{5,21},{6,70},{7,23},{8,72},{9,... | collective-permute-start | bytes 393224 | tf_op jit(solution)/shard_map/ppermute | solution.py:328
  12.7 5.8 %collective-permute-start.7 = (bf16[32,2048]{1,0:T(8,128)(2,1)S(1)}, bf16[32,2048]{1,0:T(8,128)(2,1)S(1)}, u32[]{:S(2)}, u32[]{:S(2)}) collective-permute-start(bf16[32,2048]{1,0:T(8,128)(2,1)S(1)} %slice_bitcast_fusion), channel_id=1, source_target_pairs={{0,192},{1,49},{2,194},{3,51},{4,196},{5,53},{6,198},{7,55},{8,200... | collective-permute-start | bytes 393224 | tf_op jit(solution)/shard_map/ppermute | solution.py:328
  14.6 9.3 %collective-permute-start.4 = (bf16[2,2,32,2048]{3,2,1,0:T(8,128)(2,1)S(1)}, bf16[2,2,32,2048]{3,2,1,0:T(8,128)(2,1)S(1)}, u32[]{:S(2)}, u32[]{:S(2)}) collective-permute-start(bf16[2,2,32,2048]{3,2,1,0:T(8,128)(2,1)S(1)} %pad_maximum_fusion.a0), channel_id=1, source_target_pairs={{0,16},{1,65},{2,18},{3,67},{4,20},{5,69},{6,22},{7,71},{8,24},{9,... | collective-permute-start | bytes 1572872 | tf_op jit(solution)/shard_map/ppermute | solution.py:328
  18.6 9.3 %collective-permute-start.8 = (bf16[2,2,32,2048]{3,2,1,0:T(8,128)(2,1)S(1)}, bf16[2,2,32,2048]{3,2,1,0:T(8,128)(2,1)S(1)}, u32[]{:S(2)}, u32[]{:S(2)}) collective-permute-start(bf16[2,2,32,2048]{3,2,1,0:T(8,128)(2,1)S(1)} %pad_maximum_fusion.1.b0), channel_id=1, source_target_pairs={{0,48},{1,193},{2,50},{3,195},{4,52},{5,197},{6,54},{7,199},{8,56}... | collective-permute-start | bytes 1572872 | tf_op jit(solution)/shard_map/ppermute | solution.py:328
  19.5 14.0 %collective-permute-start.11 = (bf16[2,2,32,2048]{3,2,1,0:T(8,128)(2,1)S(1)}, bf16[2,2,32,2048]{3,2,1,0:T(8,128)(2,1)S(1)}, u32[]{:S(2)}, u32[]{:S(2)}) collective-permute-start(bf16[2,2,32,2048]{3,2,1,0:T(8,128)(2,1)S(1)} %pad_maximum_fusion.a0), channel_id=1, source_target_pairs={{0,48},{1,193},{2,50},{3,195},{4,52},{5,197},{6,54},{7,199},{8,56}... | collective-permute-start | bytes 1572872 | tf_op jit(solution)/shard_map/ppermute | solution.py:328
  21.4 12.1 %collective-permute-start.12 = (bf16[2,2,32,2048]{3,2,1,0:T(8,128)(2,1)S(1)}, bf16[2,2,32,2048]{3,2,1,0:T(8,128)(2,1)S(1)}, u32[]{:S(2)}, u32[]{:S(2)}) collective-permute-start(bf16[2,2,32,2048]{3,2,1,0:T(8,128)(2,1)S(1)} %pad_maximum_fusion.1.b0), channel_id=1, source_target_pairs={{0,16},{1,65},{2,18},{3,67},{4,20},{5,69},{6,22},{7,71},{8,24},{9,... | collective-permute-start | bytes 1572872 | tf_op jit(solution)/shard_map/ppermute | solution.py:328
  23.9 12.6 %collective-permute-start.5 = (bf16[2,2,32,2048]{3,2,1,0:T(8,128)(2,1)S(1)}, bf16[2,2,32,2048]{3,2,1,0:T(8,128)(2,1)S(1)}, u32[]{:S(2)}, u32[]{:S(2)}) collective-permute-start(bf16[2,2,32,2048]{3,2,1,0:T(8,128)(2,1)S(1)} %collective-permute-done.4.a3), channel_id=1, source_target_pairs={{0,16},{1,65},{2,18},{3,67},{4,20},{5,69},{6,22},{7,71},{8,24},{9,... | collective-permute-start | bytes 1572872 | tf_op jit(solution)/shard_map/ppermute | solution.py:328
  27.9 11.2 %collective-permute-start.9 = (bf16[2,2,32,2048]{3,2,1,0:T(8,128)(2,1)S(1)}, bf16[2,2,32,2048]{3,2,1,0:T(8,128)(2,1)S(1)}, u32[]{:S(2)}, u32[]{:S(2)}) collective-permute-start(bf16[2,2,32,2048]{3,2,1,0:T(8,128)(2,1)S(1)} %collective-permute-done.8.b1), channel_id=1, source_target_pairs={{0,48},{1,193},{2,50},{3,195},{4,52},{5,197},{6,54},{7,199},{8,56}... | collective-permute-start | bytes 1572872 | tf_op jit(solution)/shard_map/ppermute | solution.py:328
  41.7 8.4 %collective-permute-start.17 = (s16[17,32,128]{2,1,0:T(8,128)(2,1)S(1)}, s16[17,32,128]{2,1,0:T(8,128)(2,1)S(1)}, u32[]{:S(2)}, u32[]{:S(2)}) collective-permute-start(s16[17,32,128]{2,1,0:T(8,128)(2,1)S(1)} %get-tuple-element.35), channel_id=1, source_target_pairs={{0,14},{1,15},{2,0},{3,1},{4,2},{5,3},{6,4},{7,5},{8,6},{9,7},{10,... | collective-permute-start | bytes 417800 | tf_op jit(solution)/shard_map/ppermute | solution.py:328
  47.5 7.1 %collective-permute-start.13 = (s16[17,32,128]{2,1,0:T(8,128)(2,1)S(1)}, s16[17,32,128]{2,1,0:T(8,128)(2,1)S(1)}, u32[]{:S(2)}, u32[]{:S(2)}) collective-permute-start(s16[17,32,128]{2,1,0:T(8,128)(2,1)S(1)} %get-tuple-element.34), channel_id=1, source_target_pairs={{0,2},{1,3},{2,4},{3,5},{4,6},{5,7},{6,8},{7,9},{8,10},{9,11},{10,... | collective-permute-start | bytes 417800 | tf_op jit(solution)/shard_map/ppermute | solution.py:328
  50.8 8.9 %collective-permute-start.18 = (s16[33,32,128]{2,1,0:T(8,128)(2,1)S(1)}, s16[33,32,128]{2,1,0:T(8,128)(2,1)S(1)}, u32[]{:S(2)}, u32[]{:S(2)}) collective-permute-start(s16[33,32,128]{2,1,0:T(8,128)(2,1)S(1)} %shard_map.74), channel_id=1, source_target_pairs={{0,14},{1,15},{2,0},{3,1},{4,2},{5,3},{6,4},{7,5},{8,6},{9,7},{10,... | collective-permute-start | bytes 811016 | tf_op jit(solution)/shard_map/ppermute | solution.py:328
  55.3 9.1 %collective-permute-start.14 = (s16[33,32,128]{2,1,0:T(8,128)(2,1)S(1)}, s16[33,32,128]{2,1,0:T(8,128)(2,1)S(1)}, u32[]{:S(2)}, u32[]{:S(2)}) collective-permute-start(s16[33,32,128]{2,1,0:T(8,128)(2,1)S(1)} %shard_map.71), channel_id=1, source_target_pairs={{0,2},{1,3},{2,4},{3,5},{4,6},{5,7},{6,8},{7,9},{8,10},{9,11},{10,... | collective-permute-start | bytes 811016 | tf_op jit(solution)/shard_map/ppermute | solution.py:328
  60.4 10.0 %collective-permute-start.19 = (s16[33,32,128]{2,1,0:T(8,128)(2,1)S(1)}, s16[33,32,128]{2,1,0:T(8,128)(2,1)S(1)}, u32[]{:S(2)}, u32[]{:S(2)}) collective-permute-start(s16[33,32,128]{2,1,0:T(8,128)(2,1)S(1)} %shard_map.75), channel_id=1, source_target_pairs={{0,14},{1,15},{2,0},{3,1},{4,2},{5,3},{6,4},{7,5},{8,6},{9,7},{10,... | collective-permute-start | bytes 811016 | tf_op jit(solution)/shard_map/ppermute | solution.py:328
  65.1 10.3 %collective-permute-start.15 = (s16[33,32,128]{2,1,0:T(8,128)(2,1)S(1)}, s16[33,32,128]{2,1,0:T(8,128)(2,1)S(1)}, u32[]{:S(2)}, u32[]{:S(2)}) collective-permute-start(s16[33,32,128]{2,1,0:T(8,128)(2,1)S(1)} %shard_map.72), channel_id=1, source_target_pairs={{0,2},{1,3},{2,4},{3,5},{4,6},{5,7},{6,8},{7,9},{8,10},{9,11},{10,... | collective-permute-start | bytes 811016 | tf_op jit(solution)/shard_map/ppermute | solution.py:328
  71.1 7.7 %collective-permute-start.20 = (s16[33,32,128]{2,1,0:T(8,128)(2,1)S(1)}, s16[33,32,128]{2,1,0:T(8,128)(2,1)S(1)}, u32[]{:S(2)}, u32[]{:S(2)}) collective-permute-start(s16[33,32,128]{2,1,0:T(8,128)(2,1)S(1)} %shard_map.76), channel_id=1, source_target_pairs={{0,14},{1,15},{2,0},{3,1},{4,2},{5,3},{6,4},{7,5},{8,6},{9,7},{10,... | collective-permute-start | bytes 811016 | tf_op jit(solution)/shard_map/ppermute | solution.py:328
  76.1 7.7 %collective-permute-start.16 = (s16[33,32,128]{2,1,0:T(8,128)(2,1)S(1)}, s16[33,32,128]{2,1,0:T(8,128)(2,1)S(1)}, u32[]{:S(2)}, u32[]{:S(2)}) collective-permute-start(s16[33,32,128]{2,1,0:T(8,128)(2,1)S(1)} %shard_map.73), channel_id=1, source_target_pairs={{0,2},{1,3},{2,4},{3,5},{4,6},{5,7},{6,8},{7,9},{8,10},{9,11},{10,... | collective-permute-start | bytes 811016 | tf_op jit(solution)/shard_map/ppermute | solution.py:328
  84.5 2.2 %collective-permute-start.21 = (f32[32,32,128]{2,1,0:T(8,128)S(1)}, f32[32,32,128]{2,1,0:T(8,128)S(1)}, u32[]{:S(2)}, u32[]{:S(2)}) collective-permute-start(f32[32,32,128]{2,1,0:T(8,128)S(1)} %shard_map.77.ours), channel_id=1, source_target_pairs={{0,1},{1,0},{2,3},{3,2},{4,5},{5,4},{6,7},{7,6},{8,9},{9,8},{10,11... | collective-permute-start | bytes 1572872 | tf_op jit(solution)/shard_map/ppermute | solution.py:328

commit v4 on v3

--- a/solution.py
+++ b/solution.py
@@ -9,7 +9,7 @@
 from jax.sharding import PartitionSpec as P
 
 FINE = 16.0
-PANEL = 4
+PANEL = 8
 VMEM_ASK = 20 * 2**20
 HIGHEST = lax.Precision.HIGHEST
 
@@ -96,7 +96,7 @@
     add_stage(1, 16, filler, lists, slab, blocks, out)
 
 
-def late_kernel(filler, lists, a2, b2, index, blocks, share, out, out_right, out_left, slab, sems):
+def late_kernel(filler, lists, a2, b2, index, blocks, share, out, out_right, out_left, home, slab, sems):
     copies = load((a2, b2), slab, sems)
     out[...] = share[...]
     for copy in copies:
@@ -106,6 +106,7 @@
     far = index[4]
     code_into(out.at[pl.ds(far, half)], out_right)
     code_into(out.at[pl.ds(far + half, half)], out_left)
+    home[...] = out[pl.ds(index[0], home.shape[0])]
 
 
 def add_blocks(kernel, flops, lists, pieces, values, whole, out_shape, row_blocks):
@@ -163,13 +164,6 @@
     code_into(total, out)
 
 
-def last_kernel(place, index, share, right, left, out):
-    here = index[place]
-    step_right, step_left = step_of(right), step_of(left)
-    for b in range(out.shape[0]):
-        out[b] = share[here + b] + decoded(right, b, step_right) + decoded(left, b, step_left)
-
-
 def on_chunk(kernel, index, share, coded, out_shape, scratch=()):
     vmem = pl.BlockSpec(memory_space=pltpu.VMEM)
     return pl.pallas_call(
@@ -183,14 +177,16 @@
     )(index, share, *coded)
 
 
-def gram_kernel(core, ours, theirs, mine, out):
+def gram_kernel(core, ours, right, left, theirs, their_right, their_left, mine, out):
     count, half, _ = ours.shape
     first = core[0] == 0
+    parts = []
+    for home, one, two in ((ours, right, left), (theirs, their_right, their_left)):
+        step_one, step_two = step_of(one), step_of(two)
+        parts.append([home[b] + decoded(one, b, step_one) + decoded(two, b, step_two) for b in range(count)])
     blocks = []
-    for b in range(count):
-        low = jnp.where(first, ours[b], theirs[b])
-        high = jnp.where(first, theirs[b], ours[b])
-        blocks.append(jnp.concatenate([low, high], axis=0))
+    for own, other in zip(*parts):
+        blocks.append(jnp.concatenate([jnp.where(first, own, other), jnp.where(first, other, own)], axis=0))
     for b in range(count // 2):
         mine[b] = jnp.where(first, blocks[b], blocks[b + count // 2])
     wide = jnp.concatenate(blocks, axis=1)
@@ -201,8 +197,8 @@
     out[:, 2 * half :] = gram[half:]
 
 
-def local_gram(core, ours, theirs):
-    count, half, size = ours.shape
+def local_gram(core, *sums):
+    count, half, size = sums[0].shape
     vmem = pl.BlockSpec(memory_space=pltpu.VMEM)
     return pl.pallas_call(
         gram_kernel,
@@ -210,10 +206,11 @@
             jax.ShapeDtypeStruct((count // 2, 2 * half, size), jnp.float32),
             jax.ShapeDtypeStruct((half, 4 * half), jnp.float32),
         ),
-        in_specs=[pl.BlockSpec(memory_space=pltpu.SMEM), vmem, vmem],
+        in_specs=[pl.BlockSpec(memory_space=pltpu.SMEM)] + [vmem] * 6,
         out_specs=(vmem, vmem),
-        compiler_params=pltpu.CompilerParams(vmem_limit_bytes=8 * 2**20),
-    )(core, ours, theirs)
+        compiler_params=pltpu.CompilerParams(vmem_limit_bytes=10 * 2**20),
+        cost_estimate=pl.CostEstimate(flops=2**27, bytes_accessed=2**21, transcendentals=0),
+    )(core, *sums)
 
 
 def finish_kernel(scale, grams, mine, embedding, factor, work):
@@ -242,7 +239,6 @@
         for p in range(PANEL):
             pivot = columns[p][t][s + p : s + p + 1, :]
             root = lax.rsqrt(pivot)
-            root = root * (1.5 - 0.5 * (pivot * root) * root)
             rows[p] = rows[p] * root
             work[j + p : j + p + 1, :] = rows[p]
             scaled = {u: columns[p][u] * root for u in range(t, tiles)}
@@ -362,6 +358,7 @@
 
     other_lists = move(listed(packed_for(1 - core)), swap)
     from_low, from_high = move(chunk, first(1)), move(chunk, first(-1))
+    far_own, far_other = move(chunk[0], first(2)), move(chunk[1], first(-2))
     depth = cols // 2
     index = ((z + jnp.arange(depth, dtype=jnp.int32)) & (depth - 1)) * (2 * per_device)
     which = core[None].astype(jnp.int32)
@@ -370,7 +367,7 @@
     )
     lists = jnp.concatenate([listed(packed_for(core)), other_lists])
     a0 = jnp.stack([chunk, from_high])
-    across = jnp.stack([move(from_low[0], first(1)), move(from_high[1], first(-1))])
+    across = jnp.stack([far_own, far_other])
     a3, a1 = move(a0, second(1)), move(a0, second(-1))
     b0 = jnp.stack([across, from_low])
     b1, b3 = move(b0, second(-1)), move(b0, second(1))
@@ -387,9 +384,11 @@
         early_kernel, work // 2, lists, (a0, b0, b1, a3), (values, other_values), (), (total, blocks), row_blocks
     )
     (share,) = add_blocks(middle_kernel, work // 4, lists, (a1, b3), (), (blocks, share), (total,), row_blocks)
-    share, right, left = add_blocks(
-        late_kernel, work // 4, lists, (a2, b2), (), (index, blocks, share), (total, part, part), row_blocks
-    )
+    whole = jax.ShapeDtypeStruct((2 * per_device, half, size), jnp.float32)
+    share, right, left, home = add_blocks(
+        late_kernel, work // 4, lists, (a2, b2), (), (index, blocks, share), (total, part, part, whole), row_blocks
+    )
+    their_home = move(home, swap)
 
     def run(kernel, d, arrays, shapes, scratch=()):
         return on_chunk(functools.partial(kernel, d % depth), index, share, arrays, shapes, scratch)
@@ -400,9 +399,7 @@
         (right,) = run(lambda place, *refs: pass_kernel(place, 0, *refs), d, [right], [coded], scratch)
         (left,) = run(lambda place, *refs, begin=begin: pass_kernel(place, begin, *refs), -d, [left], [coded], scratch)
     right, left = move(right, deep(1)), move(left, deep(-1))
-    whole = jax.ShapeDtypeStruct((2 * per_device, half, size), jnp.float32)
-    (ours,) = run(last_kernel, 0, [right, left], [whole])
-    mine, gram = local_gram(which, ours, move(ours, swap))
+    mine, gram = local_gram(which, home, right, left, their_home, move(right, swap), move(left, swap))
 
     def spread(array, axis, groups):
         count = len(groups[0])

time: 121 us -> 115 us (0.950)
  Pallas kernels: 19.7 us -> 16.8 us
  starting transfers between devices: 32 us -> 30.7 us
    pallas_call x3, Pallas kernels: 9.91 us -> 8.49 us  [add_blocks(): pl.pallas_call(functools.partial(kernel, row_blocks << 10), out_shape=out...]
    ppermute x22 -> x24, starting transfers between devices: 32 us -> 30.7 us  [move(): return lax.ppermute(array, BOTH, pairs)]
    ppermute x22 -> x24, waiting for transfers between devices: 35.7 us -> 34.7 us  [move(): return lax.ppermute(array, BOTH, pairs)]
    pallas_call x7 -> x6, Pallas kernels: 4.75 us -> 4.06 us  [on_chunk(): pl.pallas_call(kernel, out_shape=out_shape, in_specs=[pl.BlockSpec(memory...]
  transfers between devices with their start and end apart: 22 -> 24, of which waited for: 16 -> 13; matrix products, arithmetic and copies ran while one was open for 2% -> 3% of each run, Pallas kernels for 9% -> 9%
where the time goes in v4:
time: 115 us; the launch traced here: 114 us
  waiting for transfers between devices  34.7 us (30%)
  starting transfers between devices  30.7 us (27%)
  blocking collectives  27.6 us (24%)
  Pallas kernels  16.8 us (15%)
  other arithmetic  2.88 us (3%)
  between operations  1.55 us (1%)
    ppermute x24, waiting for transfers between devices, move(): return lax.ppermute(array, BOTH, pairs)  34.7 us
    ppermute x24, starting transfers between devices, move(): return lax.ppermute(array, BOTH, pairs)  30.7 us
    all_to_all x2, blocking collectives, spread(): return lax.all_to_all(copies, axis, 0, 0, axis_index_groups=groups)  27.6 us
    pallas_call x3, Pallas kernels, add_blocks(): pl.pallas_call(functools.partial(kernel, row_blocks << 10), out_shape=out...  8.49 us
    pallas_call x6, Pallas kernels, on_chunk(): pl.pallas_call(kernel, out_shape=out_shape, in_specs=[pl.BlockSpec(memory...  4.06 us
    pallas_call x1, Pallas kernels, finish(): pl.pallas_call(functools.partial(finish_kernel, scale), out_shape=(jax.Sh...  3.1 us
  transfers between devices with their start and end apart: 24, of which 13 were waited for; matrix products, arithmetic and copies ran while one was open for 3% of the time, Pallas kernels for 9%

profile of v4, /device:TPU:8, one launch (start us, length us, event | category | flops | bytes accessed | tf_op | source)
XLA Modules:
  0.0 114.2 jit_solution(2658823476317558178)
XLA Ops:
  1.4 1.1 select_bitcast_fusion.1
  3.2 1.6 %collective-permute-start.1 = (bf16[2,32,2048]{2,1,0:T(8,128)(2,1)S(1)}, bf16[2,32,2048]{2,1,0:T(8,128)(2,1)S(1)}, u32[]{:S(2)}, u32[]{:S(2)}) collective-permute-start(bf16[2,32,2048]{2,1,0:T(8,128)(2,1)S(1)} %pad_maximum_fusion.2), channel_id=1, source_target_pairs={{0,64},{1,17},{2,66},{3,19},{4,68},{5,21},{6,70},{7,23},{8,72},{9,... | collective-permute-start | bytes 786440 | tf_op jit(solution)/shard_map/ppermute | solution.py:324
  4.8 1.7 %collective-permute-start.2 = (bf16[2,32,2048]{2,1,0:T(8,128)(2,1)S(1)}, bf16[2,32,2048]{2,1,0:T(8,128)(2,1)S(1)}, u32[]{:S(2)}, u32[]{:S(2)}) collective-permute-start(bf16[2,32,2048]{2,1,0:T(8,128)(2,1)S(1)} %pad_maximum_fusion.2), channel_id=1, source_target_pairs={{0,192},{1,49},{2,194},{3,51},{4,196},{5,53},{6,198},{7,55},{8,200... | collective-permute-start | bytes 786440 | tf_op jit(solution)/shard_map/ppermute | solution.py:324
  6.5 1.9 %collective-permute-start.6 = (bf16[32,2048]{1,0:T(8,128)(2,1)S(1)}, bf16[32,2048]{1,0:T(8,128)(2,1)S(1)}, u32[]{:S(2)}, u32[]{:S(2)}) collective-permute-start(bf16[32,2048]{1,0:T(8,128)(2,1)S(1)} %get-tuple-element.48), channel_id=1, source_target_pairs={{0,128},{1,33},{2,130},{3,35},{4,132},{5,37},{6,134},{7,39},{8,136... | collective-permute-start | bytes 393224 | tf_op jit(solution)/shard_map/ppermute | solution.py:324
  8.4 1.7 %collective-permute-start.7 = (bf16[32,2048]{1,0:T(8,128)(2,1)S(1)}, bf16[32,2048]{1,0:T(8,128)(2,1)S(1)}, u32[]{:S(2)}, u32[]{:S(2)}) collective-permute-start(bf16[32,2048]{1,0:T(8,128)(2,1)S(1)} %get-tuple-element.49), channel_id=1, source_target_pairs={{0,128},{1,33},{2,130},{3,35},{4,132},{5,37},{6,134},{7,39},{8,136... | collective-permute-start | bytes 393224 | tf_op jit(solution)/shard_map/ppermute | solution.py:324
  10.1 0.7 iota_add_fusion.1
  11.5 1.7 %collective-permute-done.6 = bf16[32,2048]{1,0:T(8,128)(2,1)S(1)} collective-permute-done((bf16[32,2048]{1,0:T(8,128)(2,1)S(1)}, bf16[32,2048]{1,0:T(8,128)(2,1)S(1)}, u32[]{:S(2)}, u32[]{:S(2)}) %collective-permute-start.6) | collective-permute-done | bytes 131104 | tf_op jit(solution)/shard_map/ppermute | solution.py:324
  13.2 1.7 %collective-permute-done.7 = bf16[32,2048]{1,0:T(8,128)(2,1)S(1)} collective-permute-done((bf16[32,2048]{1,0:T(8,128)(2,1)S(1)}, bf16[32,2048]{1,0:T(8,128)(2,1)S(1)}, u32[]{:S(2)}, u32[]{:S(2)}) %collective-permute-start.7) | collective-permute-done | bytes 131104 | tf_op jit(solution)/shard_map/ppermute | solution.py:324
  15.0 1.9 %collective-permute-start.8 = (bf16[2,2,32,2048]{3,2,1,0:T(8,128)(2,1)S(1)}, bf16[2,2,32,2048]{3,2,1,0:T(8,128)(2,1)S(1)}, u32[]{:S(2)}, u32[]{:S(2)}) collective-permute-start(bf16[2,2,32,2048]{3,2,1,0:T(8,128)(2,1)S(1)} %pad_maximum_fusion.1.b0), channel_id=1, source_target_pairs={{0,48},{1,193},{2,50},{3,195},{4,52},{5,197},{6,54},{7,199},{8,56}... | collective-permute-start | bytes 1572872 | tf_op jit(solution)/shard_map/ppermute | solution.py:324
  17.2 1.6 %collective-permute-start.12 = (bf16[2,2,32,2048]{3,2,1,0:T(8,128)(2,1)S(1)}, bf16[2,2,32,2048]{3,2,1,0:T(8,128)(2,1)S(1)}, u32[]{:S(2)}, u32[]{:S(2)}) collective-permute-start(bf16[2,2,32,2048]{3,2,1,0:T(8,128)(2,1)S(1)} %pad_maximum_fusion.1.b0), channel_id=1, source_target_pairs={{0,16},{1,65},{2,18},{3,67},{4,20},{5,69},{6,22},{7,71},{8,24},{9,... | collective-permute-start | bytes 1572872 | tf_op jit(solution)/shard_map/ppermute | solution.py:324
  19.3 5.0 %collective-permute-done.8.b1 = bf16[2,2,32,2048]{3,2,1,0:T(8,128)(2,1)S(1)} collective-permute-done((bf16[2,2,32,2048]{3,2,1,0:T(8,128)(2,1)S(1)}, bf16[2,2,32,2048]{3,2,1,0:T(8,128)(2,1)S(1)}, u32[]{:S(2)}, u32[]{:S(2)}) %collective-permute-start.8) | collective-permute-done | bytes 524320 | tf_op jit(solution)/shard_map/ppermute | solution.py:324
  24.3 1.8 %collective-permute-start.9 = (bf16[2,2,32,2048]{3,2,1,0:T(8,128)(2,1)S(1)}, bf16[2,2,32,2048]{3,2,1,0:T(8,128)(2,1)S(1)}, u32[]{:S(2)}, u32[]{:S(2)}) collective-permute-start(bf16[2,2,32,2048]{3,2,1,0:T(8,128)(2,1)S(1)} %collective-permute-done.8.b1), channel_id=1, source_target_pairs={{0,48},{1,193},{2,50},{3,195},{4,52},{5,197},{6,54},{7,199},{8,56}... | collective-permute-start | bytes 1572872 | tf_op jit(solution)/shard_map/ppermute | solution.py:324
  26.6 3.7 %shard_map.68 = (f32[257,32,128]{2,1,0:T(8,128)S(1)}, bf16[2,128,128,128]{3,2,1,0:T(8,128)(2,1)S(1)}) custom-call(s32[2,256]{1,0:T(2,128)S(1)} %pad_add_fusion.lists, bf16[2,2,32,2048]{3,2,1,0:T(8,128)(2,1)S(1)} %pad_maximum_fusion.a0, bf16[2,2,32,2048]{3,2,1,0:T(8,128)(2,1)S(1)} %pad_maximum_fusion.1.b0, ...), custom_call_target="tpu_custom_call" | custom-call | flops 134217728 | bytes 12582912 | tf_op jit(solution)/shard_map/pallas_call | solution.py:117
  30.4 1.4 %collective-permute-done.12.b3 = bf16[2,2,32,2048]{3,2,1,0:T(8,128)(2,1)S(1)} collective-permute-done((bf16[2,2,32,2048]{3,2,1,0:T(8,128)(2,1)S(1)}, bf16[2,2,32,2048]{3,2,1,0:T(8,128)(2,1)S(1)}, u32[]{:S(2)}, u32[]{:S(2)}) %collective-permute-start.12) | collective-permute-done | bytes 524320 | tf_op jit(solution)/shard_map/ppermute | solution.py:324
  31.8 2.1 %shard_map.69.share = f32[257,32,128]{2,1,0:T(8,128)S(1)} custom-call(s32[2,256]{1,0:T(2,128)S(1)} %pad_add_fusion.lists, bf16[2,2,32,2048]{3,2,1,0:T(8,128)(2,1)S(1)} %collective-permute-done.11.a1, bf16[2,2,32,2048]{3,2,1,0:T(8,128)(2,1)S(1)} %collective-permute-done.12.b3, bf16[2,128,128,128]{3,2,1,0:T(8,128)(2,1)S(1)} %get-tuple-element.32.blocks, ...), custom_call_target="tpu_custom_call" | custom-call | flops 67108864 | bytes 12582912 | tf_op jit(solution)/shard_map/pallas_call | solution.py:117
  33.9 1.6 %collective-permute-done.9.b2 = bf16[2,2,32,2048]{3,2,1,0:T(8,128)(2,1)S(1)} collective-permute-done((bf16[2,2,32,2048]{3,2,1,0:T(8,128)(2,1)S(1)}, bf16[2,2,32,2048]{3,2,1,0:T(8,128)(2,1)S(1)}, u32[]{:S(2)}, u32[]{:S(2)}) %collective-permute-start.9) | collective-permute-done | bytes 524320 | tf_op jit(solution)/shard_map/ppermute | solution.py:324
  35.5 1.9 %collective-permute-done.5.a2 = bf16[2,2,32,2048]{3,2,1,0:T(8,128)(2,1)S(1)} collective-permute-done((bf16[2,2,32,2048]{3,2,1,0:T(8,128)(2,1)S(1)}, bf16[2,2,32,2048]{3,2,1,0:T(8,128)(2,1)S(1)}, u32[]{:S(2)}, u32[]{:S(2)}) %collective-permute-start.5) | collective-permute-done | bytes 524320 | tf_op jit(solution)/shard_map/ppermute | solution.py:324
  37.4 2.6 %shard_map.70 = (f32[257,32,128]{2,1,0:T(8,128)S(1)}, s16[17,32,128]{2,1,0:T(8,128)(2,1)S(1)}, s16[17,32,128]{2,1,0:T(8,128)(2,1)S(1)}, f32[32,32,128]{2,1,0:T(8,128)S(1)}) custom-call(s32[2,256]{1,0:T(2,128)S(1)} %pad_add_fusion.lists, bf16[2,2,32,2048]{3,2,1,0:T(8,128)(2,1)S(1)} %collective-permute-done.5.a2, ...), custom_call_target="tpu_custom_call" | custom-call | flops 67108864 | bytes 12582912 | tf_op jit(solution)/shard_map/pallas_call | solution.py:117
  40.0 5.2 %collective-permute-start.17 = (s16[17,32,128]{2,1,0:T(8,128)(2,1)S(1)}, s16[17,32,128]{2,1,0:T(8,128)(2,1)S(1)}, u32[]{:S(2)}, u32[]{:S(2)}) collective-permute-start(s16[17,32,128]{2,1,0:T(8,128)(2,1)S(1)} %get-tuple-element.37), channel_id=1, source_target_pairs={{0,14},{1,15},{2,0},{3,1},{4,2},{5,3},{6,4},{7,5},{8,6},{9,7},{10,... | collective-permute-start | bytes 417800 | tf_op jit(solution)/shard_map/ppermute | solution.py:324
  45.2 3.5 %collective-permute-done.17.refs_2_ = s16[17,32,128]{2,1,0:T(8,128)(2,1)S(1)} collective-permute-done((s16[17,32,128]{2,1,0:T(8,128)(2,1)S(1)}, s16[17,32,128]{2,1,0:T(8,128)(2,1)S(1)}, u32[]{:S(2)}, u32[]{:S(2)}) %collective-permute-start.17) | collective-permute-done | bytes 139296 | tf_op jit(solution)/shard_map/ppermute | solution.py:324
  49.4 3.8 %collective-permute-start.18 = (s16[33,32,128]{2,1,0:T(8,128)(2,1)S(1)}, s16[33,32,128]{2,1,0:T(8,128)(2,1)S(1)}, u32[]{:S(2)}, u32[]{:S(2)}) collective-permute-start(s16[33,32,128]{2,1,0:T(8,128)(2,1)S(1)} %shard_map.74), channel_id=1, source_target_pairs={{0,14},{1,15},{2,0},{3,1},{4,2},{5,3},{6,4},{7,5},{8,6},{9,7},{10,... | collective-permute-start | bytes 811016 | tf_op jit(solution)/shard_map/ppermute | solution.py:324
  54.0 4.8 %collective-permute-done.18.refs_2_ = s16[33,32,128]{2,1,0:T(8,128)(2,1)S(1)} collective-permute-done((s16[33,32,128]{2,1,0:T(8,128)(2,1)S(1)}, s16[33,32,128]{2,1,0:T(8,128)(2,1)S(1)}, u32[]{:S(2)}, u32[]{:S(2)}) %collective-permute-start.18) | collective-permute-done | bytes 270368 | tf_op jit(solution)/shard_map/ppermute | solution.py:324
  59.5 3.8 %collective-permute-start.19 = (s16[33,32,128]{2,1,0:T(8,128)(2,1)S(1)}, s16[33,32,128]{2,1,0:T(8,128)(2,1)S(1)}, u32[]{:S(2)}, u32[]{:S(2)}) collective-permute-start(s16[33,32,128]{2,1,0:T(8,128)(2,1)S(1)} %shard_map.75), channel_id=1, source_target_pairs={{0,14},{1,15},{2,0},{3,1},{4,2},{5,3},{6,4},{7,5},{8,6},{9,7},{10,... | collective-permute-start | bytes 811016 | tf_op jit(solution)/shard_map/ppermute | solution.py:324
  64.0 3.9 %collective-permute-done.19.refs_2_ = s16[33,32,128]{2,1,0:T(8,128)(2,1)S(1)} collective-permute-done((s16[33,32,128]{2,1,0:T(8,128)(2,1)S(1)}, s16[33,32,128]{2,1,0:T(8,128)(2,1)S(1)}, u32[]{:S(2)}, u32[]{:S(2)}) %collective-permute-start.19) | collective-permute-done | bytes 270368 | tf_op jit(solution)/shard_map/ppermute | solution.py:324
  68.6 3.8 %collective-permute-start.20 = (s16[33,32,128]{2,1,0:T(8,128)(2,1)S(1)}, s16[33,32,128]{2,1,0:T(8,128)(2,1)S(1)}, u32[]{:S(2)}, u32[]{:S(2)}) collective-permute-start(s16[33,32,128]{2,1,0:T(8,128)(2,1)S(1)} %shard_map.76), channel_id=1, source_target_pairs={{0,14},{1,15},{2,0},{3,1},{4,2},{5,3},{6,4},{7,5},{8,6},{9,7},{10,... | collective-permute-start | bytes 811016 | tf_op jit(solution)/shard_map/ppermute | solution.py:324
  73.3 3.1 %collective-permute-done.20.left = s16[33,32,128]{2,1,0:T(8,128)(2,1)S(1)} collective-permute-done((s16[33,32,128]{2,1,0:T(8,128)(2,1)S(1)}, s16[33,32,128]{2,1,0:T(8,128)(2,1)S(1)}, u32[]{:S(2)}, u32[]{:S(2)}) %collective-permute-start.20) | collective-permute-done | bytes 270368 | tf_op jit(solution)/shard_map/ppermute | solution.py:324
  76.3 4.5 %collective-permute-done.16.right = s16[33,32,128]{2,1,0:T(8,128)(2,1)S(1)} collective-permute-done((s16[33,32,128]{2,1,0:T(8,128)(2,1)S(1)}, s16[33,32,128]{2,1,0:T(8,128)(2,1)S(1)}, u32[]{:S(2)}, u32[]{:S(2)}) %collective-permute-start.16) | collective-permute-done | bytes 270368 | tf_op jit(solution)/shard_map/ppermute | solution.py:324
  80.8 1.5 %collective-permute-done.22.their_right = s16[33,32,128]{2,1,0:T(8,128)(2,1)S(1)} collective-permute-done((s16[33,32,128]{2,1,0:T(8,128)(2,1)S(1)}, s16[33,32,128]{2,1,0:T(8,128)(2,1)S(1)}, u32[]{:S(2)}, u32[]{:S(2)}) %collective-permute-start.22) | collective-permute-done | bytes 270368 | tf_op jit(solution)/shard_map/ppermute | solution.py:324
  82.4 1.1 shard_map.77
  83.5 12.0 %all_to_all.10 = f32[8,32,128]{2,1,0:T(8,128)S(1)} all-to-all(f32[8,32,128]{2,1,0:T(8,128)S(1)} %broadcast_in_dim.88), channel_id=1, replica_groups={{0,2,4,6,8,10,12,14},{1,3,5,7,9,11,13,15},{16,18,20,22,24,26,28,30},{17..., dimensions={0} | all-to-all | bytes 262144 | tf_op jit(solution)/shard_map/all_to_all | solution.py:407
  95.6 15.6 %all_to_all.11.grams = f32[16,32,128]{2,1,0:T(8,128)S(1)} all-to-all(f32[16,32,128]{2,1,0:T(8,128)S(1)} %broadcast_in_dim.89), channel_id=1, replica_groups={{0,16,32,48,64,80,96,112,128,144,160,176,192,208,224,240},{1,17,33,49,6..., dimensions={0} | all-to-all | bytes 524288 | tf_op jit(solution)/shard_map/all_to_all | solution.py:407
  111.1 3.1 %shard_map.78 = (f32[64,2048]{1,0:T(8,128)}, f32[64,64]{1,0:T(8,128)}) custom-call(f32[16,32,128]{2,1,0:T(8,128)S(1)} %all_to_all.11.grams, f32[16,64,128]{2,1,0:T(8,128)S(1)} %get-tuple-element.39.mine), custom_call_target="tpu_custom_call" | custom-call | tf_op jit(solution)/shard_map/pallas_call | solution.py:267
  (55 shorter events, 7.4 us)
Async XLA Ops:
  0.6 1.9 %collective-permute-start = (bf16[64,2048]{1,0:T(8,128)(2,1)}, bf16[64,2048]{1,0:T(8,128)(2,1)S(1)}, u32[]{:S(2)}, u32[]{:S(2)}) collective-permute-start(bf16[64,2048]{1,0:T(8,128)(2,1)} %param.5), channel_id=1, source_target_pairs={{0,1},{1,0},{2,3},{3,2},{4,5},{5,4},{6,7},{7,6},{8,9},{9,8},{10,11... | collective-permute-start | bytes 786440 | tf_op jit(solution)/shard_map/ppermute | solution.py:324
  1.4 25.3 %copy-start = (bf16[128,128,128]{2,1,0:T(8,128)(2,1)S(1)}, bf16[128,128,128]{2,1,0:T(8,128)(2,1)}, u32[]{:S(2)}) copy-start(bf16[128,128,128]{2,1,0:T(8,128)(2,1)} %own_values) | copy-start | bytes 12582916
  2.5 24.1 %collective-permute-start.10 = (bf16[128,128,128]{2,1,0:T(8,128)(2,1)}, bf16[128,128,128]{2,1,0:T(8,128)(2,1)S(1)}, u32[]{:S(2)}, u32[]{:S(2)}) collective-permute-start(bf16[128,128,128]{2,1,0:T(8,128)(2,1)} %own_values), channel_id=1, source_target_pairs={{0,1},{1,0},{2,3},{3,2},{4,5},{5,4},{6,7},{7,6},{8,9},{9,8},{10,11... | collective-permute-start | bytes 12582920 | tf_op jit(solution)/shard_map/ppermute | solution.py:324
  3.2 11.8 %collective-permute-start.1 = (bf16[2,32,2048]{2,1,0:T(8,128)(2,1)S(1)}, bf16[2,32,2048]{2,1,0:T(8,128)(2,1)S(1)}, u32[]{:S(2)}, u32[]{:S(2)}) collective-permute-start(bf16[2,32,2048]{2,1,0:T(8,128)(2,1)S(1)} %pad_maximum_fusion.2), channel_id=1, source_target_pairs={{0,64},{1,17},{2,66},{3,19},{4,68},{5,21},{6,70},{7,23},{8,72},{9,... | collective-permute-start | bytes 786440 | tf_op jit(solution)/shard_map/ppermute | solution.py:324
  4.8 10.2 %collective-permute-start.2 = (bf16[2,32,2048]{2,1,0:T(8,128)(2,1)S(1)}, bf16[2,32,2048]{2,1,0:T(8,128)(2,1)S(1)}, u32[]{:S(2)}, u32[]{:S(2)}) collective-permute-start(bf16[2,32,2048]{2,1,0:T(8,128)(2,1)S(1)} %pad_maximum_fusion.2), channel_id=1, source_target_pairs={{0,192},{1,49},{2,194},{3,51},{4,196},{5,53},{6,198},{7,55},{8,200... | collective-permute-start | bytes 786440 | tf_op jit(solution)/shard_map/ppermute | solution.py:324
  6.5 6.7 %collective-permute-start.6 = (bf16[32,2048]{1,0:T(8,128)(2,1)S(1)}, bf16[32,2048]{1,0:T(8,128)(2,1)S(1)}, u32[]{:S(2)}, u32[]{:S(2)}) collective-permute-start(bf16[32,2048]{1,0:T(8,128)(2,1)S(1)} %get-tuple-element.48), channel_id=1, source_target_pairs={{0,128},{1,33},{2,130},{3,35},{4,132},{5,37},{6,134},{7,39},{8,136... | collective-permute-start | bytes 393224 | tf_op jit(solution)/shard_map/ppermute | solution.py:324
  8.4 6.5 %collective-permute-start.7 = (bf16[32,2048]{1,0:T(8,128)(2,1)S(1)}, bf16[32,2048]{1,0:T(8,128)(2,1)S(1)}, u32[]{:S(2)}, u32[]{:S(2)}) collective-permute-start(bf16[32,2048]{1,0:T(8,128)(2,1)S(1)} %get-tuple-element.49), channel_id=1, source_target_pairs={{0,128},{1,33},{2,130},{3,35},{4,132},{5,37},{6,134},{7,39},{8,136... | collective-permute-start | bytes 393224 | tf_op jit(solution)/shard_map/ppermute | solution.py:324
  13.2 1.7 %collective-permute-start.3 = (s32[1,256]{1,0:T(1,128)S(1)}, s32[1,256]{1,0:T(1,128)S(1)}, u32[]{:S(2)}, u32[]{:S(2)}) collective-permute-start(s32[1,256]{1,0:T(1,128)S(1)} %bitcast.40), channel_id=1, source_target_pairs={{0,1},{1,0},{2,3},{3,2},{4,5},{5,4},{6,7},{7,6},{8,9},{9,8},{10,11... | collective-permute-start | bytes 3080 | tf_op jit(solution)/shard_map/ppermute | solution.py:324
  15.0 9.3 %collective-permute-start.8 = (bf16[2,2,32,2048]{3,2,1,0:T(8,128)(2,1)S(1)}, bf16[2,2,32,2048]{3,2,1,0:T(8,128)(2,1)S(1)}, u32[]{:S(2)}, u32[]{:S(2)}) collective-permute-start(bf16[2,2,32,2048]{3,2,1,0:T(8,128)(2,1)S(1)} %pad_maximum_fusion.1.b0), channel_id=1, source_target_pairs={{0,48},{1,193},{2,50},{3,195},{4,52},{5,197},{6,54},{7,199},{8,56}... | collective-permute-start | bytes 1572872 | tf_op jit(solution)/shard_map/ppermute | solution.py:324
  16.9 9.3 %collective-permute-start.4 = (bf16[2,2,32,2048]{3,2,1,0:T(8,128)(2,1)S(1)}, bf16[2,2,32,2048]{3,2,1,0:T(8,128)(2,1)S(1)}, u32[]{:S(2)}, u32[]{:S(2)}) collective-permute-start(bf16[2,2,32,2048]{3,2,1,0:T(8,128)(2,1)S(1)} %pad_maximum_fusion.a0), channel_id=1, source_target_pairs={{0,16},{1,65},{2,18},{3,67},{4,20},{5,69},{6,22},{7,71},{8,24},{9,... | collective-permute-start | bytes 1572872 | tf_op jit(solution)/shard_map/ppermute | solution.py:324
  17.2 14.5 %collective-permute-start.12 = (bf16[2,2,32,2048]{3,2,1,0:T(8,128)(2,1)S(1)}, bf16[2,2,32,2048]{3,2,1,0:T(8,128)(2,1)S(1)}, u32[]{:S(2)}, u32[]{:S(2)}) collective-permute-start(bf16[2,2,32,2048]{3,2,1,0:T(8,128)(2,1)S(1)} %pad_maximum_fusion.1.b0), channel_id=1, source_target_pairs={{0,16},{1,65},{2,18},{3,67},{4,20},{5,69},{6,22},{7,71},{8,24},{9,... | collective-permute-start | bytes 1572872 | tf_op jit(solution)/shard_map/ppermute | solution.py:324
  18.8 13.0 %collective-permute-start.11 = (bf16[2,2,32,2048]{3,2,1,0:T(8,128)(2,1)S(1)}, bf16[2,2,32,2048]{3,2,1,0:T(8,128)(2,1)S(1)}, u32[]{:S(2)}, u32[]{:S(2)}) collective-permute-start(bf16[2,2,32,2048]{3,2,1,0:T(8,128)(2,1)S(1)} %pad_maximum_fusion.a0), channel_id=1, source_target_pairs={{0,48},{1,193},{2,50},{3,195},{4,52},{5,197},{6,54},{7,199},{8,56}... | collective-permute-start | bytes 1572872 | tf_op jit(solution)/shard_map/ppermute | solution.py:324
  24.3 11.2 %collective-permute-start.9 = (bf16[2,2,32,2048]{3,2,1,0:T(8,128)(2,1)S(1)}, bf16[2,2,32,2048]{3,2,1,0:T(8,128)(2,1)S(1)}, u32[]{:S(2)}, u32[]{:S(2)}) collective-permute-start(bf16[2,2,32,2048]{3,2,1,0:T(8,128)(2,1)S(1)} %collective-permute-done.8.b1), channel_id=1, source_target_pairs={{0,48},{1,193},{2,50},{3,195},{4,52},{5,197},{6,54},{7,199},{8,56}... | collective-permute-start | bytes 1572872 | tf_op jit(solution)/shard_map/ppermute | solution.py:324
  26.2 11.2 %collective-permute-start.5 = (bf16[2,2,32,2048]{3,2,1,0:T(8,128)(2,1)S(1)}, bf16[2,2,32,2048]{3,2,1,0:T(8,128)(2,1)S(1)}, u32[]{:S(2)}, u32[]{:S(2)}) collective-permute-start(bf16[2,2,32,2048]{3,2,1,0:T(8,128)(2,1)S(1)} %collective-permute-done.4.a3), channel_id=1, source_target_pairs={{0,16},{1,65},{2,18},{3,67},{4,20},{5,69},{6,22},{7,71},{8,24},{9,... | collective-permute-start | bytes 1572872 | tf_op jit(solution)/shard_map/ppermute | solution.py:324
  40.0 8.7 %collective-permute-start.17 = (s16[17,32,128]{2,1,0:T(8,128)(2,1)S(1)}, s16[17,32,128]{2,1,0:T(8,128)(2,1)S(1)}, u32[]{:S(2)}, u32[]{:S(2)}) collective-permute-start(s16[17,32,128]{2,1,0:T(8,128)(2,1)S(1)} %get-tuple-element.37), channel_id=1, source_target_pairs={{0,14},{1,15},{2,0},{3,1},{4,2},{5,3},{6,4},{7,5},{8,6},{9,7},{10,... | collective-permute-start | bytes 417800 | tf_op jit(solution)/shard_map/ppermute | solution.py:324
  45.2 8.0 %collective-permute-start.13 = (s16[17,32,128]{2,1,0:T(8,128)(2,1)S(1)}, s16[17,32,128]{2,1,0:T(8,128)(2,1)S(1)}, u32[]{:S(2)}, u32[]{:S(2)}) collective-permute-start(s16[17,32,128]{2,1,0:T(8,128)(2,1)S(1)} %get-tuple-element.36), channel_id=1, source_target_pairs={{0,2},{1,3},{2,4},{3,5},{4,6},{5,7},{6,8},{7,9},{8,10},{9,11},{10,... | collective-permute-start | bytes 417800 | tf_op jit(solution)/shard_map/ppermute | solution.py:324
  49.4 9.3 %collective-permute-start.18 = (s16[33,32,128]{2,1,0:T(8,128)(2,1)S(1)}, s16[33,32,128]{2,1,0:T(8,128)(2,1)S(1)}, u32[]{:S(2)}, u32[]{:S(2)}) collective-permute-start(s16[33,32,128]{2,1,0:T(8,128)(2,1)S(1)} %shard_map.74), channel_id=1, source_target_pairs={{0,14},{1,15},{2,0},{3,1},{4,2},{5,3},{6,4},{7,5},{8,6},{9,7},{10,... | collective-permute-start | bytes 811016 | tf_op jit(solution)/shard_map/ppermute | solution.py:324
  53.9 9.4 %collective-permute-start.14 = (s16[33,32,128]{2,1,0:T(8,128)(2,1)S(1)}, s16[33,32,128]{2,1,0:T(8,128)(2,1)S(1)}, u32[]{:S(2)}, u32[]{:S(2)}) collective-permute-start(s16[33,32,128]{2,1,0:T(8,128)(2,1)S(1)} %shard_map.71), channel_id=1, source_target_pairs={{0,2},{1,3},{2,4},{3,5},{4,6},{5,7},{6,8},{7,9},{8,10},{9,11},{10,... | collective-permute-start | bytes 811016 | tf_op jit(solution)/shard_map/ppermute | solution.py:324
  59.5 8.4 %collective-permute-start.19 = (s16[33,32,128]{2,1,0:T(8,128)(2,1)S(1)}, s16[33,32,128]{2,1,0:T(8,128)(2,1)S(1)}, u32[]{:S(2)}, u32[]{:S(2)}) collective-permute-start(s16[33,32,128]{2,1,0:T(8,128)(2,1)S(1)} %shard_map.75), channel_id=1, source_target_pairs={{0,14},{1,15},{2,0},{3,1},{4,2},{5,3},{6,4},{7,5},{8,6},{9,7},{10,... | collective-permute-start | bytes 811016 | tf_op jit(solution)/shard_map/ppermute | solution.py:324
  63.9 8.4 %collective-permute-start.15 = (s16[33,32,128]{2,1,0:T(8,128)(2,1)S(1)}, s16[33,32,128]{2,1,0:T(8,128)(2,1)S(1)}, u32[]{:S(2)}, u32[]{:S(2)}) collective-permute-start(s16[33,32,128]{2,1,0:T(8,128)(2,1)S(1)} %shard_map.72), channel_id=1, source_target_pairs={{0,2},{1,3},{2,4},{3,5},{4,6},{5,7},{6,8},{7,9},{8,10},{9,11},{10,... | collective-permute-start | bytes 811016 | tf_op jit(solution)/shard_map/ppermute | solution.py:324
  68.6 7.7 %collective-permute-start.20 = (s16[33,32,128]{2,1,0:T(8,128)(2,1)S(1)}, s16[33,32,128]{2,1,0:T(8,128)(2,1)S(1)}, u32[]{:S(2)}, u32[]{:S(2)}) collective-permute-start(s16[33,32,128]{2,1,0:T(8,128)(2,1)S(1)} %shard_map.76), channel_id=1, source_target_pairs={{0,14},{1,15},{2,0},{3,1},{4,2},{5,3},{6,4},{7,5},{8,6},{9,7},{10,... | collective-permute-start | bytes 811016 | tf_op jit(solution)/shard_map/ppermute | solution.py:324
  73.1 7.7 %collective-permute-start.16 = (s16[33,32,128]{2,1,0:T(8,128)(2,1)S(1)}, s16[33,32,128]{2,1,0:T(8,128)(2,1)S(1)}, u32[]{:S(2)}, u32[]{:S(2)}) collective-permute-start(s16[33,32,128]{2,1,0:T(8,128)(2,1)S(1)} %shard_map.73), channel_id=1, source_target_pairs={{0,2},{1,3},{2,4},{3,5},{4,6},{5,7},{6,8},{7,9},{8,10},{9,11},{10,... | collective-permute-start | bytes 811016 | tf_op jit(solution)/shard_map/ppermute | solution.py:324
  73.2 7.7 %collective-permute-start.21 = (f32[32,32,128]{2,1,0:T(8,128)S(1)}, f32[32,32,128]{2,1,0:T(8,128)S(1)}, u32[]{:S(2)}, u32[]{:S(2)}) collective-permute-start(f32[32,32,128]{2,1,0:T(8,128)S(1)} %get-tuple-element.34.ours), channel_id=1, source_target_pairs={{0,1},{1,0},{2,3},{3,2},{4,5},{5,4},{6,7},{7,6},{8,9},{9,8},{10,11... | collective-permute-start | bytes 1572872 | tf_op jit(solution)/shard_map/ppermute | solution.py:324
  76.3 4.5 %collective-permute-start.23 = (s16[33,32,128]{2,1,0:T(8,128)(2,1)S(1)}, s16[33,32,128]{2,1,0:T(8,128)(2,1)S(1)}, u32[]{:S(2)}, u32[]{:S(2)}) collective-permute-start(s16[33,32,128]{2,1,0:T(8,128)(2,1)S(1)} %collective-permute-done.20.left), channel_id=1, source_target_pairs={{0,1},{1,0},{2,3},{3,2},{4,5},{5,4},{6,7},{7,6},{8,9},{9,8},{10,11... | collective-permute-start | bytes 811016 | tf_op jit(solution)/shard_map/ppermute | solution.py:324
  80.8 1.5 %collective-permute-start.22 = (s16[33,32,128]{2,1,0:T(8,128)(2,1)S(1)}, s16[33,32,128]{2,1,0:T(8,128)(2,1)S(1)}, u32[]{:S(2)}, u32[]{:S(2)}) collective-permute-start(s16[33,32,128]{2,1,0:T(8,128)(2,1)S(1)} %collective-permute-done.16.right), channel_id=1, source_target_pairs={{0,1},{1,0},{2,3},{3,2},{4,5},{5,4},{6,7},{7,6},{8,9},{9,8},{10,11... | collective-permute-start | bytes 811016 | tf_op jit(solution)/shard_map/ppermute | solution.py:324

commit v5 on v4

--- a/solution.py
+++ b/solution.py
@@ -26,7 +26,7 @@
 
     def flush(step, made):
         for i in range(group):
-            row = (entry(step * group + i) >> 10) & 511
+            row = (entry(step * group + i) >> 11) & 511
             out[row] = out[row] + made[i]
 
     def loop(step, made):
@@ -42,8 +42,8 @@
     size = values[0].shape[0]
     left = []
     for entry in entries:
-        offset = pl.multiple_of(((entry >> 2) & 15) * size, size)
-        left.append(slab[(entry >> 6) & 15, side, :, pl.ds(offset, size)])
+        offset = pl.multiple_of(((entry >> 3) & 15) * size, size)
+        left.append(slab[(entry >> 7) & 15, side, :, pl.ds(offset, size)])
     both = lax.dot_general(
         jnp.concatenate(left, axis=0),
         jnp.concatenate(values, axis=0),
@@ -69,9 +69,9 @@
     for side in range(2):
 
         def block(*entries, side=side):
-            return products(slab, side, entries, [blocks[side, entry >> 19] for entry in entries])
-
-        begin, count = lists[side, slots + stage], lists[side, slots + 4 + stage]
+            return products(slab, side, entries, [blocks[side, entry >> 20] for entry in entries])
+
+        begin, count = lists[side, slots + stage], lists[side, slots + 8 + stage]
         add_products(group, lists, side, begin, count, filler, block, out)
 
 
@@ -96,16 +96,24 @@
     add_stage(1, 16, filler, lists, slab, blocks, out)
 
 
-def late_kernel(filler, lists, a2, b2, index, blocks, share, out, out_right, out_left, home, slab, sems):
+def late_kernel(filler, lists, a2, b2, index, blocks, share, out, out_right, out_left, slab, sems):
     copies = load((a2, b2), slab, sems)
     out[...] = share[...]
     for copy in copies:
         copy.wait()
-    add_stage(2, 16, filler, lists, slab, blocks, out)
+    add_stage(2, 4, filler, lists, slab, blocks, out)
     half = out_right.shape[0] - 1
     far = index[4]
     code_into(out.at[pl.ds(far, half)], out_right)
     code_into(out.at[pl.ds(far + half, half)], out_left)
+
+
+def last_kernel(filler, lists, a2, b2, index, blocks, share, out, home, slab, sems):
+    copies = load((a2, b2), slab, sems)
+    out[...] = share[...]
+    for copy in copies:
+        copy.wait()
+    add_stage(3, 16, filler, lists, slab, blocks, out)
     home[...] = out[pl.ds(index[0], home.shape[0])]
 
 
@@ -115,7 +123,7 @@
     there = sum(piece.shape[0] for piece in pieces)
     pieces = tuple(pieces) + tuple(values)
     return pl.pallas_call(
-        functools.partial(kernel, row_blocks << 10),
+        functools.partial(kernel, row_blocks << 11),
         out_shape=out_shape,
         in_specs=[smem]
         + [pl.BlockSpec(memory_space=pl.ANY)] * len(pieces)
@@ -331,6 +339,7 @@
     values, other_basis = lax.optimization_barrier((values, other_basis))
     other_values = move(values, swap)
 
+    depth = cols // 2
     low, high = slice(0, half), slice(half, None)
     chunk = jnp.stack([jnp.where(core == 0, array[low], array[high]) for array in (basis, other_basis)])
     chunk, block_row, block_col, block_count = lax.optimization_barrier((chunk, block_row, block_col, block_count))
@@ -341,25 +350,25 @@
         dx, dy = ((source >> 2) - x) & 3, (source - y) & 3
         near, far = jnp.where(which == 0, dx, dy), jnp.where(which == 0, dy, dx)
         middle = ((far == 1) & (near < 2)) | ((far == 3) & (near >= 2))
-        stage = jnp.where(far == 2, 2, jnp.where(middle, 1, 0))
+        farthest = (lax.div(block_row, 2 * per_device) - z) & (depth - 1)
+        stage = jnp.where(far == 2, jnp.where(farthest == depth // 2, 2, 3), jnp.where(middle, 1, 0))
         place = near + jnp.where(stage > 0, 0, jnp.where(far == 0, 0, jnp.where(far == 1, 2, 6)))
-        stage = jnp.where(slot < block_count, stage, 3)
-        return stage | (offset << 2) | (place << 6) | (block_row << 10) | (slot << 19)
+        stage = jnp.where(slot < block_count, stage, 4)
+        return stage | (offset << 3) | (place << 7) | (block_row << 11) | (slot << 20)
 
     def listed(packed):
-        key = packed[0] & 3
+        key = packed[0] & 7
         place = jnp.arange(slots, dtype=jnp.int32)
         order = key * slots + place
         rank = jnp.sum((order[:, None] < order[None, :]).astype(jnp.int32), axis=0)
         entries = jnp.sum(jnp.where(rank[None, :] == place[:, None], packed, 0), axis=1)
-        begins = jnp.sum((key[None, :] < place[:4, None]).astype(jnp.int32), axis=1)
-        counts = jnp.sum((key[None, :] == place[: slots - 4, None]).astype(jnp.int32), axis=1)
+        begins = jnp.sum((key[None, :] < place[:8, None]).astype(jnp.int32), axis=1)
+        counts = jnp.sum((key[None, :] == place[: slots - 8, None]).astype(jnp.int32), axis=1)
         return jnp.concatenate([entries, begins, counts])[None]
 
     other_lists = move(listed(packed_for(1 - core)), swap)
     from_low, from_high = move(chunk, first(1)), move(chunk, first(-1))
     far_own, far_other = move(chunk[0], first(2)), move(chunk[1], first(-2))
-    depth = cols // 2
     index = ((z + jnp.arange(depth, dtype=jnp.int32)) & (depth - 1)) * (2 * per_device)
     which = core[None].astype(jnp.int32)
     from_low, from_high, other_lists, index, which = lax.optimization_barrier(
@@ -385,8 +394,11 @@
     )
     (share,) = add_blocks(middle_kernel, work // 4, lists, (a1, b3), (), (blocks, share), (total,), row_blocks)
     whole = jax.ShapeDtypeStruct((2 * per_device, half, size), jnp.float32)
-    share, right, left, home = add_blocks(
-        late_kernel, work // 4, lists, (a2, b2), (), (index, blocks, share), (total, part, part, whole), row_blocks
+    share, right, left = add_blocks(
+        late_kernel, work // 16, lists, (a2, b2), (), (index, blocks, share), (total, part, part), row_blocks
+    )
+    share, home = add_blocks(
+        last_kernel, work // 4, lists, (a2, b2), (), (index, blocks, share), (total, whole), row_blocks
     )
     their_home = move(home, swap)
 

time: 115 us -> 113 us (0.983)
  waiting for transfers between devices: 34.7 us -> 28.4 us
  Pallas kernels: 16.8 us -> 20.6 us
    ppermute x24, waiting for transfers between devices: 34.7 us -> 28.4 us  [move(): return lax.ppermute(array, BOTH, pairs)]
    pallas_call x3 -> x4, Pallas kernels: 8.49 us -> 12.3 us  [add_blocks(): pl.pallas_call(functools.partial(kernel, row_blocks << 11), out_shape=out...]
  transfers between devices with their start and end apart: 24 -> 24, of which waited for: 13 -> 12; matrix products, arithmetic and copies ran while one was open for 3% -> 3% of each run, Pallas kernels for 9% -> 13%
where the time goes in v5:
time: 113 us
  starting transfers between devices  31.1 us (28%)
  blocking collectives  28.6 us (25%)
  waiting for transfers between devices  28.4 us (25%)
  Pallas kernels  20.6 us (18%)
  other arithmetic  2.9 us (3%)
  between operations  1.72 us (2%)
    ppermute x24, starting transfers between devices, move(): return lax.ppermute(array, BOTH, pairs)  31.1 us
    all_to_all x2, blocking collectives, spread(): return lax.all_to_all(copies, axis, 0, 0, axis_index_groups=groups)  28.6 us
    ppermute x24, waiting for transfers between devices, move(): return lax.ppermute(array, BOTH, pairs)  28.4 us
    pallas_call x4, Pallas kernels, add_blocks(): pl.pallas_call(functools.partial(kernel, row_blocks << 11), out_shape=out...  12.3 us
    pallas_call x6, Pallas kernels, on_chunk(): pl.pallas_call(kernel, out_shape=out_shape, in_specs=[pl.BlockSpec(memory...  4.06 us
    pallas_call x1, Pallas kernels, finish(): pl.pallas_call(functools.partial(finish_kernel, scale), out_shape=(jax.Sh...  3.1 us
  transfers between devices with their start and end apart: 24, of which 12 were waited for; matrix products, arithmetic and copies ran while one was open for 3% of the time, Pallas kernels for 13%

profile of v5, /device:TPU:8, one launch (start us, length us, event | category | flops | bytes accessed | tf_op | source)
XLA Modules:
  0.0 113.3 jit_solution(4691080869631333541)
XLA Ops:
  1.6 1.2 %select_bitcast_fusion.1 = bf16[1,32,2048]{2,1,0:T(8,128)(2,1)S(1)} fusion(bf16[64,2048]{1,0:T(8,128)(2,1)} %param.5, pred[]{:T(512)S(6)} %eq.92), kind=kLoop, calls=%fused_computation.7 | loop fusion | flops 65536 | bytes 393217 | tf_op jit(solution)/shard_map/stack | solution.py:344
  3.3 1.6 %collective-permute-start.1 = (bf16[2,32,2048]{2,1,0:T(8,128)(2,1)S(1)}, bf16[2,32,2048]{2,1,0:T(8,128)(2,1)S(1)}, u32[]{:S(2)}, u32[]{:S(2)}) collective-permute-start(bf16[2,32,2048]{2,1,0:T(8,128)(2,1)S(1)} %pad_maximum_fusion.2), channel_id=1, source_target_pairs={{0,64},{1,17},{2,66},{3,19},{4,68},{5,21},{6,70},{7,23},{8,72},{9,... | collective-permute-start | bytes 786440 | tf_op jit(solution)/shard_map/ppermute | solution.py:332
  4.9 1.7 %collective-permute-start.2 = (bf16[2,32,2048]{2,1,0:T(8,128)(2,1)S(1)}, bf16[2,32,2048]{2,1,0:T(8,128)(2,1)S(1)}, u32[]{:S(2)}, u32[]{:S(2)}) collective-permute-start(bf16[2,32,2048]{2,1,0:T(8,128)(2,1)S(1)} %pad_maximum_fusion.2), channel_id=1, source_target_pairs={{0,192},{1,49},{2,194},{3,51},{4,196},{5,53},{6,198},{7,55},{8,200... | collective-permute-start | bytes 786440 | tf_op jit(solution)/shard_map/ppermute | solution.py:332
  6.7 1.9 %collective-permute-start.6 = (bf16[32,2048]{1,0:T(8,128)(2,1)S(1)}, bf16[32,2048]{1,0:T(8,128)(2,1)S(1)}, u32[]{:S(2)}, u32[]{:S(2)}) collective-permute-start(bf16[32,2048]{1,0:T(8,128)(2,1)S(1)} %get-tuple-element.50), channel_id=1, source_target_pairs={{0,128},{1,33},{2,130},{3,35},{4,132},{5,37},{6,134},{7,39},{8,136... | collective-permute-start | bytes 393224 | tf_op jit(solution)/shard_map/ppermute | solution.py:332
  8.6 1.7 %collective-permute-start.7 = (bf16[32,2048]{1,0:T(8,128)(2,1)S(1)}, bf16[32,2048]{1,0:T(8,128)(2,1)S(1)}, u32[]{:S(2)}, u32[]{:S(2)}) collective-permute-start(bf16[32,2048]{1,0:T(8,128)(2,1)S(1)} %get-tuple-element.51), channel_id=1, source_target_pairs={{0,128},{1,33},{2,130},{3,35},{4,132},{5,37},{6,134},{7,39},{8,136... | collective-permute-start | bytes 393224 | tf_op jit(solution)/shard_map/ppermute | solution.py:332
  10.3 0.7 iota_add_fusion.1
  11.7 1.7 %collective-permute-done.6 = bf16[32,2048]{1,0:T(8,128)(2,1)S(1)} collective-permute-done((bf16[32,2048]{1,0:T(8,128)(2,1)S(1)}, bf16[32,2048]{1,0:T(8,128)(2,1)S(1)}, u32[]{:S(2)}, u32[]{:S(2)}) %collective-permute-start.6) | collective-permute-done | bytes 131104 | tf_op jit(solution)/shard_map/ppermute | solution.py:332
  13.4 1.7 %collective-permute-done.7 = bf16[32,2048]{1,0:T(8,128)(2,1)S(1)} collective-permute-done((bf16[32,2048]{1,0:T(8,128)(2,1)S(1)}, bf16[32,2048]{1,0:T(8,128)(2,1)S(1)}, u32[]{:S(2)}, u32[]{:S(2)}) %collective-permute-start.7) | collective-permute-done | bytes 131104 | tf_op jit(solution)/shard_map/ppermute | solution.py:332
  15.2 1.9 %collective-permute-start.8 = (bf16[2,2,32,2048]{3,2,1,0:T(8,128)(2,1)S(1)}, bf16[2,2,32,2048]{3,2,1,0:T(8,128)(2,1)S(1)}, u32[]{:S(2)}, u32[]{:S(2)}) collective-permute-start(bf16[2,2,32,2048]{3,2,1,0:T(8,128)(2,1)S(1)} %pad_maximum_fusion.1.b0), channel_id=1, source_target_pairs={{0,48},{1,193},{2,50},{3,195},{4,52},{5,197},{6,54},{7,199},{8,56}... | collective-permute-start | bytes 1572872 | tf_op jit(solution)/shard_map/ppermute | solution.py:332
  17.4 1.6 %collective-permute-start.12 = (bf16[2,2,32,2048]{3,2,1,0:T(8,128)(2,1)S(1)}, bf16[2,2,32,2048]{3,2,1,0:T(8,128)(2,1)S(1)}, u32[]{:S(2)}, u32[]{:S(2)}) collective-permute-start(bf16[2,2,32,2048]{3,2,1,0:T(8,128)(2,1)S(1)} %pad_maximum_fusion.1.b0), channel_id=1, source_target_pairs={{0,16},{1,65},{2,18},{3,67},{4,20},{5,69},{6,22},{7,71},{8,24},{9,... | collective-permute-start | bytes 1572872 | tf_op jit(solution)/shard_map/ppermute | solution.py:332
  19.4 5.0 %collective-permute-done.8.b1 = bf16[2,2,32,2048]{3,2,1,0:T(8,128)(2,1)S(1)} collective-permute-done((bf16[2,2,32,2048]{3,2,1,0:T(8,128)(2,1)S(1)}, bf16[2,2,32,2048]{3,2,1,0:T(8,128)(2,1)S(1)}, u32[]{:S(2)}, u32[]{:S(2)}) %collective-permute-start.8) | collective-permute-done | bytes 524320 | tf_op jit(solution)/shard_map/ppermute | solution.py:332
  24.4 1.8 %collective-permute-start.9 = (bf16[2,2,32,2048]{3,2,1,0:T(8,128)(2,1)S(1)}, bf16[2,2,32,2048]{3,2,1,0:T(8,128)(2,1)S(1)}, u32[]{:S(2)}, u32[]{:S(2)}) collective-permute-start(bf16[2,2,32,2048]{3,2,1,0:T(8,128)(2,1)S(1)} %collective-permute-done.8.b1), channel_id=1, source_target_pairs={{0,48},{1,193},{2,50},{3,195},{4,52},{5,197},{6,54},{7,199},{8,56}... | collective-permute-start | bytes 1572872 | tf_op jit(solution)/shard_map/ppermute | solution.py:332
  26.8 5.7 %shard_map.68 = (f32[257,32,128]{2,1,0:T(8,128)S(1)}, bf16[2,128,128,128]{3,2,1,0:T(8,128)(2,1)S(1)}) custom-call(s32[2,256]{1,0:T(2,128)S(1)} %pad_add_fusion.lists, bf16[2,2,32,2048]{3,2,1,0:T(8,128)(2,1)S(1)} %pad_maximum_fusion.a0, bf16[2,2,32,2048]{3,2,1,0:T(8,128)(2,1)S(1)} %pad_maximum_fusion.1.b0, ...), custom_call_target="tpu_custom_call" | custom-call | flops 134217728 | bytes 12582912 | tf_op jit(solution)/shard_map/pallas_call | solution.py:125
  32.5 2.5 %shard_map.69.share = f32[257,32,128]{2,1,0:T(8,128)S(1)} custom-call(s32[2,256]{1,0:T(2,128)S(1)} %pad_add_fusion.lists, bf16[2,2,32,2048]{3,2,1,0:T(8,128)(2,1)S(1)} %collective-permute-done.11.a1, bf16[2,2,32,2048]{3,2,1,0:T(8,128)(2,1)S(1)} %collective-permute-done.12.b3, bf16[2,128,128,128]{3,2,1,0:T(8,128)(2,1)S(1)} %get-tuple-element.33.blocks, ...), custom_call_target="tpu_custom_call" | custom-call | flops 67108864 | bytes 12582912 | tf_op jit(solution)/shard_map/pallas_call | solution.py:125
  35.7 1.9 %collective-permute-done.5.a2 = bf16[2,2,32,2048]{3,2,1,0:T(8,128)(2,1)S(1)} collective-permute-done((bf16[2,2,32,2048]{3,2,1,0:T(8,128)(2,1)S(1)}, bf16[2,2,32,2048]{3,2,1,0:T(8,128)(2,1)S(1)}, u32[]{:S(2)}, u32[]{:S(2)}) %collective-permute-start.5) | collective-permute-done | bytes 524320 | tf_op jit(solution)/shard_map/ppermute | solution.py:332
  37.6 1.6 %shard_map.70 = (f32[257,32,128]{2,1,0:T(8,128)S(1)}, s16[17,32,128]{2,1,0:T(8,128)(2,1)S(1)}, s16[17,32,128]{2,1,0:T(8,128)(2,1)S(1)}) custom-call(s32[2,256]{1,0:T(2,128)S(1)} %pad_add_fusion.lists, bf16[2,2,32,2048]{3,2,1,0:T(8,128)(2,1)S(1)} %collective-permute-done.5.a2, bf16[2,2,32,2048]{3,2,1,0:T(8,128)(2,1)S(1)} %collective-permute-done.9.b2, ...), custom_call_target="tpu_custom_call" | custom-call | flops 16777216 | bytes 12582912 | tf_op jit(solution)/shard_map/pallas_call | solution.py:125
  39.2 5.6 %collective-permute-start.17 = (s16[17,32,128]{2,1,0:T(8,128)(2,1)S(1)}, s16[17,32,128]{2,1,0:T(8,128)(2,1)S(1)}, u32[]{:S(2)}, u32[]{:S(2)}) collective-permute-start(s16[17,32,128]{2,1,0:T(8,128)(2,1)S(1)} %get-tuple-element.39), channel_id=1, source_target_pairs={{0,14},{1,15},{2,0},{3,1},{4,2},{5,3},{6,4},{7,5},{8,6},{9,7},{10,... | collective-permute-start | bytes 417800 | tf_op jit(solution)/shard_map/ppermute | solution.py:332
  44.8 2.5 %shard_map.71 = (f32[257,32,128]{2,1,0:T(8,128)S(1)}, f32[32,32,128]{2,1,0:T(8,128)S(1)}) custom-call(s32[2,256]{1,0:T(2,128)S(1)} %pad_add_fusion.lists, bf16[2,2,32,2048]{3,2,1,0:T(8,128)(2,1)S(1)} %collective-permute-done.5.a2, bf16[2,2,32,2048]{3,2,1,0:T(8,128)(2,1)S(1)} %collective-permute-done.9.b2, s32[8]{0:T(128)S(1)} %and_multiply_fusion.index.refs_0_, ...), custom_call_target="tpu_custom_call" | custom-call | flops 67108864 | bytes 12582912 | tf_op jit(solution)/shard_map/pallas_call | solution.py:125
  48.6 3.8 %collective-permute-start.18 = (s16[33,32,128]{2,1,0:T(8,128)(2,1)S(1)}, s16[33,32,128]{2,1,0:T(8,128)(2,1)S(1)}, u32[]{:S(2)}, u32[]{:S(2)}) collective-permute-start(s16[33,32,128]{2,1,0:T(8,128)(2,1)S(1)} %shard_map.75), channel_id=1, source_target_pairs={{0,14},{1,15},{2,0},{3,1},{4,2},{5,3},{6,4},{7,5},{8,6},{9,7},{10,... | collective-permute-start | bytes 811016 | tf_op jit(solution)/shard_map/ppermute | solution.py:332
  53.1 4.3 %collective-permute-done.18.refs_2_ = s16[33,32,128]{2,1,0:T(8,128)(2,1)S(1)} collective-permute-done((s16[33,32,128]{2,1,0:T(8,128)(2,1)S(1)}, s16[33,32,128]{2,1,0:T(8,128)(2,1)S(1)}, u32[]{:S(2)}, u32[]{:S(2)}) %collective-permute-start.18) | collective-permute-done | bytes 270368 | tf_op jit(solution)/shard_map/ppermute | solution.py:332
  58.1 3.8 %collective-permute-start.19 = (s16[33,32,128]{2,1,0:T(8,128)(2,1)S(1)}, s16[33,32,128]{2,1,0:T(8,128)(2,1)S(1)}, u32[]{:S(2)}, u32[]{:S(2)}) collective-permute-start(s16[33,32,128]{2,1,0:T(8,128)(2,1)S(1)} %shard_map.76), channel_id=1, source_target_pairs={{0,14},{1,15},{2,0},{3,1},{4,2},{5,3},{6,4},{7,5},{8,6},{9,7},{10,... | collective-permute-start | bytes 811016 | tf_op jit(solution)/shard_map/ppermute | solution.py:332
  61.9 0.7 shard_map.73
  62.7 3.4 %collective-permute-done.19.refs_2_ = s16[33,32,128]{2,1,0:T(8,128)(2,1)S(1)} collective-permute-done((s16[33,32,128]{2,1,0:T(8,128)(2,1)S(1)}, s16[33,32,128]{2,1,0:T(8,128)(2,1)S(1)}, u32[]{:S(2)}, u32[]{:S(2)}) %collective-permute-start.19) | collective-permute-done | bytes 270368 | tf_op jit(solution)/shard_map/ppermute | solution.py:332
  66.7 3.8 %collective-permute-start.20 = (s16[33,32,128]{2,1,0:T(8,128)(2,1)S(1)}, s16[33,32,128]{2,1,0:T(8,128)(2,1)S(1)}, u32[]{:S(2)}, u32[]{:S(2)}) collective-permute-start(s16[33,32,128]{2,1,0:T(8,128)(2,1)S(1)} %shard_map.77), channel_id=1, source_target_pairs={{0,14},{1,15},{2,0},{3,1},{4,2},{5,3},{6,4},{7,5},{8,6},{9,7},{10,... | collective-permute-start | bytes 811016 | tf_op jit(solution)/shard_map/ppermute | solution.py:332
  70.5 0.7 shard_map.74
  71.4 3.1 %collective-permute-done.20.left = s16[33,32,128]{2,1,0:T(8,128)(2,1)S(1)} collective-permute-done((s16[33,32,128]{2,1,0:T(8,128)(2,1)S(1)}, s16[33,32,128]{2,1,0:T(8,128)(2,1)S(1)}, u32[]{:S(2)}, u32[]{:S(2)}) %collective-permute-start.20) | collective-permute-done | bytes 270368 | tf_op jit(solution)/shard_map/ppermute | solution.py:332
  74.5 4.5 %collective-permute-done.16.right = s16[33,32,128]{2,1,0:T(8,128)(2,1)S(1)} collective-permute-done((s16[33,32,128]{2,1,0:T(8,128)(2,1)S(1)}, s16[33,32,128]{2,1,0:T(8,128)(2,1)S(1)}, u32[]{:S(2)}, u32[]{:S(2)}) %collective-permute-start.16) | collective-permute-done | bytes 270368 | tf_op jit(solution)/shard_map/ppermute | solution.py:332
  79.0 1.5 %collective-permute-done.22.their_right = s16[33,32,128]{2,1,0:T(8,128)(2,1)S(1)} collective-permute-done((s16[33,32,128]{2,1,0:T(8,128)(2,1)S(1)}, s16[33,32,128]{2,1,0:T(8,128)(2,1)S(1)}, u32[]{:S(2)}, u32[]{:S(2)}) %collective-permute-start.22) | collective-permute-done | bytes 270368 | tf_op jit(solution)/shard_map/ppermute | solution.py:332
  80.5 1.1 shard_map.78
  81.6 13.3 %all_to_all.10 = f32[8,32,128]{2,1,0:T(8,128)S(1)} all-to-all(f32[8,32,128]{2,1,0:T(8,128)S(1)} %broadcast_in_dim.87), channel_id=1, replica_groups={{0,2,4,6,8,10,12,14},{1,3,5,7,9,11,13,15},{16,18,20,22,24,26,28,30},{17..., dimensions={0} | all-to-all | bytes 262144 | tf_op jit(solution)/shard_map/all_to_all | solution.py:419
  95.0 15.3 %all_to_all.11.grams = f32[16,32,128]{2,1,0:T(8,128)S(1)} all-to-all(f32[16,32,128]{2,1,0:T(8,128)S(1)} %broadcast_in_dim.88), channel_id=1, replica_groups={{0,16,32,48,64,80,96,112,128,144,160,176,192,208,224,240},{1,17,33,49,6..., dimensions={0} | all-to-all | bytes 524288 | tf_op jit(solution)/shard_map/all_to_all | solution.py:419
  110.2 3.1 %shard_map.79 = (f32[64,2048]{1,0:T(8,128)}, f32[64,64]{1,0:T(8,128)}) custom-call(f32[16,32,128]{2,1,0:T(8,128)S(1)} %all_to_all.11.grams, f32[16,64,128]{2,1,0:T(8,128)S(1)} %get-tuple-element.41.mine), custom_call_target="tpu_custom_call" | custom-call | tf_op jit(solution)/shard_map/pallas_call | solution.py:275
  (56 shorter events, 7.2 us)
Async XLA Ops:
  0.6 2.1 %collective-permute-start = (bf16[64,2048]{1,0:T(8,128)(2,1)}, bf16[64,2048]{1,0:T(8,128)(2,1)S(1)}, u32[]{:S(2)}, u32[]{:S(2)}) collective-permute-start(bf16[64,2048]{1,0:T(8,128)(2,1)} %param.5), channel_id=1, source_target_pairs={{0,1},{1,0},{2,3},{3,2},{4,5},{5,4},{6,7},{7,6},{8,9},{9,8},{10,11... | collective-permute-start | bytes 786440 | tf_op jit(solution)/shard_map/ppermute | solution.py:332
  0.7 26.1 %copy-start = (bf16[128,128,128]{2,1,0:T(8,128)(2,1)S(1)}, bf16[128,128,128]{2,1,0:T(8,128)(2,1)}, u32[]{:S(2)}) copy-start(bf16[128,128,128]{2,1,0:T(8,128)(2,1)} %own_values) | copy-start | bytes 12582916
  2.7 24.1 %collective-permute-start.10 = (bf16[128,128,128]{2,1,0:T(8,128)(2,1)}, bf16[128,128,128]{2,1,0:T(8,128)(2,1)S(1)}, u32[]{:S(2)}, u32[]{:S(2)}) collective-permute-start(bf16[128,128,128]{2,1,0:T(8,128)(2,1)} %own_values), channel_id=1, source_target_pairs={{0,1},{1,0},{2,3},{3,2},{4,5},{5,4},{6,7},{7,6},{8,9},{9,8},{10,11... | collective-permute-start | bytes 12582920 | tf_op jit(solution)/shard_map/ppermute | solution.py:332
  3.3 11.8 %collective-permute-start.1 = (bf16[2,32,2048]{2,1,0:T(8,128)(2,1)S(1)}, bf16[2,32,2048]{2,1,0:T(8,128)(2,1)S(1)}, u32[]{:S(2)}, u32[]{:S(2)}) collective-permute-start(bf16[2,32,2048]{2,1,0:T(8,128)(2,1)S(1)} %pad_maximum_fusion.2), channel_id=1, source_target_pairs={{0,64},{1,17},{2,66},{3,19},{4,68},{5,21},{6,70},{7,23},{8,72},{9,... | collective-permute-start | bytes 786440 | tf_op jit(solution)/shard_map/ppermute | solution.py:332
  4.9 10.2 %collective-permute-start.2 = (bf16[2,32,2048]{2,1,0:T(8,128)(2,1)S(1)}, bf16[2,32,2048]{2,1,0:T(8,128)(2,1)S(1)}, u32[]{:S(2)}, u32[]{:S(2)}) collective-permute-start(bf16[2,32,2048]{2,1,0:T(8,128)(2,1)S(1)} %pad_maximum_fusion.2), channel_id=1, source_target_pairs={{0,192},{1,49},{2,194},{3,51},{4,196},{5,53},{6,198},{7,55},{8,200... | collective-permute-start | bytes 786440 | tf_op jit(solution)/shard_map/ppermute | solution.py:332
  6.7 6.7 %collective-permute-start.6 = (bf16[32,2048]{1,0:T(8,128)(2,1)S(1)}, bf16[32,2048]{1,0:T(8,128)(2,1)S(1)}, u32[]{:S(2)}, u32[]{:S(2)}) collective-permute-start(bf16[32,2048]{1,0:T(8,128)(2,1)S(1)} %get-tuple-element.50), channel_id=1, source_target_pairs={{0,128},{1,33},{2,130},{3,35},{4,132},{5,37},{6,134},{7,39},{8,136... | collective-permute-start | bytes 393224 | tf_op jit(solution)/shard_map/ppermute | solution.py:332
  8.6 6.5 %collective-permute-start.7 = (bf16[32,2048]{1,0:T(8,128)(2,1)S(1)}, bf16[32,2048]{1,0:T(8,128)(2,1)S(1)}, u32[]{:S(2)}, u32[]{:S(2)}) collective-permute-start(bf16[32,2048]{1,0:T(8,128)(2,1)S(1)} %get-tuple-element.51), channel_id=1, source_target_pairs={{0,128},{1,33},{2,130},{3,35},{4,132},{5,37},{6,134},{7,39},{8,136... | collective-permute-start | bytes 393224 | tf_op jit(solution)/shard_map/ppermute | solution.py:332
  13.4 1.7 %collective-permute-start.3 = (s32[1,256]{1,0:T(1,128)S(1)}, s32[1,256]{1,0:T(1,128)S(1)}, u32[]{:S(2)}, u32[]{:S(2)}) collective-permute-start(s32[1,256]{1,0:T(1,128)S(1)} %bitcast.40), channel_id=1, source_target_pairs={{0,1},{1,0},{2,3},{3,2},{4,5},{5,4},{6,7},{7,6},{8,9},{9,8},{10,11... | collective-permute-start | bytes 3080 | tf_op jit(solution)/shard_map/ppermute | solution.py:332
  15.2 9.3 %collective-permute-start.8 = (bf16[2,2,32,2048]{3,2,1,0:T(8,128)(2,1)S(1)}, bf16[2,2,32,2048]{3,2,1,0:T(8,128)(2,1)S(1)}, u32[]{:S(2)}, u32[]{:S(2)}) collective-permute-start(bf16[2,2,32,2048]{3,2,1,0:T(8,128)(2,1)S(1)} %pad_maximum_fusion.1.b0), channel_id=1, source_target_pairs={{0,48},{1,193},{2,50},{3,195},{4,52},{5,197},{6,54},{7,199},{8,56}... | collective-permute-start | bytes 1572872 | tf_op jit(solution)/shard_map/ppermute | solution.py:332
  17.1 9.3 %collective-permute-start.4 = (bf16[2,2,32,2048]{3,2,1,0:T(8,128)(2,1)S(1)}, bf16[2,2,32,2048]{3,2,1,0:T(8,128)(2,1)S(1)}, u32[]{:S(2)}, u32[]{:S(2)}) collective-permute-start(bf16[2,2,32,2048]{3,2,1,0:T(8,128)(2,1)S(1)} %pad_maximum_fusion.a0), channel_id=1, source_target_pairs={{0,16},{1,65},{2,18},{3,67},{4,20},{5,69},{6,22},{7,71},{8,24},{9,... | collective-permute-start | bytes 1572872 | tf_op jit(solution)/shard_map/ppermute | solution.py:332
  17.4 15.1 %collective-permute-start.12 = (bf16[2,2,32,2048]{3,2,1,0:T(8,128)(2,1)S(1)}, bf16[2,2,32,2048]{3,2,1,0:T(8,128)(2,1)S(1)}, u32[]{:S(2)}, u32[]{:S(2)}) collective-permute-start(bf16[2,2,32,2048]{3,2,1,0:T(8,128)(2,1)S(1)} %pad_maximum_fusion.1.b0), channel_id=1, source_target_pairs={{0,16},{1,65},{2,18},{3,67},{4,20},{5,69},{6,22},{7,71},{8,24},{9,... | collective-permute-start | bytes 1572872 | tf_op jit(solution)/shard_map/ppermute | solution.py:332
  19.0 13.5 %collective-permute-start.11 = (bf16[2,2,32,2048]{3,2,1,0:T(8,128)(2,1)S(1)}, bf16[2,2,32,2048]{3,2,1,0:T(8,128)(2,1)S(1)}, u32[]{:S(2)}, u32[]{:S(2)}) collective-permute-start(bf16[2,2,32,2048]{3,2,1,0:T(8,128)(2,1)S(1)} %pad_maximum_fusion.a0), channel_id=1, source_target_pairs={{0,48},{1,193},{2,50},{3,195},{4,52},{5,197},{6,54},{7,199},{8,56}... | collective-permute-start | bytes 1572872 | tf_op jit(solution)/shard_map/ppermute | solution.py:332
  24.4 11.2 %collective-permute-start.9 = (bf16[2,2,32,2048]{3,2,1,0:T(8,128)(2,1)S(1)}, bf16[2,2,32,2048]{3,2,1,0:T(8,128)(2,1)S(1)}, u32[]{:S(2)}, u32[]{:S(2)}) collective-permute-start(bf16[2,2,32,2048]{3,2,1,0:T(8,128)(2,1)S(1)} %collective-permute-done.8.b1), channel_id=1, source_target_pairs={{0,48},{1,193},{2,50},{3,195},{4,52},{5,197},{6,54},{7,199},{8,56}... | collective-permute-start | bytes 1572872 | tf_op jit(solution)/shard_map/ppermute | solution.py:332
  26.3 11.2 %collective-permute-start.5 = (bf16[2,2,32,2048]{3,2,1,0:T(8,128)(2,1)S(1)}, bf16[2,2,32,2048]{3,2,1,0:T(8,128)(2,1)S(1)}, u32[]{:S(2)}, u32[]{:S(2)}) collective-permute-start(bf16[2,2,32,2048]{3,2,1,0:T(8,128)(2,1)S(1)} %collective-permute-done.4.a3), channel_id=1, source_target_pairs={{0,16},{1,65},{2,18},{3,67},{4,20},{5,69},{6,22},{7,71},{8,24},{9,... | collective-permute-start | bytes 1572872 | tf_op jit(solution)/shard_map/ppermute | solution.py:332
  39.2 8.7 %collective-permute-start.17 = (s16[17,32,128]{2,1,0:T(8,128)(2,1)S(1)}, s16[17,32,128]{2,1,0:T(8,128)(2,1)S(1)}, u32[]{:S(2)}, u32[]{:S(2)}) collective-permute-start(s16[17,32,128]{2,1,0:T(8,128)(2,1)S(1)} %get-tuple-element.39), channel_id=1, source_target_pairs={{0,14},{1,15},{2,0},{3,1},{4,2},{5,3},{6,4},{7,5},{8,6},{9,7},{10,... | collective-permute-start | bytes 417800 | tf_op jit(solution)/shard_map/ppermute | solution.py:332
  44.8 7.6 %collective-permute-start.13 = (s16[17,32,128]{2,1,0:T(8,128)(2,1)S(1)}, s16[17,32,128]{2,1,0:T(8,128)(2,1)S(1)}, u32[]{:S(2)}, u32[]{:S(2)}) collective-permute-start(s16[17,32,128]{2,1,0:T(8,128)(2,1)S(1)} %get-tuple-element.38), channel_id=1, source_target_pairs={{0,2},{1,3},{2,4},{3,5},{4,6},{5,7},{6,8},{7,9},{8,10},{9,11},{10,... | collective-permute-start | bytes 417800 | tf_op jit(solution)/shard_map/ppermute | solution.py:332
  48.6 8.9 %collective-permute-start.18 = (s16[33,32,128]{2,1,0:T(8,128)(2,1)S(1)}, s16[33,32,128]{2,1,0:T(8,128)(2,1)S(1)}, u32[]{:S(2)}, u32[]{:S(2)}) collective-permute-start(s16[33,32,128]{2,1,0:T(8,128)(2,1)S(1)} %shard_map.75), channel_id=1, source_target_pairs={{0,14},{1,15},{2,0},{3,1},{4,2},{5,3},{6,4},{7,5},{8,6},{9,7},{10,... | collective-permute-start | bytes 811016 | tf_op jit(solution)/shard_map/ppermute | solution.py:332
  53.0 8.9 %collective-permute-start.14 = (s16[33,32,128]{2,1,0:T(8,128)(2,1)S(1)}, s16[33,32,128]{2,1,0:T(8,128)(2,1)S(1)}, u32[]{:S(2)}, u32[]{:S(2)}) collective-permute-start(s16[33,32,128]{2,1,0:T(8,128)(2,1)S(1)} %shard_map.72), channel_id=1, source_target_pairs={{0,2},{1,3},{2,4},{3,5},{4,6},{5,7},{6,8},{7,9},{8,10},{9,11},{10,... | collective-permute-start | bytes 811016 | tf_op jit(solution)/shard_map/ppermute | solution.py:332
  58.1 7.9 %collective-permute-start.19 = (s16[33,32,128]{2,1,0:T(8,128)(2,1)S(1)}, s16[33,32,128]{2,1,0:T(8,128)(2,1)S(1)}, u32[]{:S(2)}, u32[]{:S(2)}) collective-permute-start(s16[33,32,128]{2,1,0:T(8,128)(2,1)S(1)} %shard_map.76), channel_id=1, source_target_pairs={{0,14},{1,15},{2,0},{3,1},{4,2},{5,3},{6,4},{7,5},{8,6},{9,7},{10,... | collective-permute-start | bytes 811016 | tf_op jit(solution)/shard_map/ppermute | solution.py:332
  62.6 7.9 %collective-permute-start.15 = (s16[33,32,128]{2,1,0:T(8,128)(2,1)S(1)}, s16[33,32,128]{2,1,0:T(8,128)(2,1)S(1)}, u32[]{:S(2)}, u32[]{:S(2)}) collective-permute-start(s16[33,32,128]{2,1,0:T(8,128)(2,1)S(1)} %shard_map.73), channel_id=1, source_target_pairs={{0,2},{1,3},{2,4},{3,5},{4,6},{5,7},{6,8},{7,9},{8,10},{9,11},{10,... | collective-permute-start | bytes 811016 | tf_op jit(solution)/shard_map/ppermute | solution.py:332
  66.7 7.7 %collective-permute-start.20 = (s16[33,32,128]{2,1,0:T(8,128)(2,1)S(1)}, s16[33,32,128]{2,1,0:T(8,128)(2,1)S(1)}, u32[]{:S(2)}, u32[]{:S(2)}) collective-permute-start(s16[33,32,128]{2,1,0:T(8,128)(2,1)S(1)} %shard_map.77), channel_id=1, source_target_pairs={{0,14},{1,15},{2,0},{3,1},{4,2},{5,3},{6,4},{7,5},{8,6},{9,7},{10,... | collective-permute-start | bytes 811016 | tf_op jit(solution)/shard_map/ppermute | solution.py:332
  71.2 7.7 %collective-permute-start.16 = (s16[33,32,128]{2,1,0:T(8,128)(2,1)S(1)}, s16[33,32,128]{2,1,0:T(8,128)(2,1)S(1)}, u32[]{:S(2)}, u32[]{:S(2)}) collective-permute-start(s16[33,32,128]{2,1,0:T(8,128)(2,1)S(1)} %shard_map.74), channel_id=1, source_target_pairs={{0,2},{1,3},{2,4},{3,5},{4,6},{5,7},{6,8},{7,9},{8,10},{9,11},{10,... | collective-permute-start | bytes 811016 | tf_op jit(solution)/shard_map/ppermute | solution.py:332
  71.3 7.7 %collective-permute-start.21 = (f32[32,32,128]{2,1,0:T(8,128)S(1)}, f32[32,32,128]{2,1,0:T(8,128)S(1)}, u32[]{:S(2)}, u32[]{:S(2)}) collective-permute-start(f32[32,32,128]{2,1,0:T(8,128)S(1)} %get-tuple-element.36.ours), channel_id=1, source_target_pairs={{0,1},{1,0},{2,3},{3,2},{4,5},{5,4},{6,7},{7,6},{8,9},{9,8},{10,11... | collective-permute-start | bytes 1572872 | tf_op jit(solution)/shard_map/ppermute | solution.py:332
  74.5 4.5 %collective-permute-start.23 = (s16[33,32,128]{2,1,0:T(8,128)(2,1)S(1)}, s16[33,32,128]{2,1,0:T(8,128)(2,1)S(1)}, u32[]{:S(2)}, u32[]{:S(2)}) collective-permute-start(s16[33,32,128]{2,1,0:T(8,128)(2,1)S(1)} %collective-permute-done.20.left), channel_id=1, source_target_pairs={{0,1},{1,0},{2,3},{3,2},{4,5},{5,4},{6,7},{7,6},{8,9},{9,8},{10,11... | collective-permute-start | bytes 811016 | tf_op jit(solution)/shard_map/ppermute | solution.py:332
  79.0 1.5 %collective-permute-start.22 = (s16[33,32,128]{2,1,0:T(8,128)(2,1)S(1)}, s16[33,32,128]{2,1,0:T(8,128)(2,1)S(1)}, u32[]{:S(2)}, u32[]{:S(2)}) collective-permute-start(s16[33,32,128]{2,1,0:T(8,128)(2,1)S(1)} %collective-permute-done.16.right), channel_id=1, source_target_pairs={{0,1},{1,0},{2,3},{3,2},{4,5},{5,4},{6,7},{7,6},{8,9},{9,8},{10,11... | collective-permute-start | bytes 811016 | tf_op jit(solution)/shard_map/ppermute | solution.py:332

commit v6 on v5

--- a/solution.py
+++ b/solution.py
@@ -201,8 +201,11 @@
     gram = lax.dot_general(
         wide, wide, (((1,), (1,)), ((), ())), precision=HIGHEST, preferred_element_type=jnp.float32
     )
-    out[:, : 2 * half] = gram[:half]
-    out[:, 2 * half :] = gram[half:]
+    quarter, few = half // 2, half // 4
+    out[:quarter, : 2 * half] = gram[:quarter]
+    out[:quarter, 2 * half :] = gram[quarter:half]
+    for n in range(4):
+        out[quarter:, n * half : (n + 1) * half] = gram[half + n * few : half + (n + 1) * few, half:]
 
 
 def local_gram(core, *sums):
@@ -212,7 +215,7 @@
         gram_kernel,
         out_shape=(
             jax.ShapeDtypeStruct((count // 2, 2 * half, size), jnp.float32),
-            jax.ShapeDtypeStruct((half, 4 * half), jnp.float32),
+            jax.ShapeDtypeStruct((half // 2 + half // 4, 4 * half), jnp.float32),
         ),
         in_specs=[pl.BlockSpec(memory_space=pltpu.SMEM)] + [vmem] * 6,
         out_specs=(vmem, vmem),
@@ -228,8 +231,12 @@
     total = grams[0]
     for n in range(1, grams.shape[0]):
         total = total + grams[n]
-    work[: order // 2, :order] = total[:, :order]
-    work[order // 2 :, :order] = total[:, order:]
+    half, quarter, few = order // 2, order // 4, order // 8
+    work[:quarter, :order] = total[:quarter, :order]
+    work[quarter:half, :order] = total[:quarter, order:]
+    for n in range(4):
+        work[half + n * few : half + (n + 1) * few, half:order] = total[quarter:, n * half : (n + 1) * half]
+    work[half:, :half] = work[:half, half:order].T
     work[:, order:] = jnp.zeros((order, order), jnp.float32)
     lane = lax.broadcasted_iota(jnp.int32, (tile, 2 * order), 1)
     sub = lax.broadcasted_iota(jnp.int32, (tile, 2 * order), 0)

time: 113 us -> 113 us (level)
  Pallas kernels: 20.6 us -> 18.9 us
    pallas_call x4, Pallas kernels: 12.3 us -> 10.6 us  [add_blocks(): pl.pallas_call(functools.partial(kernel, row_blocks << 11), out_shape=out...]
  transfers between devices with their start and end apart: 24 -> 24, of which waited for: 12 -> 13; matrix products, arithmetic and copies ran while one was open for 3% -> 3% of each run, Pallas kernels for 13% -> 12%
where the time goes in v6:
time: 113 us
  starting transfers between devices  31.4 us (28%)
  waiting for transfers between devices  28.9 us (26%)
  blocking collectives  28.7 us (25%)
  Pallas kernels  18.9 us (17%)
  other arithmetic  2.9 us (3%)
  between operations  1.71 us (2%)
    ppermute x24, starting transfers between devices, move(): return lax.ppermute(array, BOTH, pairs)  31.4 us
    ppermute x24, waiting for transfers between devices, move(): return lax.ppermute(array, BOTH, pairs)  28.9 us
    all_to_all x2, blocking collectives, spread(): return lax.all_to_all(copies, axis, 0, 0, axis_index_groups=groups)  28.7 us
    pallas_call x4, Pallas kernels, add_blocks(): pl.pallas_call(functools.partial(kernel, row_blocks << 11), out_shape=out...  10.6 us
    pallas_call x6, Pallas kernels, on_chunk(): pl.pallas_call(kernel, out_shape=out_shape, in_specs=[pl.BlockSpec(memory...  4.06 us
    pallas_call x1, Pallas kernels, finish(): pl.pallas_call(functools.partial(finish_kernel, scale), out_shape=(jax.Sh...  3.13 us
  transfers between devices with their start and end apart: 24, of which 13 were waited for; matrix products, arithmetic and copies ran while one was open for 3% of the time, Pallas kernels for 12%

profile of v6, /device:TPU:8, one launch (start us, length us, event | category | flops | bytes accessed | tf_op | source)
XLA Modules:
  0.0 112.7 jit_solution(14186477169871167851)
XLA Ops:
  1.6 1.2 %select_bitcast_fusion.1 = bf16[1,32,2048]{2,1,0:T(8,128)(2,1)S(1)} fusion(bf16[64,2048]{1,0:T(8,128)(2,1)} %param.5, pred[]{:T(512)S(6)} %eq.92), kind=kLoop, calls=%fused_computation.7 | loop fusion | flops 65536 | bytes 393217 | tf_op jit(solution)/shard_map/stack | solution.py:351
  3.3 1.6 %collective-permute-start.1 = (bf16[2,32,2048]{2,1,0:T(8,128)(2,1)S(1)}, bf16[2,32,2048]{2,1,0:T(8,128)(2,1)S(1)}, u32[]{:S(2)}, u32[]{:S(2)}) collective-permute-start(bf16[2,32,2048]{2,1,0:T(8,128)(2,1)S(1)} %pad_maximum_fusion.2), channel_id=1, source_target_pairs={{0,64},{1,17},{2,66},{3,19},{4,68},{5,21},{6,70},{7,23},{8,72},{9,... | collective-permute-start | bytes 786440 | tf_op jit(solution)/shard_map/ppermute | solution.py:339
  4.9 1.7 %collective-permute-start.2 = (bf16[2,32,2048]{2,1,0:T(8,128)(2,1)S(1)}, bf16[2,32,2048]{2,1,0:T(8,128)(2,1)S(1)}, u32[]{:S(2)}, u32[]{:S(2)}) collective-permute-start(bf16[2,32,2048]{2,1,0:T(8,128)(2,1)S(1)} %pad_maximum_fusion.2), channel_id=1, source_target_pairs={{0,192},{1,49},{2,194},{3,51},{4,196},{5,53},{6,198},{7,55},{8,200... | collective-permute-start | bytes 786440 | tf_op jit(solution)/shard_map/ppermute | solution.py:339
  6.7 1.9 %collective-permute-start.6 = (bf16[32,2048]{1,0:T(8,128)(2,1)S(1)}, bf16[32,2048]{1,0:T(8,128)(2,1)S(1)}, u32[]{:S(2)}, u32[]{:S(2)}) collective-permute-start(bf16[32,2048]{1,0:T(8,128)(2,1)S(1)} %get-tuple-element.50), channel_id=1, source_target_pairs={{0,128},{1,33},{2,130},{3,35},{4,132},{5,37},{6,134},{7,39},{8,136... | collective-permute-start | bytes 393224 | tf_op jit(solution)/shard_map/ppermute | solution.py:339
  8.6 1.7 %collective-permute-start.7 = (bf16[32,2048]{1,0:T(8,128)(2,1)S(1)}, bf16[32,2048]{1,0:T(8,128)(2,1)S(1)}, u32[]{:S(2)}, u32[]{:S(2)}) collective-permute-start(bf16[32,2048]{1,0:T(8,128)(2,1)S(1)} %get-tuple-element.51), channel_id=1, source_target_pairs={{0,128},{1,33},{2,130},{3,35},{4,132},{5,37},{6,134},{7,39},{8,136... | collective-permute-start | bytes 393224 | tf_op jit(solution)/shard_map/ppermute | solution.py:339
  10.3 0.7 iota_add_fusion.1
  11.7 1.7 %collective-permute-done.6 = bf16[32,2048]{1,0:T(8,128)(2,1)S(1)} collective-permute-done((bf16[32,2048]{1,0:T(8,128)(2,1)S(1)}, bf16[32,2048]{1,0:T(8,128)(2,1)S(1)}, u32[]{:S(2)}, u32[]{:S(2)}) %collective-permute-start.6) | collective-permute-done | bytes 131104 | tf_op jit(solution)/shard_map/ppermute | solution.py:339
  13.4 1.7 %collective-permute-done.7 = bf16[32,2048]{1,0:T(8,128)(2,1)S(1)} collective-permute-done((bf16[32,2048]{1,0:T(8,128)(2,1)S(1)}, bf16[32,2048]{1,0:T(8,128)(2,1)S(1)}, u32[]{:S(2)}, u32[]{:S(2)}) %collective-permute-start.7) | collective-permute-done | bytes 131104 | tf_op jit(solution)/shard_map/ppermute | solution.py:339
  15.2 1.9 %collective-permute-start.8 = (bf16[2,2,32,2048]{3,2,1,0:T(8,128)(2,1)S(1)}, bf16[2,2,32,2048]{3,2,1,0:T(8,128)(2,1)S(1)}, u32[]{:S(2)}, u32[]{:S(2)}) collective-permute-start(bf16[2,2,32,2048]{3,2,1,0:T(8,128)(2,1)S(1)} %pad_maximum_fusion.1.b0), channel_id=1, source_target_pairs={{0,48},{1,193},{2,50},{3,195},{4,52},{5,197},{6,54},{7,199},{8,56}... | collective-permute-start | bytes 1572872 | tf_op jit(solution)/shard_map/ppermute | solution.py:339
  17.4 1.6 %collective-permute-start.12 = (bf16[2,2,32,2048]{3,2,1,0:T(8,128)(2,1)S(1)}, bf16[2,2,32,2048]{3,2,1,0:T(8,128)(2,1)S(1)}, u32[]{:S(2)}, u32[]{:S(2)}) collective-permute-start(bf16[2,2,32,2048]{3,2,1,0:T(8,128)(2,1)S(1)} %pad_maximum_fusion.1.b0), channel_id=1, source_target_pairs={{0,16},{1,65},{2,18},{3,67},{4,20},{5,69},{6,22},{7,71},{8,24},{9,... | collective-permute-start | bytes 1572872 | tf_op jit(solution)/shard_map/ppermute | solution.py:339
  19.4 5.0 %collective-permute-done.8.b1 = bf16[2,2,32,2048]{3,2,1,0:T(8,128)(2,1)S(1)} collective-permute-done((bf16[2,2,32,2048]{3,2,1,0:T(8,128)(2,1)S(1)}, bf16[2,2,32,2048]{3,2,1,0:T(8,128)(2,1)S(1)}, u32[]{:S(2)}, u32[]{:S(2)}) %collective-permute-start.8) | collective-permute-done | bytes 524320 | tf_op jit(solution)/shard_map/ppermute | solution.py:339
  24.4 1.8 %collective-permute-start.9 = (bf16[2,2,32,2048]{3,2,1,0:T(8,128)(2,1)S(1)}, bf16[2,2,32,2048]{3,2,1,0:T(8,128)(2,1)S(1)}, u32[]{:S(2)}, u32[]{:S(2)}) collective-permute-start(bf16[2,2,32,2048]{3,2,1,0:T(8,128)(2,1)S(1)} %collective-permute-done.8.b1), channel_id=1, source_target_pairs={{0,48},{1,193},{2,50},{3,195},{4,52},{5,197},{6,54},{7,199},{8,56}... | collective-permute-start | bytes 1572872 | tf_op jit(solution)/shard_map/ppermute | solution.py:339
  26.8 3.8 %shard_map.68 = (f32[257,32,128]{2,1,0:T(8,128)S(1)}, bf16[2,128,128,128]{3,2,1,0:T(8,128)(2,1)S(1)}) custom-call(s32[2,256]{1,0:T(2,128)S(1)} %pad_add_fusion.lists, bf16[2,2,32,2048]{3,2,1,0:T(8,128)(2,1)S(1)} %pad_maximum_fusion.a0, bf16[2,2,32,2048]{3,2,1,0:T(8,128)(2,1)S(1)} %pad_maximum_fusion.1.b0, ...), custom_call_target="tpu_custom_call" | custom-call | flops 134217728 | bytes 12582912 | tf_op jit(solution)/shard_map/pallas_call | solution.py:125
  30.6 1.4 %collective-permute-done.12.b3 = bf16[2,2,32,2048]{3,2,1,0:T(8,128)(2,1)S(1)} collective-permute-done((bf16[2,2,32,2048]{3,2,1,0:T(8,128)(2,1)S(1)}, bf16[2,2,32,2048]{3,2,1,0:T(8,128)(2,1)S(1)}, u32[]{:S(2)}, u32[]{:S(2)}) %collective-permute-start.12) | collective-permute-done | bytes 524320 | tf_op jit(solution)/shard_map/ppermute | solution.py:339
  32.0 2.9 %shard_map.69.share = f32[257,32,128]{2,1,0:T(8,128)S(1)} custom-call(s32[2,256]{1,0:T(2,128)S(1)} %pad_add_fusion.lists, bf16[2,2,32,2048]{3,2,1,0:T(8,128)(2,1)S(1)} %collective-permute-done.11.a1, bf16[2,2,32,2048]{3,2,1,0:T(8,128)(2,1)S(1)} %collective-permute-done.12.b3, bf16[2,128,128,128]{3,2,1,0:T(8,128)(2,1)S(1)} %get-tuple-element.33.blocks, ...), custom_call_target="tpu_custom_call" | custom-call | flops 67108864 | bytes 12582912 | tf_op jit(solution)/shard_map/pallas_call | solution.py:125
  34.9 0.8 collective-permute-done.9.b2
  35.7 1.9 %collective-permute-done.5.a2 = bf16[2,2,32,2048]{3,2,1,0:T(8,128)(2,1)S(1)} collective-permute-done((bf16[2,2,32,2048]{3,2,1,0:T(8,128)(2,1)S(1)}, bf16[2,2,32,2048]{3,2,1,0:T(8,128)(2,1)S(1)}, u32[]{:S(2)}, u32[]{:S(2)}) %collective-permute-start.5) | collective-permute-done | bytes 524320 | tf_op jit(solution)/shard_map/ppermute | solution.py:339
  37.6 1.4 %shard_map.70 = (f32[257,32,128]{2,1,0:T(8,128)S(1)}, s16[17,32,128]{2,1,0:T(8,128)(2,1)S(1)}, s16[17,32,128]{2,1,0:T(8,128)(2,1)S(1)}) custom-call(s32[2,256]{1,0:T(2,128)S(1)} %pad_add_fusion.lists, bf16[2,2,32,2048]{3,2,1,0:T(8,128)(2,1)S(1)} %collective-permute-done.5.a2, bf16[2,2,32,2048]{3,2,1,0:T(8,128)(2,1)S(1)} %collective-permute-done.9.b2, ...), custom_call_target="tpu_custom_call" | custom-call | flops 16777216 | bytes 12582912 | tf_op jit(solution)/shard_map/pallas_call | solution.py:125
  39.0 6.0 %collective-permute-start.17 = (s16[17,32,128]{2,1,0:T(8,128)(2,1)S(1)}, s16[17,32,128]{2,1,0:T(8,128)(2,1)S(1)}, u32[]{:S(2)}, u32[]{:S(2)}) collective-permute-start(s16[17,32,128]{2,1,0:T(8,128)(2,1)S(1)} %get-tuple-element.39), channel_id=1, source_target_pairs={{0,14},{1,15},{2,0},{3,1},{4,2},{5,3},{6,4},{7,5},{8,6},{9,7},{10,... | collective-permute-start | bytes 417800 | tf_op jit(solution)/shard_map/ppermute | solution.py:339
  45.0 2.5 %shard_map.71 = (f32[257,32,128]{2,1,0:T(8,128)S(1)}, f32[32,32,128]{2,1,0:T(8,128)S(1)}) custom-call(s32[2,256]{1,0:T(2,128)S(1)} %pad_add_fusion.lists, bf16[2,2,32,2048]{3,2,1,0:T(8,128)(2,1)S(1)} %collective-permute-done.5.a2, bf16[2,2,32,2048]{3,2,1,0:T(8,128)(2,1)S(1)} %collective-permute-done.9.b2, s32[8]{0:T(128)S(1)} %and_multiply_fusion.index.refs_0_, ...), custom_call_target="tpu_custom_call" | custom-call | flops 67108864 | bytes 12582912 | tf_op jit(solution)/shard_map/pallas_call | solution.py:125
  48.4 3.8 %collective-permute-start.18 = (s16[33,32,128]{2,1,0:T(8,128)(2,1)S(1)}, s16[33,32,128]{2,1,0:T(8,128)(2,1)S(1)}, u32[]{:S(2)}, u32[]{:S(2)}) collective-permute-start(s16[33,32,128]{2,1,0:T(8,128)(2,1)S(1)} %shard_map.75), channel_id=1, source_target_pairs={{0,14},{1,15},{2,0},{3,1},{4,2},{5,3},{6,4},{7,5},{8,6},{9,7},{10,... | collective-permute-start | bytes 811016 | tf_op jit(solution)/shard_map/ppermute | solution.py:339
  52.9 3.9 %collective-permute-done.18.refs_2_ = s16[33,32,128]{2,1,0:T(8,128)(2,1)S(1)} collective-permute-done((s16[33,32,128]{2,1,0:T(8,128)(2,1)S(1)}, s16[33,32,128]{2,1,0:T(8,128)(2,1)S(1)}, u32[]{:S(2)}, u32[]{:S(2)}) %collective-permute-start.18) | collective-permute-done | bytes 270368 | tf_op jit(solution)/shard_map/ppermute | solution.py:339
  57.5 3.8 %collective-permute-start.19 = (s16[33,32,128]{2,1,0:T(8,128)(2,1)S(1)}, s16[33,32,128]{2,1,0:T(8,128)(2,1)S(1)}, u32[]{:S(2)}, u32[]{:S(2)}) collective-permute-start(s16[33,32,128]{2,1,0:T(8,128)(2,1)S(1)} %shard_map.76), channel_id=1, source_target_pairs={{0,14},{1,15},{2,0},{3,1},{4,2},{5,3},{6,4},{7,5},{8,6},{9,7},{10,... | collective-permute-start | bytes 811016 | tf_op jit(solution)/shard_map/ppermute | solution.py:339
  62.0 3.2 %collective-permute-done.19.refs_2_ = s16[33,32,128]{2,1,0:T(8,128)(2,1)S(1)} collective-permute-done((s16[33,32,128]{2,1,0:T(8,128)(2,1)S(1)}, s16[33,32,128]{2,1,0:T(8,128)(2,1)S(1)}, u32[]{:S(2)}, u32[]{:S(2)}) %collective-permute-start.19) | collective-permute-done | bytes 270368 | tf_op jit(solution)/shard_map/ppermute | solution.py:339
  65.9 3.8 %collective-permute-start.20 = (s16[33,32,128]{2,1,0:T(8,128)(2,1)S(1)}, s16[33,32,128]{2,1,0:T(8,128)(2,1)S(1)}, u32[]{:S(2)}, u32[]{:S(2)}) collective-permute-start(s16[33,32,128]{2,1,0:T(8,128)(2,1)S(1)} %shard_map.77), channel_id=1, source_target_pairs={{0,14},{1,15},{2,0},{3,1},{4,2},{5,3},{6,4},{7,5},{8,6},{9,7},{10,... | collective-permute-start | bytes 811016 | tf_op jit(solution)/shard_map/ppermute | solution.py:339
  70.6 3.1 %collective-permute-done.20.left = s16[33,32,128]{2,1,0:T(8,128)(2,1)S(1)} collective-permute-done((s16[33,32,128]{2,1,0:T(8,128)(2,1)S(1)}, s16[33,32,128]{2,1,0:T(8,128)(2,1)S(1)}, u32[]{:S(2)}, u32[]{:S(2)}) %collective-permute-start.20) | collective-permute-done | bytes 270368 | tf_op jit(solution)/shard_map/ppermute | solution.py:339
  73.7 4.5 %collective-permute-done.16.right = s16[33,32,128]{2,1,0:T(8,128)(2,1)S(1)} collective-permute-done((s16[33,32,128]{2,1,0:T(8,128)(2,1)S(1)}, s16[33,32,128]{2,1,0:T(8,128)(2,1)S(1)}, u32[]{:S(2)}, u32[]{:S(2)}) %collective-permute-start.16) | collective-permute-done | bytes 270368 | tf_op jit(solution)/shard_map/ppermute | solution.py:339
  78.2 1.5 %collective-permute-done.22.their_right = s16[33,32,128]{2,1,0:T(8,128)(2,1)S(1)} collective-permute-done((s16[33,32,128]{2,1,0:T(8,128)(2,1)S(1)}, s16[33,32,128]{2,1,0:T(8,128)(2,1)S(1)}, u32[]{:S(2)}, u32[]{:S(2)}) %collective-permute-start.22) | collective-permute-done | bytes 270368 | tf_op jit(solution)/shard_map/ppermute | solution.py:339
  79.7 1.1 shard_map.78
  80.8 12.1 %all_to_all.10 = f32[8,24,128]{2,1,0:T(8,128)S(1)} all-to-all(f32[8,24,128]{2,1,0:T(8,128)S(1)} %broadcast_in_dim.87), channel_id=1, replica_groups={{0,2,4,6,8,10,12,14},{1,3,5,7,9,11,13,15},{16,18,20,22,24,26,28,30},{17..., dimensions={0} | all-to-all | bytes 196608 | tf_op jit(solution)/shard_map/all_to_all | solution.py:426
  93.0 16.5 %all_to_all.11.grams = f32[16,24,128]{2,1,0:T(8,128)S(1)} all-to-all(f32[16,24,128]{2,1,0:T(8,128)S(1)} %broadcast_in_dim.88), channel_id=1, replica_groups={{0,16,32,48,64,80,96,112,128,144,160,176,192,208,224,240},{1,17,33,49,6..., dimensions={0} | all-to-all | bytes 393216 | tf_op jit(solution)/shard_map/all_to_all | solution.py:426
  109.5 3.1 %shard_map.79 = (f32[64,2048]{1,0:T(8,128)}, f32[64,64]{1,0:T(8,128)}) custom-call(f32[16,24,128]{2,1,0:T(8,128)S(1)} %all_to_all.11.grams, f32[16,64,128]{2,1,0:T(8,128)S(1)} %get-tuple-element.41.mine), custom_call_target="tpu_custom_call" | custom-call | tf_op jit(solution)/shard_map/pallas_call | solution.py:282
  (56 shorter events, 7.6 us)
Async XLA Ops:
  0.6 2.1 %collective-permute-start = (bf16[64,2048]{1,0:T(8,128)(2,1)}, bf16[64,2048]{1,0:T(8,128)(2,1)S(1)}, u32[]{:S(2)}, u32[]{:S(2)}) collective-permute-start(bf16[64,2048]{1,0:T(8,128)(2,1)} %param.5), channel_id=1, source_target_pairs={{0,1},{1,0},{2,3},{3,2},{4,5},{5,4},{6,7},{7,6},{8,9},{9,8},{10,11... | collective-permute-start | bytes 786440 | tf_op jit(solution)/shard_map/ppermute | solution.py:339
  0.7 26.1 %copy-start = (bf16[128,128,128]{2,1,0:T(8,128)(2,1)S(1)}, bf16[128,128,128]{2,1,0:T(8,128)(2,1)}, u32[]{:S(2)}) copy-start(bf16[128,128,128]{2,1,0:T(8,128)(2,1)} %own_values) | copy-start | bytes 12582916
  2.7 24.1 %collective-permute-start.10 = (bf16[128,128,128]{2,1,0:T(8,128)(2,1)}, bf16[128,128,128]{2,1,0:T(8,128)(2,1)S(1)}, u32[]{:S(2)}, u32[]{:S(2)}) collective-permute-start(bf16[128,128,128]{2,1,0:T(8,128)(2,1)} %own_values), channel_id=1, source_target_pairs={{0,1},{1,0},{2,3},{3,2},{4,5},{5,4},{6,7},{7,6},{8,9},{9,8},{10,11... | collective-permute-start | bytes 12582920 | tf_op jit(solution)/shard_map/ppermute | solution.py:339
  3.3 11.8 %collective-permute-start.1 = (bf16[2,32,2048]{2,1,0:T(8,128)(2,1)S(1)}, bf16[2,32,2048]{2,1,0:T(8,128)(2,1)S(1)}, u32[]{:S(2)}, u32[]{:S(2)}) collective-permute-start(bf16[2,32,2048]{2,1,0:T(8,128)(2,1)S(1)} %pad_maximum_fusion.2), channel_id=1, source_target_pairs={{0,64},{1,17},{2,66},{3,19},{4,68},{5,21},{6,70},{7,23},{8,72},{9,... | collective-permute-start | bytes 786440 | tf_op jit(solution)/shard_map/ppermute | solution.py:339
  4.9 10.2 %collective-permute-start.2 = (bf16[2,32,2048]{2,1,0:T(8,128)(2,1)S(1)}, bf16[2,32,2048]{2,1,0:T(8,128)(2,1)S(1)}, u32[]{:S(2)}, u32[]{:S(2)}) collective-permute-start(bf16[2,32,2048]{2,1,0:T(8,128)(2,1)S(1)} %pad_maximum_fusion.2), channel_id=1, source_target_pairs={{0,192},{1,49},{2,194},{3,51},{4,196},{5,53},{6,198},{7,55},{8,200... | collective-permute-start | bytes 786440 | tf_op jit(solution)/shard_map/ppermute | solution.py:339
  6.7 6.7 %collective-permute-start.6 = (bf16[32,2048]{1,0:T(8,128)(2,1)S(1)}, bf16[32,2048]{1,0:T(8,128)(2,1)S(1)}, u32[]{:S(2)}, u32[]{:S(2)}) collective-permute-start(bf16[32,2048]{1,0:T(8,128)(2,1)S(1)} %get-tuple-element.50), channel_id=1, source_target_pairs={{0,128},{1,33},{2,130},{3,35},{4,132},{5,37},{6,134},{7,39},{8,136... | collective-permute-start | bytes 393224 | tf_op jit(solution)/shard_map/ppermute | solution.py:339
  8.6 6.5 %collective-permute-start.7 = (bf16[32,2048]{1,0:T(8,128)(2,1)S(1)}, bf16[32,2048]{1,0:T(8,128)(2,1)S(1)}, u32[]{:S(2)}, u32[]{:S(2)}) collective-permute-start(bf16[32,2048]{1,0:T(8,128)(2,1)S(1)} %get-tuple-element.51), channel_id=1, source_target_pairs={{0,128},{1,33},{2,130},{3,35},{4,132},{5,37},{6,134},{7,39},{8,136... | collective-permute-start | bytes 393224 | tf_op jit(solution)/shard_map/ppermute | solution.py:339
  13.4 1.7 %collective-permute-start.3 = (s32[1,256]{1,0:T(1,128)S(1)}, s32[1,256]{1,0:T(1,128)S(1)}, u32[]{:S(2)}, u32[]{:S(2)}) collective-permute-start(s32[1,256]{1,0:T(1,128)S(1)} %bitcast.40), channel_id=1, source_target_pairs={{0,1},{1,0},{2,3},{3,2},{4,5},{5,4},{6,7},{7,6},{8,9},{9,8},{10,11... | collective-permute-start | bytes 3080 | tf_op jit(solution)/shard_map/ppermute | solution.py:339
  15.2 9.3 %collective-permute-start.8 = (bf16[2,2,32,2048]{3,2,1,0:T(8,128)(2,1)S(1)}, bf16[2,2,32,2048]{3,2,1,0:T(8,128)(2,1)S(1)}, u32[]{:S(2)}, u32[]{:S(2)}) collective-permute-start(bf16[2,2,32,2048]{3,2,1,0:T(8,128)(2,1)S(1)} %pad_maximum_fusion.1.b0), channel_id=1, source_target_pairs={{0,48},{1,193},{2,50},{3,195},{4,52},{5,197},{6,54},{7,199},{8,56}... | collective-permute-start | bytes 1572872 | tf_op jit(solution)/shard_map/ppermute | solution.py:339
  17.1 9.3 %collective-permute-start.4 = (bf16[2,2,32,2048]{3,2,1,0:T(8,128)(2,1)S(1)}, bf16[2,2,32,2048]{3,2,1,0:T(8,128)(2,1)S(1)}, u32[]{:S(2)}, u32[]{:S(2)}) collective-permute-start(bf16[2,2,32,2048]{3,2,1,0:T(8,128)(2,1)S(1)} %pad_maximum_fusion.a0), channel_id=1, source_target_pairs={{0,16},{1,65},{2,18},{3,67},{4,20},{5,69},{6,22},{7,71},{8,24},{9,... | collective-permute-start | bytes 1572872 | tf_op jit(solution)/shard_map/ppermute | solution.py:339
  17.4 14.5 %collective-permute-start.12 = (bf16[2,2,32,2048]{3,2,1,0:T(8,128)(2,1)S(1)}, bf16[2,2,32,2048]{3,2,1,0:T(8,128)(2,1)S(1)}, u32[]{:S(2)}, u32[]{:S(2)}) collective-permute-start(bf16[2,2,32,2048]{3,2,1,0:T(8,128)(2,1)S(1)} %pad_maximum_fusion.1.b0), channel_id=1, source_target_pairs={{0,16},{1,65},{2,18},{3,67},{4,20},{5,69},{6,22},{7,71},{8,24},{9,... | collective-permute-start | bytes 1572872 | tf_op jit(solution)/shard_map/ppermute | solution.py:339
  19.0 13.0 %collective-permute-start.11 = (bf16[2,2,32,2048]{3,2,1,0:T(8,128)(2,1)S(1)}, bf16[2,2,32,2048]{3,2,1,0:T(8,128)(2,1)S(1)}, u32[]{:S(2)}, u32[]{:S(2)}) collective-permute-start(bf16[2,2,32,2048]{3,2,1,0:T(8,128)(2,1)S(1)} %pad_maximum_fusion.a0), channel_id=1, source_target_pairs={{0,48},{1,193},{2,50},{3,195},{4,52},{5,197},{6,54},{7,199},{8,56}... | collective-permute-start | bytes 1572872 | tf_op jit(solution)/shard_map/ppermute | solution.py:339
  24.4 11.2 %collective-permute-start.9 = (bf16[2,2,32,2048]{3,2,1,0:T(8,128)(2,1)S(1)}, bf16[2,2,32,2048]{3,2,1,0:T(8,128)(2,1)S(1)}, u32[]{:S(2)}, u32[]{:S(2)}) collective-permute-start(bf16[2,2,32,2048]{3,2,1,0:T(8,128)(2,1)S(1)} %collective-permute-done.8.b1), channel_id=1, source_target_pairs={{0,48},{1,193},{2,50},{3,195},{4,52},{5,197},{6,54},{7,199},{8,56}... | collective-permute-start | bytes 1572872 | tf_op jit(solution)/shard_map/ppermute | solution.py:339
  26.3 11.2 %collective-permute-start.5 = (bf16[2,2,32,2048]{3,2,1,0:T(8,128)(2,1)S(1)}, bf16[2,2,32,2048]{3,2,1,0:T(8,128)(2,1)S(1)}, u32[]{:S(2)}, u32[]{:S(2)}) collective-permute-start(bf16[2,2,32,2048]{3,2,1,0:T(8,128)(2,1)S(1)} %collective-permute-done.4.a3), channel_id=1, source_target_pairs={{0,16},{1,65},{2,18},{3,67},{4,20},{5,69},{6,22},{7,71},{8,24},{9,... | collective-permute-start | bytes 1572872 | tf_op jit(solution)/shard_map/ppermute | solution.py:339
  39.0 8.7 %collective-permute-start.17 = (s16[17,32,128]{2,1,0:T(8,128)(2,1)S(1)}, s16[17,32,128]{2,1,0:T(8,128)(2,1)S(1)}, u32[]{:S(2)}, u32[]{:S(2)}) collective-permute-start(s16[17,32,128]{2,1,0:T(8,128)(2,1)S(1)} %get-tuple-element.39), channel_id=1, source_target_pairs={{0,14},{1,15},{2,0},{3,1},{4,2},{5,3},{6,4},{7,5},{8,6},{9,7},{10,... | collective-permute-start | bytes 417800 | tf_op jit(solution)/shard_map/ppermute | solution.py:339
  45.0 7.2 %collective-permute-start.13 = (s16[17,32,128]{2,1,0:T(8,128)(2,1)S(1)}, s16[17,32,128]{2,1,0:T(8,128)(2,1)S(1)}, u32[]{:S(2)}, u32[]{:S(2)}) collective-permute-start(s16[17,32,128]{2,1,0:T(8,128)(2,1)S(1)} %get-tuple-element.38), channel_id=1, source_target_pairs={{0,2},{1,3},{2,4},{3,5},{4,6},{5,7},{6,8},{7,9},{8,10},{9,11},{10,... | collective-permute-start | bytes 417800 | tf_op jit(solution)/shard_map/ppermute | solution.py:339
  48.4 8.4 %collective-permute-start.18 = (s16[33,32,128]{2,1,0:T(8,128)(2,1)S(1)}, s16[33,32,128]{2,1,0:T(8,128)(2,1)S(1)}, u32[]{:S(2)}, u32[]{:S(2)}) collective-permute-start(s16[33,32,128]{2,1,0:T(8,128)(2,1)S(1)} %shard_map.75), channel_id=1, source_target_pairs={{0,14},{1,15},{2,0},{3,1},{4,2},{5,3},{6,4},{7,5},{8,6},{9,7},{10,... | collective-permute-start | bytes 811016 | tf_op jit(solution)/shard_map/ppermute | solution.py:339
  52.8 8.5 %collective-permute-start.14 = (s16[33,32,128]{2,1,0:T(8,128)(2,1)S(1)}, s16[33,32,128]{2,1,0:T(8,128)(2,1)S(1)}, u32[]{:S(2)}, u32[]{:S(2)}) collective-permute-start(s16[33,32,128]{2,1,0:T(8,128)(2,1)S(1)} %shard_map.72), channel_id=1, source_target_pairs={{0,2},{1,3},{2,4},{3,5},{4,6},{5,7},{6,8},{7,9},{8,10},{9,11},{10,... | collective-permute-start | bytes 811016 | tf_op jit(solution)/shard_map/ppermute | solution.py:339
  57.5 7.7 %collective-permute-start.19 = (s16[33,32,128]{2,1,0:T(8,128)(2,1)S(1)}, s16[33,32,128]{2,1,0:T(8,128)(2,1)S(1)}, u32[]{:S(2)}, u32[]{:S(2)}) collective-permute-start(s16[33,32,128]{2,1,0:T(8,128)(2,1)S(1)} %shard_map.76), channel_id=1, source_target_pairs={{0,14},{1,15},{2,0},{3,1},{4,2},{5,3},{6,4},{7,5},{8,6},{9,7},{10,... | collective-permute-start | bytes 811016 | tf_op jit(solution)/shard_map/ppermute | solution.py:339
  62.0 7.7 %collective-permute-start.15 = (s16[33,32,128]{2,1,0:T(8,128)(2,1)S(1)}, s16[33,32,128]{2,1,0:T(8,128)(2,1)S(1)}, u32[]{:S(2)}, u32[]{:S(2)}) collective-permute-start(s16[33,32,128]{2,1,0:T(8,128)(2,1)S(1)} %shard_map.73), channel_id=1, source_target_pairs={{0,2},{1,3},{2,4},{3,5},{4,6},{5,7},{6,8},{7,9},{8,10},{9,11},{10,... | collective-permute-start | bytes 811016 | tf_op jit(solution)/shard_map/ppermute | solution.py:339
  65.9 7.7 %collective-permute-start.20 = (s16[33,32,128]{2,1,0:T(8,128)(2,1)S(1)}, s16[33,32,128]{2,1,0:T(8,128)(2,1)S(1)}, u32[]{:S(2)}, u32[]{:S(2)}) collective-permute-start(s16[33,32,128]{2,1,0:T(8,128)(2,1)S(1)} %shard_map.77), channel_id=1, source_target_pairs={{0,14},{1,15},{2,0},{3,1},{4,2},{5,3},{6,4},{7,5},{8,6},{9,7},{10,... | collective-permute-start | bytes 811016 | tf_op jit(solution)/shard_map/ppermute | solution.py:339
  70.4 7.7 %collective-permute-start.16 = (s16[33,32,128]{2,1,0:T(8,128)(2,1)S(1)}, s16[33,32,128]{2,1,0:T(8,128)(2,1)S(1)}, u32[]{:S(2)}, u32[]{:S(2)}) collective-permute-start(s16[33,32,128]{2,1,0:T(8,128)(2,1)S(1)} %shard_map.74), channel_id=1, source_target_pairs={{0,2},{1,3},{2,4},{3,5},{4,6},{5,7},{6,8},{7,9},{8,10},{9,11},{10,... | collective-permute-start | bytes 811016 | tf_op jit(solution)/shard_map/ppermute | solution.py:339
  70.5 7.7 %collective-permute-start.21 = (f32[32,32,128]{2,1,0:T(8,128)S(1)}, f32[32,32,128]{2,1,0:T(8,128)S(1)}, u32[]{:S(2)}, u32[]{:S(2)}) collective-permute-start(f32[32,32,128]{2,1,0:T(8,128)S(1)} %get-tuple-element.36.ours), channel_id=1, source_target_pairs={{0,1},{1,0},{2,3},{3,2},{4,5},{5,4},{6,7},{7,6},{8,9},{9,8},{10,11... | collective-permute-start | bytes 1572872 | tf_op jit(solution)/shard_map/ppermute | solution.py:339
  73.7 4.5 %collective-permute-start.23 = (s16[33,32,128]{2,1,0:T(8,128)(2,1)S(1)}, s16[33,32,128]{2,1,0:T(8,128)(2,1)S(1)}, u32[]{:S(2)}, u32[]{:S(2)}) collective-permute-start(s16[33,32,128]{2,1,0:T(8,128)(2,1)S(1)} %collective-permute-done.20.left), channel_id=1, source_target_pairs={{0,1},{1,0},{2,3},{3,2},{4,5},{5,4},{6,7},{7,6},{8,9},{9,8},{10,11... | collective-permute-start | bytes 811016 | tf_op jit(solution)/shard_map/ppermute | solution.py:339
  78.1 1.5 %collective-permute-start.22 = (s16[33,32,128]{2,1,0:T(8,128)(2,1)S(1)}, s16[33,32,128]{2,1,0:T(8,128)(2,1)S(1)}, u32[]{:S(2)}, u32[]{:S(2)}) collective-permute-start(s16[33,32,128]{2,1,0:T(8,128)(2,1)S(1)} %collective-permute-done.16.right), channel_id=1, source_target_pairs={{0,1},{1,0},{2,3},{3,2},{4,5},{5,4},{6,7},{7,6},{8,9},{9,8},{10,11... | collective-permute-start | bytes 811016 | tf_op jit(solution)/shard_map/ppermute | solution.py:339
